TPU v7x, 512 devices: a whole 4x4x16 slice. The times are simulated.
512 devices in a mesh: row: 32 (over x, y, core), col: 16 (over z).
Axes of the slice: x: 4, y: 4, z: 16, core: 2. Of those that a mesh axis runs over, the one named last changes fastest.
Arguments:
- rhs_head: float32 [2, 2048, 4096], P(None, 'row', 'col'), may hold values from -6 to 6
- rhs_tail: float32 [14336, 4096], P('row', 'col'), may hold values from -6 to 6
- diag_inv: float32 [2, 2048, 2048], P(None, 'row'), as said below
- factor_cross: float32 [2048, 2048], P('row', 'col'), may hold values from -0.125 to 0.125
- factor_tail: float32 [14336, 2, 2048], P('row', None, 'col'), may hold values from -0.09375 to 0.09375
Outputs:
- solved: float32 [2, 2048, 4096], P(None, 'row', 'col')
- updated_tail: float32 [14336, 4096], P('row', 'col')
Inputs may be any that keep to these rules, and one draw needn't show every extreme that they name: diag_inv[k] is lower triangular with diagonal entries from 0.5 to 1.5.
All inputs are finite; a program needn't handle non-finite values.
Results may differ from a plain program's by a relative error of at most 0.000092.
Values sent between devices are 32-bit elements; how exact they have to be, the bound alone decides.
No kernel may reach another device: no remote copies, remote signals or barrier semaphores. Data moves between devices by JAX's collectives and lax.ppermute only.
A program may use at most 64 MiB of HBM per device.

v0:
```python
import jax
import jax.numpy as jnp
from jax import lax
from jax.sharding import PartitionSpec as P


def product(matrix, operand):
    return jnp.dot(
        matrix, operand, precision=lax.Precision.HIGHEST, preferred_element_type=jnp.float32
    )


def apply_solved(solved_block, factor_slabs):
    fragment = lax.all_gather(solved_block, "row", axis=0, tiled=True)
    return tuple((product(factor_slab, fragment) for factor_slab in factor_slabs))


def solve_rows(inverse_rows, head_block):
    return product(inverse_rows, lax.all_gather(head_block, "row", axis=0, tiled=True))


def local(rhs_head, rhs_tail, diag_inv, factor_cross, factor_tail):
    cross_wide, tail_wide = (
        lax.all_gather(factor_cross[:, None, :], "col", axis=2, tiled=True),
        lax.all_gather(factor_tail, "col", axis=2, tiled=True),
    )
    cross_wide = cross_wide[:, 0, :]
    head_block = rhs_head[0]
    tail_block = rhs_tail
    solved = []
    for panel_index in range(2):
        if panel_index == 0:
            factor_slabs = (tail_wide[:, 0, :], cross_wide)
        else:
            factor_slabs = (tail_wide[:, 1, :],)
        own_rows = solve_rows(diag_inv[panel_index], head_block)
        updates = apply_solved(own_rows, factor_slabs)
        solved.append(own_rows)
        tail_block = tail_block - updates[0]
        if panel_index == 0:
            head_block = rhs_head[1] - updates[1]
    return (jnp.stack(solved), tail_block)


def solution(mesh):
    return jax.shard_map(
        local,
        mesh=mesh,
        in_specs=(
            P(None, "row", "col"),
            P("row", "col"),
            P(None, "row", None),
            P("row", "col"),
            P("row", None, "col"),
        ),
        out_specs=(P(None, "row", "col"), P("row", "col")),
        check_vma=False,
    )
```

profile of v0, /device:TPU:1, one launch (start us, length us, event | category | flops | bytes accessed | tf_op | source)
XLA Modules:
  0.0 394.5 jit_solution(16702248391941810694)
XLA Ops:
  7.2 0.0 copy-start.3
  7.2 0.0 copy-start.4
  7.2 0.0 all-gather.16.cloned.1.call-start
  7.2 1.5 slice.19
  8.7 0.0 all-gather.16.cloned.1.call-update
  8.7 0.0 all-gather.8.cloned.1.call-start
  8.8 67.8 %all-gather.16.cloned.1.call-done = f32[1,2048,256]{2,1,0:T(8,128)} async-done(((f32[1,64,256]{2,1,0:T(8,128)}), f32[1,2048,256]{2,1,0:T(8,128)}) %all-gather.16.cloned.1.call-update) | async-done | bytes 2097168 | tf_op jit(solution)/shard_map/all_gather | solution.py:19
  76.6 3.6 fusion.2
  80.2 0.0 all-gather.8.cloned.1.call-update
  80.2 0.0 all-gather.10.cloned.1.call-start
  80.3 0.0 copy-done.4
  80.3 26.9 %all-gather.1 = f32[64,2048]{1,0:T(8,128)S(1)} all-gather(f32[64,128]{1,0:T(8,128)S(1)} %copy-done.4), channel_id=3, replica_groups=mesh['row'=32,'col'=16] {'col'}, dimensions={1}, use_global_device_ids=true | all-gather | bytes 557056 | tf_op jit(solution)/shard_map/all_gather | solution.py:24
  107.2 31.7 %all-gather.8.cloned.1.call-done = f32[2048,256]{1,0:T(8,128)} async-done(((f32[64,256]{1,0:T(8,128)}), f32[2048,256]{1,0:T(8,128)}) %all-gather.8.cloned.1.call-update) | async-done | bytes 2097168 | tf_op jit(solution)/shard_map/all_gather | solution.py:14
  138.9 0.0 copy-done.3
  138.9 3.5 fusion.8
  142.4 0.0 all-gather.10.cloned.1.call-update
  142.4 0.0 copy-start
  142.4 0.0 all-gather.12.cloned.1.call-start
  142.5 2.0 copy.7
  144.4 0.0 all-gather.12.cloned.1.call-update
  144.5 0.0 all-gather.14.cloned.1.call-start
  144.5 56.5 %all-gather.10.cloned.1.call-done = f32[2048,256]{1,0:T(8,128)} async-done(((f32[64,256]{1,0:T(8,128)}), f32[2048,256]{1,0:T(8,128)}) %all-gather.10.cloned.1.call-update) | async-done | bytes 2097168 | tf_op jit(solution)/shard_map/all_gather | solution.py:19
  201.1 0.0 copy-done.1
  201.1 3.5 fusion.9
  204.6 0.0 all-gather.14.cloned.1.call-update
  204.6 0.0 copy-done.2
  204.6 1.5 pad_maximum_fusion
  206.2 108.9 %all-gather.12.cloned.1.call-done = f32[448,2,2048]{2,0,1:T(8,128)} async-done(((f32[448,2,128]{2,0,1:T(8,128)}), f32[448,2,2048]{2,0,1:T(8,128)}) %all-gather.12.cloned.1.call-update) | async-done | bytes 7340048 | tf_op jit(solution)/shard_map/all_gather | solution.py:25
  315.0 0.0 copy-done
  315.0 5.2 %fusion.7 = f32[448,256]{1,0:T(8,128)S(1)} fusion(f32[448,256]{1,0:T(8,128)} %param.6, f32[2048,256]{1,0:T(8,128)S(1)} %copy-done, f32[448,2,2048]{2,0,1:T(8,128)} %all-gather.12.cloned.1.call-done), kind=kOutput, calls=%fused_computation.9 | convolution fusion | flops 2818686976 | bytes 6684672 | tf_op jit(solution)/shard_map/dot_general | solution.py:8
  320.3 61.1 %all-gather.14.cloned.1.call-done = f32[2048,256]{1,0:T(8,128)} async-done(((f32[64,256]{1,0:T(8,128)}), f32[2048,256]{1,0:T(8,128)}) %all-gather.14.cloned.1.call-update) | async-done | bytes 2097168 | tf_op jit(solution)/shard_map/all_gather | solution.py:14
  381.4 6.6 %fusion.6 = f32[448,256]{1,0:T(8,128)} fusion(f32[448,256]{1,0:T(8,128)S(1)} %fusion.7, f32[2048,256]{1,0:T(8,128)} %all-gather.14.cloned.1.call-done, f32[448,2,2048]{2,0,1:T(8,128)} %all-gather.12.cloned.1.call-done), kind=kOutput, calls=%fused_computation.8 | convolution fusion | flops 2818686976 | bytes 6684672 | tf_op jit(solution)/shard_map/dot_general | solution.py:8
  (2 shorter events, 0.0 us)
Async XLA Ops:
  7.2 131.7 %copy-start.3 = (f32[2,64,256]{2,1,0:T(8,128)S(1)}, f32[2,64,256]{2,1,0:T(8,128)}, u32[]{:S(2)}) copy-start(f32[2,64,256]{2,1,0:T(8,128)} %param.5) | copy-start | bytes 393220
  7.2 73.1 %copy-start.4 = (f32[64,128]{1,0:T(8,128)S(1)}, f32[64,128]{1,0:T(8,128)}, u32[]{:S(2)}) copy-start(f32[64,128]{1,0:T(8,128)} %param.8) | copy-start | bytes 98308
  7.2 69.4 %all-gather.16.cloned.1.call-start = ((), (), s32[]{:S(2)}) async-start(), calls=%async_computation.4 | async-start | bytes 2162688 | tf_op jit(solution)/shard_map/all_gather | solution.py:19
  8.7 130.1 %all-gather.8.cloned.1.call-start = ((), (), s32[]{:S(2)}) async-start(), calls=%async_computation | async-start | bytes 2162688 | tf_op jit(solution)/shard_map/all_gather | solution.py:14
  80.2 120.8 %all-gather.10.cloned.1.call-start = ((), (), s32[]{:S(2)}) async-start(), calls=%async_computation.1 | async-start | bytes 2162688 | tf_op jit(solution)/shard_map/all_gather | solution.py:19
  107.2 93.9 %copy-start.1 = (f32[2,64,2048]{2,1,0:T(8,128)S(1)}, f32[2,64,2048]{2,1,0:T(8,128)}, u32[]{:S(2)}) copy-start(f32[2,64,2048]{2,1,0:T(8,128)} %param.7) | copy-start | bytes 3145732
  142.4 62.2 %copy-start.2 = (f32[64,256]{1,0:T(8,128)S(1)}, f32[64,256]{1,0:T(8,128)}, u32[]{:S(2)}) copy-start(f32[64,256]{1,0:T(8,128)} %fusion.2) | copy-start | bytes 196612
  142.4 172.6 %copy-start = (f32[2048,256]{1,0:T(8,128)S(1)}, f32[2048,256]{1,0:T(8,128)}, u32[]{:S(2)}) copy-start(f32[2048,256]{1,0:T(8,128)} %all-gather.8.cloned.1.call-done) | copy-start | bytes 6291460
  142.4 172.6 %all-gather.12.cloned.1.call-start = ((), (), s32[]{:S(2)}) async-start(), calls=%async_computation.2 | async-start | bytes 7798784 | tf_op jit(solution)/shard_map/all_gather | solution.py:25
  144.5 236.9 %all-gather.14.cloned.1.call-start = ((), (), s32[]{:S(2)}) async-start(), calls=%async_computation.3 | async-start | bytes 2162688 | tf_op jit(solution)/shard_map/all_gather | solution.py:14
Sparse Core Ops, SparseCore 0:
  11.7 64.8 all-gather.15
  80.3 58.4 all-gather.7
  142.6 58.4 all-gather.9
  203.5 111.4 all-gather.11
  318.0 63.3 all-gather.13
where the time goes:
time: 395 us
  waiting for transfers between devices  326 us (83%)
  blocking collectives  26.9 us (7%)
  matrix products  22.5 us (6%)
  between operations  13.8 us (3%)
    all_gather x2, waiting for transfers between devices, solve_rows(): lax.all_gather(head_block, 'row', axis=0, tiled=True)  124 us
    all_gather x1, waiting for transfers between devices, local(): lax.all_gather(factor_tail, 'col', axis=2, tiled=True)  109 us
    all_gather x2, waiting for transfers between devices, apply_solved(): fragment = lax.all_gather(solved_block, 'row', axis=0, tiled=True)  92.8 us
    all_gather x1, blocking collectives, local(): lax.all_gather(factor_cross[:, None, :], 'col', axis=2, tiled=True)  26.9 us
    dot_general x5, matrix products, product(): jnp.dot(matrix, operand, precision=lax.Precision.HIGHEST, preferred_eleme...  22.5 us
  transfers between devices with their start and end apart: 5, of which 5 were waited for; matrix products, arithmetic and copies ran while one was open for 3% of the time, Pallas kernels for 0%

commit v1 on v0

v1 whole, which is shorter than its diff:
```python
import functools

import jax
import jax.numpy as jnp
from jax import lax
from jax.experimental import pallas as pl
from jax.experimental.pallas import tpu as pltpu
from jax.sharding import PartitionSpec as P

CORES = 2
TAIL_STEPS = 4


def swap(value):
    rows = lax.axis_size("row")
    return lax.ppermute(value, "row", [(i, i ^ 1) for i in range(rows)])


def gather_chips(copies):
    rows = lax.axis_size("row")
    groups = [list(range(core, rows, CORES)) for core in range(CORES)]
    blocks = lax.all_to_all(copies, "row", 0, 0, axis_index_groups=groups, tiled=True)
    return blocks.reshape(-1, blocks.shape[-1])


def gather_half(copies):
    chips, cores, rows, half = copies.shape
    return lax.all_to_all(copies.reshape(chips * cores, rows, half), "row", 0, 0, tiled=True).reshape(-1, half)


def gather_panels(block):
    planes = lax.axis_size("col")
    return lax.all_to_all(jnp.broadcast_to(block[None], (planes,) + block.shape), "col", 0, 0, tiled=True)


def split(value):
    high = value.astype(jnp.bfloat16)
    low = (value - high.astype(jnp.float32)).astype(jnp.bfloat16)
    return high, low


def product(left, right):
    left_high, left_low = split(left)
    right_high, right_low = split(right)
    dot = functools.partial(jnp.dot, preferred_element_type=jnp.float32)
    return dot(left_high, right_high) + (dot(left_high, right_low) + dot(left_low, right_high))


def in_order(own, other, axis):
    first = lax.axis_index("row") % CORES == 0
    return jnp.concatenate([jnp.where(first, own, other), jnp.where(first, other, own)], axis=axis)


def spread(value, out):
    for chip in range(out.shape[0]):
        out[chip] = value


def prepare_kernel(heads, copies, keep, send):
    half = keep.shape[1]
    halves = [heads[0][:, core * half : (core + 1) * half] for core in range(CORES)]
    for chip in range(copies.shape[0]):
        for core in range(CORES):
            copies[chip, core] = halves[core]
    first = lax.axis_index("row") % CORES == 0
    left, right = heads[1][:, :half], heads[1][:, half:]
    keep[...] = jnp.where(first, left, right)
    send[...] = jnp.where(first, right, left)


def solve_kernel(own, other, operand, out):
    spread(product(in_order(own[0], other[0], 0), operand[...]), out)


def cross_kernel(own, other, head, head_other, operand, out):
    row_of = lambda blocks: jnp.concatenate([blocks[i] for i in range(blocks.shape[0])], axis=1)
    left = in_order(row_of(own), row_of(other), 0)
    spread(in_order(head[...], head_other[...], 0) - product(left, operand[...]), out)


def tail_kernel(tail, factor, first, first_other, second, second_other, out, solved, total):
    step = pl.program_id(0)
    row = lax.axis_index("row")
    own_rows, depth, rows = solved.shape[1], factor.shape[2], out.shape[0]
    per_step = first.shape[0] // own_rows

    @pl.when(step == row // per_step)
    def _():
        at = pl.ds(pl.multiple_of((row % per_step) * own_rows, own_rows), own_rows)
        solved[0] = in_order(first[at, :], first_other[at, :], 1)
        solved[1] = in_order(second[at, :], second_other[at, :], 1)

    left, right = [], []
    for block in range(factor.shape[0]):
        at = pl.ds(block * depth, depth)
        for panel, (own, other) in enumerate(((first, first_other), (second, second_other))):
            left.append(factor[block, pl.ds(panel, rows, stride=2), :])
            right.append(jnp.concatenate([own[at, :], other[at, :]], axis=1))
    part = product(jnp.concatenate(left, axis=1), jnp.concatenate(right, axis=0))

    @pl.when(step == 0)
    def _():
        total[...] = part

    @pl.when(step > 0)
    def _():
        total[...] += part

    @pl.when(step == pl.num_programs(0) - 1)
    def _():
        half = out.shape[1] // 2
        out[...] = tail[...] - in_order(total[:, :half], total[:, half:], 1)


def params(mib):
    return pltpu.CompilerParams(vmem_limit_bytes=mib * 1024 * 1024)


def estimate(flops, size):
    return pl.CostEstimate(flops=flops, bytes_accessed=size, transcendentals=0)


def prepare(heads):
    _, rows, columns = heads.shape
    half = columns // CORES
    chips = lax.axis_size("row") // CORES
    part = jax.ShapeDtypeStruct((rows, half), jnp.float32)
    return pl.pallas_call(
        prepare_kernel,
        out_shape=(jax.ShapeDtypeStruct((chips, CORES, rows, half), jnp.float32), part, part),
        compiler_params=params(8),
        cost_estimate=estimate(0, 4 * (chips + 3) * rows * columns),
    )(heads)


def solve_chip(panel, own, other, operand):
    _, rows, depth = own.shape
    columns = operand.shape[1]
    chips = lax.axis_size("row") // CORES
    inverse = pl.BlockSpec((1, rows, depth), lambda step: (panel, 0, 0))
    shape = (chips, CORES * rows, columns)
    return pl.pallas_call(
        solve_kernel,
        grid=(1,),
        in_specs=[inverse, inverse, pl.BlockSpec(operand.shape, lambda step: (0, 0))],
        out_specs=pl.BlockSpec(shape, lambda step: (0, 0, 0)),
        out_shape=jax.ShapeDtypeStruct(shape, jnp.float32),
        compiler_params=params(16),
        cost_estimate=estimate(12 * rows * depth * columns, 4 * depth * (2 * rows + 2 * columns)),
    )(own, other, operand)


def cross_chip(own, other, head, head_other, operand):
    _, rows, _ = own.shape
    depth, columns = operand.shape
    chips = lax.axis_size("row") // CORES
    return pl.pallas_call(
        cross_kernel,
        out_shape=jax.ShapeDtypeStruct((chips, CORES * rows, columns), jnp.float32),
        compiler_params=params(16),
        cost_estimate=estimate(12 * rows * depth * columns, 4 * depth * (2 * rows + 2 * columns)),
    )(own, other, head, head_other, operand)


def tail_rows(tail, factor, halves):
    rows, columns = tail.shape
    blocks, double, width = factor.shape
    depth, half = halves[0].shape
    own_rows = depth // lax.axis_size("row")
    whole = lambda shape: pl.BlockSpec(shape, lambda step: (0,) * len(shape))
    shapes = [
        jax.ShapeDtypeStruct((rows, columns), jnp.float32),
        jax.ShapeDtypeStruct((2, own_rows, columns), jnp.float32),
    ]
    return pl.pallas_call(
        tail_kernel,
        grid=(TAIL_STEPS,),
        in_specs=[
            whole(tail.shape),
            pl.BlockSpec((blocks // TAIL_STEPS, double, width), lambda step: (step, 0, 0)),
        ]
        + [pl.BlockSpec((depth // TAIL_STEPS, half), lambda step: (step, 0)) for _ in halves],
        out_specs=[whole(shape.shape) for shape in shapes],
        out_shape=shapes,
        scratch_shapes=[pltpu.VMEM((rows, columns), jnp.float32)],
        compiler_params=params(55),
        cost_estimate=estimate(12 * rows * depth * columns, 4 * blocks * double * width),
    )(tail, factor, *halves)


def local(rhs_head, rhs_tail, diag_inv, factor_cross, factor_tail):
    rows, _, width = factor_tail.shape
    factor = lax.all_gather(factor_tail.reshape(2 * rows, width), "col", axis=0)
    copies, head, head_other = prepare(rhs_head)
    copies, diag_inv, factor_cross, head_other = lax.optimization_barrier(
        (copies, diag_inv, factor_cross, head_other)
    )
    first_head = gather_half(copies)
    inverse_other = swap(diag_inv)
    head_other = swap(head_other)
    cross = gather_panels(factor_cross)
    cross_other = swap(cross)

    first = gather_chips(solve_chip(0, diag_inv, inverse_other, first_head))
    second_head = gather_chips(cross_chip(cross, cross_other, head, head_other, first))
    second = gather_chips(solve_chip(1, diag_inv, inverse_other, second_head))
    tail, solved = tail_rows(rhs_tail, factor, (first, swap(first), second, swap(second)))
    return solved, tail


def solution(mesh):
    return jax.shard_map(
        local,
        mesh=mesh,
        in_specs=(
            P(None, "row", "col"),
            P("row", "col"),
            P(None, "row", None),
            P("row", "col"),
            P("row", None, "col"),
        ),
        out_specs=(P(None, "row", "col"), P("row", "col")),
        check_vma=False,
    )
```

time: 395 us -> 164 us (0.42)
  waiting for transfers between devices: 326 us -> 40 us
  starting transfers between devices: 0.21 us -> 45.5 us
  matrix products: 22.5 us -> 0 us
  blocking collectives: 26.9 us -> 46.2 us
  Pallas kernels: 0 us -> 13.6 us
    all_gather x5 -> x1, waiting for transfers between devices: 326 us -> 0.01 us  [local(): factor = lax.all_gather(factor_tail.reshape(2 * rows, width), 'col', axis=0)]
    all_to_all x0 -> x2, blocking collectives: none -> 46.2 us  [the longest x1 26.7 us: gather_half(): lax.all_to_all(copies.reshape(chips * cores, rows, half), 'row', 0, 0, ti...]
    all_to_all x0 -> x3, waiting for transfers between devices: none -> 33.3 us  [the longest x1 23.7 us: gather_panels(): lax.all_to_all(jnp.broadcast_to(block[None], (planes,) + block.shape), 'c...]
    all_gather x1 -> x0, blocking collectives: 26.9 us -> none  [local(): lax.all_gather(factor_cross[:, None, :], 'col', axis=2, tiled=True)]
    ppermute x0 -> x5, starting transfers between devices: none -> 23.6 us  [swap(): return lax.ppermute(value, 'row', [(i, i ^ 1) for i in range(rows)])]
    dot_general x5 -> x0, matrix products: 22.5 us -> none  [product(): jnp.dot(matrix, operand, precision=lax.Precision.HIGHEST, preferred_eleme...]
    all_to_all x0 -> x3, starting transfers between devices: none -> 21.8 us  [the longest x1 13.7 us: gather_panels(): lax.all_to_all(jnp.broadcast_to(block[None], (planes,) + block.shape), 'c...]
    pallas_call x0 -> x5, Pallas kernels: none -> 13.6 us  [the longest x1 7.71 us: tail_rows(): pl.pallas_call(tail_kernel, grid=(TAIL_STEPS,), in_specs=[whole(tail.shap...]
  transfers between devices with their start and end apart: 5 -> 9, of which waited for: 5 -> 6; matrix products, arithmetic and copies ran while one was open for 3% -> 1% of each run, Pallas kernels for 0% -> 4%
where the time goes in v1:
time: 164 us; the launch traced here: 163 us
  blocking collectives  46.2 us (28%)
  starting transfers between devices  45.5 us (28%)
  waiting for transfers between devices  40 us (24%)
  between operations  14.1 us (9%)
  Pallas kernels  13.6 us (8%)
  local copies, waits for them, and re-layouts  3.77 us (2%)
    all_to_all x1, blocking collectives, gather_half(): lax.all_to_all(copies.reshape(chips * cores, rows, half), 'row', 0, 0, ti...  26.7 us
    all_to_all x1, waiting for transfers between devices, gather_panels(): lax.all_to_all(jnp.broadcast_to(block[None], (planes,) + block.shape), 'c...  23.7 us
    ppermute x5, starting transfers between devices, swap(): return lax.ppermute(value, 'row', [(i, i ^ 1) for i in range(rows)])  23.6 us
    all_to_all x1, blocking collectives, gather_chips(): lax.all_to_all(copies, 'row', 0, 0, axis_index_groups=groups, tiled=True)  19.5 us
    all_to_all x1, starting transfers between devices, gather_panels(): lax.all_to_all(jnp.broadcast_to(block[None], (planes,) + block.shape), 'c...  13.7 us
    all_to_all x2, waiting for transfers between devices, gather_chips(): lax.all_to_all(copies, 'row', 0, 0, axis_index_groups=groups, tiled=True)  9.58 us
    all_to_all x2, starting transfers between devices, gather_chips(): lax.all_to_all(copies, 'row', 0, 0, axis_index_groups=groups, tiled=True)  8.1 us
    pallas_call x1, Pallas kernels, tail_rows(): pl.pallas_call(tail_kernel, grid=(TAIL_STEPS,), in_specs=[whole(tail.shap...  7.71 us
  transfers between devices with their start and end apart: 9, of which 6 were waited for; matrix products, arithmetic and copies ran while one was open for 1% of the time, Pallas kernels for 4%

profile of v1, /device:TPU:1, one launch (start us, length us, event | category | flops | bytes accessed | tf_op | source)
XLA Modules:
  0.0 163.2 jit_solution(4205234538127586736)
XLA Ops:
  7.2 0.0 all-gather.2.cloned.1.call-start
  7.2 0.7 all-gather.2.cloned.1.call-update
  7.9 0.9 copy-done.3
  8.8 0.1 shard_map.68
  8.9 0.0 copy-start.2
  8.9 26.7 %all_to_all.25 = f32[32,64,128]{2,1,0:T(8,128)S(1)} all-to-all(f32[32,64,128]{2,1,0:T(8,128)S(1)} %bitcast.11), channel_id=1, replica_groups=mesh['row'=32,'col'=16] {'row'}, dimensions={0} | all-to-all | bytes 2097152 | tf_op jit(solution)/shard_map/all_to_all | solution.py:28
  35.6 1.6 broadcast_in_dim.2
  37.2 13.7 %all-to-all-start.2 = ((f32[16,64,128]{2,1,0:T(8,128)}), f32[16,64,128]{2,1,0:T(8,128)}, u32[]{:S(2)}, u32[]{:S(2)}) async-start(f32[16,64,128]{2,1,0:T(8,128)} %broadcast_in_dim.2), calls=%async_computation.2 | async-start | bytes 1048576 | tf_op jit(solution)/shard_map/all_to_all | solution.py:33
  51.0 2.3 %collective-permute-start = (f32[2,64,2048]{2,1,0:T(8,128)}, f32[2,64,2048]{2,1,0:T(8,128)S(1)}, u32[]{:S(2)}, u32[]{:S(2)}) collective-permute-start(f32[2,64,2048]{2,1,0:T(8,128)} %own.1), channel_id=1, source_target_pairs={{0,16},{16,0},{32,48},{48,32},{64,80},{80,64},{96,112},{112,96},{1... | collective-permute-start | bytes 3145736 | tf_op jit(solution)/shard_map/ppermute | solution.py:16
  53.3 2.5 %collective-permute-done.other = f32[2,64,2048]{2,1,0:T(8,128)S(1)} collective-permute-done((f32[2,64,2048]{2,1,0:T(8,128)}, f32[2,64,2048]{2,1,0:T(8,128)S(1)}, u32[]{:S(2)}, u32[]{:S(2)}) %collective-permute-start) | collective-permute-done | bytes 1048608 | tf_op jit(solution)/shard_map/ppermute | solution.py:16
  55.8 1.2 copy-done.1
  57.0 1.8 %shard_map.69 = f32[16,128,128]{2,1,0:T(8,128)} custom-call(f32[2,64,2048]{2,1,0:T(8,128)S(1)} %copy-done.1, f32[2,64,2048]{2,1,0:T(8,128)S(1)} %collective-permute-done.other, f32[2048,128]{1,0:T(8,128)S(1)} %bitcast.9), custom_call_target="tpu_custom_call" | custom-call | flops 201326592 | bytes 3145728 | tf_op jit(solution)/shard_map/pallas_call | solution.py:142
  58.8 23.7 %all-to-all-done.2.own = f32[16,64,128]{2,1,0:T(8,128)} async-done(((f32[16,64,128]{2,1,0:T(8,128)}), f32[16,64,128]{2,1,0:T(8,128)}, u32[]{:S(2)}, u32[]{:S(2)}) %all-to-all-start.2) | async-done | bytes 524320 | tf_op jit(solution)/shard_map/all_to_all | solution.py:33
  82.5 3.7 %all-to-all-start.1 = ((f32[16,128,128]{2,1,0:T(8,128)}), f32[16,128,128]{2,1,0:T(8,128)S(1)}, u32[]{:S(2)}, u32[]{:S(2)}) async-start(f32[16,128,128]{2,1,0:T(8,128)} %shard_map.69), calls=%async_computation.1 | async-start | bytes 2097152 | tf_op jit(solution)/shard_map/all_to_all | solution.py:22
  86.2 5.6 %collective-permute-start.2 = (f32[16,64,128]{2,1,0:T(8,128)}, f32[16,64,128]{2,1,0:T(8,128)}, u32[]{:S(2)}, u32[]{:S(2)}) collective-permute-start(f32[16,64,128]{2,1,0:T(8,128)} %all-to-all-done.2.own), channel_id=1, source_target_pairs={{0,16},{16,0},{32,48},{48,32},{64,80},{80,64},{96,112},{112,96},{1... | collective-permute-start | bytes 1572872 | tf_op jit(solution)/shard_map/ppermute | solution.py:16
  91.7 1.9 %collective-permute-start.3 = (f32[64,128]{1,0:T(8,128)S(1)}, f32[64,128]{1,0:T(8,128)S(1)}, u32[]{:S(2)}, u32[]{:S(2)}) collective-permute-start(f32[64,128]{1,0:T(8,128)S(1)} %get-tuple-element.17), channel_id=1, source_target_pairs={{0,16},{16,0},{32,48},{48,32},{64,80},{80,64},{96,112},{112,96},{1... | collective-permute-start | bytes 98312 | tf_op jit(solution)/shard_map/ppermute | solution.py:16
  93.7 1.2 collective-permute-done.3.head_other
  94.8 3.4 %all-to-all-done.1 = f32[16,128,128]{2,1,0:T(8,128)S(1)} async-done(((f32[16,128,128]{2,1,0:T(8,128)}), f32[16,128,128]{2,1,0:T(8,128)S(1)}, u32[]{:S(2)}, u32[]{:S(2)}) %all-to-all-start.1) | async-done | bytes 1048608 | tf_op jit(solution)/shard_map/all_to_all | solution.py:22
  98.3 0.0 collective-permute-done.2.other
  98.3 2.3 %shard_map.70 = f32[16,128,128]{2,1,0:T(8,128)S(1)} custom-call(f32[16,64,128]{2,1,0:T(8,128)} %all-to-all-done.2.own, f32[16,64,128]{2,1,0:T(8,128)} %collective-permute-done.2.other, f32[64,128]{1,0:T(8,128)S(1)} %get-tuple-element.16.head, f32[64,128]{1,0:T(8,128)S(1)} %collective-permute-done.3.head_other, f32[2048,128]{1,0:T(8,128)S(1)} %bitcast.6), custom_call_target="tpu_custom_call" | custom-call | flops 201326592 | bytes 3145728 | tf_op jit(solution)/shard_map/pallas_call | solution.py:157
  100.6 19.5 %all_to_all.26 = f32[16,128,128]{2,1,0:T(8,128)S(1)} all-to-all(f32[16,128,128]{2,1,0:T(8,128)S(1)} %shard_map.70), channel_id=1, replica_groups={{0,32,64,96,128,160,192,224,256,288,320,352,384,416,448,480},{16,48,80,..., dimensions={0} | all-to-all | bytes 2097152 | tf_op jit(solution)/shard_map/all_to_all | solution.py:22
  120.1 0.0 copy-done.2
  120.1 1.8 %shard_map.71 = f32[16,128,128]{2,1,0:T(8,128)} custom-call(f32[2,64,2048]{2,1,0:T(8,128)S(1)} %copy-done.2, f32[2,64,2048]{2,1,0:T(8,128)S(1)} %collective-permute-done.other, f32[2048,128]{1,0:T(8,128)S(1)} %bitcast.10), custom_call_target="tpu_custom_call" | custom-call | flops 201326592 | bytes 3145728 | tf_op jit(solution)/shard_map/pallas_call | solution.py:142
  121.9 4.4 %all-to-all-start.4 = ((f32[16,128,128]{2,1,0:T(8,128)}), f32[16,128,128]{2,1,0:T(8,128)S(1)}, u32[]{:S(2)}, u32[]{:S(2)}) async-start(f32[16,128,128]{2,1,0:T(8,128)} %shard_map.71), calls=%async_computation.4 | async-start | bytes 2097152 | tf_op jit(solution)/shard_map/all_to_all | solution.py:22
  126.3 6.1 %collective-permute-start.1 = (f32[2048,128]{1,0:T(8,128)S(1)}, f32[2048,128]{1,0:T(8,128)S(1)}, u32[]{:S(2)}, u32[]{:S(2)}) collective-permute-start(f32[2048,128]{1,0:T(8,128)S(1)} %bitcast.7), channel_id=1, source_target_pairs={{0,16},{16,0},{32,48},{48,32},{64,80},{80,64},{96,112},{112,96},{1... | collective-permute-start | bytes 3145736 | tf_op jit(solution)/shard_map/ppermute | solution.py:16
  132.4 6.1 %all-to-all-done.4 = f32[16,128,128]{2,1,0:T(8,128)S(1)} async-done(((f32[16,128,128]{2,1,0:T(8,128)}), f32[16,128,128]{2,1,0:T(8,128)S(1)}, u32[]{:S(2)}, u32[]{:S(2)}) %all-to-all-start.4) | async-done | bytes 1048608 | tf_op jit(solution)/shard_map/all_to_all | solution.py:22
  138.5 7.7 %collective-permute-start.4 = (f32[2048,128]{1,0:T(8,128)S(1)}, f32[2048,128]{1,0:T(8,128)}, u32[]{:S(2)}, u32[]{:S(2)}) collective-permute-start(f32[2048,128]{1,0:T(8,128)S(1)} %bitcast.12), channel_id=1, source_target_pairs={{0,16},{16,0},{32,48},{48,32},{64,80},{80,64},{96,112},{112,96},{1... | collective-permute-start | bytes 3145736 | tf_op jit(solution)/shard_map/ppermute | solution.py:16
  146.3 0.0 collective-permute-done.1.first_other
  146.3 2.4 %collective-permute-done.4.second_other = f32[2048,128]{1,0:T(8,128)} collective-permute-done((f32[2048,128]{1,0:T(8,128)S(1)}, f32[2048,128]{1,0:T(8,128)}, u32[]{:S(2)}, u32[]{:S(2)}) %collective-permute-start.4) | collective-permute-done | bytes 1048608 | tf_op jit(solution)/shard_map/ppermute | solution.py:16
  148.7 0.0 copy-done
  148.7 0.0 copy-done.5
  148.7 7.7 %shard_map.72 = (f32[448,256]{1,0:T(8,128)}, f32[2,64,256]{2,1,0:T(8,128)}) custom-call(f32[448,256]{1,0:T(8,128)} %tail.1, f32[16,896,128]{2,1,0:T(8,128)} %all-gather.2.cloned.1.call-done.factor, f32[2048,128]{1,0:T(8,128)} %bitcast.8, f32[2048,128]{1,0:T(8,128)} %copy-done.5, f32[2048,128]{1,0:T(8,128)} %bitcast.13, ...), custom_call_target="tpu_custom_call" | custom-call | flops 2818572288 | bytes 7340032 | tf_op jit(solution)/shard_map/pallas_call | solution.py:175
  (7 shorter events, 0.0 us)
Async XLA Ops:
  7.2 141.5 %all-gather.2.cloned.1.call-start = ((), (), s32[]{:S(2)}) async-start(), calls=%async_computation.5 | async-start | bytes 7798784 | tf_op jit(solution)/shard_map/all_gather | solution.py:193
  7.9 0.9 copy-start.3
  8.9 111.2 %copy-start.2 = (f32[2,64,2048]{2,1,0:T(8,128)S(1)}, f32[2,64,2048]{2,1,0:T(8,128)}, u32[]{:S(2)}) copy-start(f32[2,64,2048]{2,1,0:T(8,128)} %own.1) | copy-start | bytes 3145732
  37.2 45.3 %all-to-all-start.2 = ((f32[16,64,128]{2,1,0:T(8,128)}), f32[16,64,128]{2,1,0:T(8,128)}, u32[]{:S(2)}, u32[]{:S(2)}) async-start(f32[16,64,128]{2,1,0:T(8,128)} %broadcast_in_dim.2), calls=%async_computation.2 | async-start | bytes 1048576 | tf_op jit(solution)/shard_map/all_to_all | solution.py:33
  51.0 4.8 %collective-permute-start = (f32[2,64,2048]{2,1,0:T(8,128)}, f32[2,64,2048]{2,1,0:T(8,128)S(1)}, u32[]{:S(2)}, u32[]{:S(2)}) collective-permute-start(f32[2,64,2048]{2,1,0:T(8,128)} %own.1), channel_id=1, source_target_pairs={{0,16},{16,0},{32,48},{48,32},{64,80},{80,64},{96,112},{112,96},{1... | collective-permute-start | bytes 3145736 | tf_op jit(solution)/shard_map/ppermute | solution.py:16
  55.8 1.2 copy-start.1
  82.5 15.8 %all-to-all-start.1 = ((f32[16,128,128]{2,1,0:T(8,128)}), f32[16,128,128]{2,1,0:T(8,128)S(1)}, u32[]{:S(2)}, u32[]{:S(2)}) async-start(f32[16,128,128]{2,1,0:T(8,128)} %shard_map.69), calls=%async_computation.1 | async-start | bytes 2097152 | tf_op jit(solution)/shard_map/all_to_all | solution.py:22
  86.2 12.1 %collective-permute-start.2 = (f32[16,64,128]{2,1,0:T(8,128)}, f32[16,64,128]{2,1,0:T(8,128)}, u32[]{:S(2)}, u32[]{:S(2)}) collective-permute-start(f32[16,64,128]{2,1,0:T(8,128)} %all-to-all-done.2.own), channel_id=1, source_target_pairs={{0,16},{16,0},{32,48},{48,32},{64,80},{80,64},{96,112},{112,96},{1... | collective-permute-start | bytes 1572872 | tf_op jit(solution)/shard_map/ppermute | solution.py:16
  91.7 3.1 %collective-permute-start.3 = (f32[64,128]{1,0:T(8,128)S(1)}, f32[64,128]{1,0:T(8,128)S(1)}, u32[]{:S(2)}, u32[]{:S(2)}) collective-permute-start(f32[64,128]{1,0:T(8,128)S(1)} %get-tuple-element.17), channel_id=1, source_target_pairs={{0,16},{16,0},{32,48},{48,32},{64,80},{80,64},{96,112},{112,96},{1... | collective-permute-start | bytes 98312 | tf_op jit(solution)/shard_map/ppermute | solution.py:16
  98.3 50.4 %copy-start = (f32[16,128,128]{2,1,0:T(8,128)}, f32[16,128,128]{2,1,0:T(8,128)S(1)}, u32[]{:S(2)}) copy-start(f32[16,128,128]{2,1,0:T(8,128)S(1)} %all-to-all-done.1) | copy-start | bytes 3145732
  121.9 16.7 %all-to-all-start.4 = ((f32[16,128,128]{2,1,0:T(8,128)}), f32[16,128,128]{2,1,0:T(8,128)S(1)}, u32[]{:S(2)}, u32[]{:S(2)}) async-start(f32[16,128,128]{2,1,0:T(8,128)} %shard_map.71), calls=%async_computation.4 | async-start | bytes 2097152 | tf_op jit(solution)/shard_map/all_to_all | solution.py:22
  126.3 20.0 %collective-permute-start.1 = (f32[2048,128]{1,0:T(8,128)S(1)}, f32[2048,128]{1,0:T(8,128)S(1)}, u32[]{:S(2)}, u32[]{:S(2)}) collective-permute-start(f32[2048,128]{1,0:T(8,128)S(1)} %bitcast.7), channel_id=1, source_target_pairs={{0,16},{16,0},{32,48},{48,32},{64,80},{80,64},{96,112},{112,96},{1... | collective-permute-start | bytes 3145736 | tf_op jit(solution)/shard_map/ppermute | solution.py:16
  138.5 10.1 %copy-start.4 = (f32[16,128,128]{2,1,0:T(8,128)}, f32[16,128,128]{2,1,0:T(8,128)S(1)}, u32[]{:S(2)}) copy-start(f32[16,128,128]{2,1,0:T(8,128)S(1)} %all-to-all-done.4) | copy-start | bytes 3145732
  138.5 10.1 %collective-permute-start.4 = (f32[2048,128]{1,0:T(8,128)S(1)}, f32[2048,128]{1,0:T(8,128)}, u32[]{:S(2)}, u32[]{:S(2)}) collective-permute-start(f32[2048,128]{1,0:T(8,128)S(1)} %bitcast.12), channel_id=1, source_target_pairs={{0,16},{16,0},{32,48},{48,32},{64,80},{80,64},{96,112},{112,96},{1... | collective-permute-start | bytes 3145736 | tf_op jit(solution)/shard_map/ppermute | solution.py:16
  146.3 2.4 %copy-start.5 = (f32[2048,128]{1,0:T(8,128)}, f32[2048,128]{1,0:T(8,128)S(1)}, u32[]{:S(2)}) copy-start(f32[2048,128]{1,0:T(8,128)S(1)} %collective-permute-done.1.first_other) | copy-start | bytes 3145732
Sparse Core Ops, SparseCore 0:
  10.1 123.1 all-gather.1

commit v2 on v1

--- a/solution.py
+++ b/solution.py
@@ -26,11 +26,6 @@
 def gather_half(copies):
     chips, cores, rows, half = copies.shape
     return lax.all_to_all(copies.reshape(chips * cores, rows, half), "row", 0, 0, tiled=True).reshape(-1, half)
-
-
-def gather_panels(block):
-    planes = lax.axis_size("col")
-    return lax.all_to_all(jnp.broadcast_to(block[None], (planes,) + block.shape), "col", 0, 0, tiled=True)
 
 
 def split(value):
@@ -198,7 +193,8 @@
     first_head = gather_half(copies)
     inverse_other = swap(diag_inv)
     head_other = swap(head_other)
-    cross = gather_panels(factor_cross)
+    cross = lax.all_gather(factor_cross, "col", axis=0)
+    first_head, cross = lax.optimization_barrier((first_head, cross))
     cross_other = swap(cross)
 
     first = gather_chips(solve_chip(0, diag_inv, inverse_other, first_head))

time: 164 us -> 149 us (0.909)
  waiting for transfers between devices: 40 us -> 9.41 us
  blocking collectives: 46.2 us -> 57.8 us
  starting transfers between devices: 45.5 us -> 48.2 us
  local copies, waits for them, and re-layouts: 3.77 us -> 6.45 us
    all_gather x0 -> x1, blocking collectives: none -> 37.9 us  [local(): cross = lax.all_gather(factor_cross, 'col', axis=0)]
    all_to_all x1 -> x0, blocking collectives: 26.7 us -> none  [gather_half(): lax.all_to_all(copies.reshape(chips * cores, rows, half), 'row', 0, 0, ti...]
    all_to_all x1, waiting for transfers between devices: 23.7 us -> 0.01 us  [gather_half(): lax.all_to_all(copies.reshape(chips * cores, rows, half), 'row', 0, 0, ti...]
    ppermute x5, starting transfers between devices: 23.6 us -> 34.1 us  [swap(): return lax.ppermute(value, 'row', [(i, i ^ 1) for i in range(rows)])]
    all_to_all x1, starting transfers between devices: 13.7 us -> 3.73 us  [gather_half(): lax.all_to_all(copies.reshape(chips * cores, rows, half), 'row', 0, 0, ti...]
    all_to_all x2, waiting for transfers between devices: 9.58 us -> 5.18 us  [gather_chips(): lax.all_to_all(copies, 'row', 0, 0, axis_index_groups=groups, tiled=True)]
    unnamed x12 -> x20, local copies, waits for them, and re-layouts: 2.14 us -> 6.45 us
    ppermute x5, waiting for transfers between devices: 6.03 us -> 3.56 us  [swap(): return lax.ppermute(value, 'row', [(i, i ^ 1) for i in range(rows)])]
  transfers between devices with their start and end apart: 9 -> 9, of which waited for: 6 -> 3; matrix products, arithmetic and copies ran while one was open for 1% -> 0% of each run, Pallas kernels for 4% -> 3%
where the time goes in v2:
time: 149 us; the launch traced here: 148 us
  blocking collectives  57.8 us (39%)
  starting transfers between devices  48.2 us (32%)
  between operations  14.2 us (10%)
  Pallas kernels  12.1 us (8%)
  waiting for transfers between devices  9.41 us (6%)
  local copies, waits for them, and re-layouts  6.45 us (4%)
    all_gather x1, blocking collectives, local(): cross = lax.all_gather(factor_cross, 'col', axis=0)  37.9 us
    ppermute x5, starting transfers between devices, swap(): return lax.ppermute(value, 'row', [(i, i ^ 1) for i in range(rows)])  34.1 us
    all_to_all x1, blocking collectives, gather_chips(): lax.all_to_all(copies, 'row', 0, 0, axis_index_groups=groups, tiled=True)  19.9 us
    all_to_all x2, starting transfers between devices, gather_chips(): lax.all_to_all(copies, 'row', 0, 0, axis_index_groups=groups, tiled=True)  10.3 us
    pallas_call x1, Pallas kernels, tail_rows(): pl.pallas_call(tail_kernel, grid=(TAIL_STEPS,), in_specs=[whole(tail.shap...  7.72 us
    unnamed x20, local copies, waits for them, and re-layouts  6.45 us
    all_to_all x2, waiting for transfers between devices, gather_chips(): lax.all_to_all(copies, 'row', 0, 0, axis_index_groups=groups, tiled=True)  5.18 us
    all_to_all x1, starting transfers between devices, gather_half(): lax.all_to_all(copies.reshape(chips * cores, rows, half), 'row', 0, 0, ti...  3.73 us
  transfers between devices with their start and end apart: 9, of which 3 were waited for; matrix products, arithmetic and copies ran while one was open for 0% of the time, Pallas kernels for 3%

profile of v2, /device:TPU:1, one launch (start us, length us, event | category | flops | bytes accessed | tf_op | source)
XLA Modules:
  0.0 148.1 jit_solution(5962147637325325242)
XLA Ops:
  7.2 0.0 all-gather.3.cloned.1.call-start
  7.2 0.0 copy-start.2
  7.2 0.7 all-gather.3.cloned.1.call-update
  7.9 0.9 copy-done.7
  8.8 0.1 shard_map.68
  8.9 1.1 copy-done.4
  10.0 8.8 %collective-permute-start = (f32[2,64,2048]{2,1,0:T(8,128)}, f32[2,64,2048]{2,1,0:T(8,128)S(1)}, u32[]{:S(2)}, u32[]{:S(2)}) collective-permute-start(f32[2,64,2048]{2,1,0:T(8,128)} %own.1), channel_id=1, source_target_pairs={{0,16},{16,0},{32,48},{48,32},{64,80},{80,64},{96,112},{112,96},{1... | collective-permute-start | bytes 3145736 | tf_op jit(solution)/shard_map/ppermute | solution.py:16
  18.8 3.7 %all-to-all-start = ((f32[32,64,128]{2,1,0:T(8,128)}), f32[32,64,128]{2,1,0:T(8,128)S(1)}, u32[]{:S(2)}, u32[]{:S(2)}) async-start(f32[32,64,128]{2,1,0:T(8,128)} %bitcast.14), calls=%async_computation | async-start | bytes 2097152 | tf_op jit(solution)/shard_map/all_to_all | solution.py:28
  22.5 37.9 %all-gather = f32[1024,128]{1,0:T(8,128)} all-gather(f32[64,128]{1,0:T(8,128)} %param.8), channel_id=2, replica_groups=mesh['row'=32,'col'=16] {'col'}, dimensions={0}, use_global_device_ids=true | all-gather | bytes 557056 | tf_op jit(solution)/shard_map/all_gather | solution.py:196
  60.4 0.0 all-to-all-done
  60.4 0.0 collective-permute-done.other
  60.4 1.2 copy-done.1
  61.6 1.8 %shard_map.69 = f32[16,128,128]{2,1,0:T(8,128)} custom-call(f32[2,64,2048]{2,1,0:T(8,128)S(1)} %copy-done.1, f32[2,64,2048]{2,1,0:T(8,128)S(1)} %collective-permute-done.other, f32[2048,128]{1,0:T(8,128)S(1)} %bitcast.10), custom_call_target="tpu_custom_call" | custom-call | flops 201326592 | bytes 3145728 | tf_op jit(solution)/shard_map/pallas_call | solution.py:137
  63.4 6.7 %all-to-all-start.1 = ((f32[16,128,128]{2,1,0:T(8,128)}), f32[16,128,128]{2,1,0:T(8,128)S(1)}, u32[]{:S(2)}, u32[]{:S(2)}) async-start(f32[16,128,128]{2,1,0:T(8,128)} %shard_map.69), calls=%async_computation.1 | async-start | bytes 2097152 | tf_op jit(solution)/shard_map/all_to_all | solution.py:22
  70.1 8.5 %collective-permute-start.2 = (f32[16,64,128]{2,1,0:T(8,128)}, f32[16,64,128]{2,1,0:T(8,128)S(1)}, u32[]{:S(2)}, u32[]{:S(2)}) collective-permute-start(f32[16,64,128]{2,1,0:T(8,128)} %bitcast.12), channel_id=1, source_target_pairs={{0,16},{16,0},{32,48},{48,32},{64,80},{80,64},{96,112},{112,96},{1... | collective-permute-start | bytes 1572872 | tf_op jit(solution)/shard_map/ppermute | solution.py:16
  78.6 1.9 %collective-permute-start.3 = (f32[64,128]{1,0:T(8,128)S(1)}, f32[64,128]{1,0:T(8,128)S(1)}, u32[]{:S(2)}, u32[]{:S(2)}) collective-permute-start(f32[64,128]{1,0:T(8,128)S(1)} %get-tuple-element.21), channel_id=1, source_target_pairs={{0,16},{16,0},{32,48},{48,32},{64,80},{80,64},{96,112},{112,96},{1... | collective-permute-start | bytes 98312 | tf_op jit(solution)/shard_map/ppermute | solution.py:16
  80.5 1.2 collective-permute-done.3.head_other
  81.7 0.0 collective-permute-done.2.other
  81.7 0.8 copy-done.5
  82.5 0.0 all-to-all-done.1
  82.5 1.4 copy-done.3
  83.9 1.0 copy-done.6
  85.0 0.7 shard_map.70
  85.7 19.9 %all_to_all.20 = f32[16,128,128]{2,1,0:T(8,128)S(1)} all-to-all(f32[16,128,128]{2,1,0:T(8,128)S(1)} %shard_map.70), channel_id=1, replica_groups={{0,32,64,96,128,160,192,224,256,288,320,352,384,416,448,480},{16,48,80,..., dimensions={0} | all-to-all | bytes 2097152 | tf_op jit(solution)/shard_map/all_to_all | solution.py:22
  105.6 1.8 %shard_map.71 = f32[16,128,128]{2,1,0:T(8,128)} custom-call(f32[2,64,2048]{2,1,0:T(8,128)S(1)} %copy-done.2, f32[2,64,2048]{2,1,0:T(8,128)S(1)} %collective-permute-done.other, f32[2048,128]{1,0:T(8,128)S(1)} %bitcast.11), custom_call_target="tpu_custom_call" | custom-call | flops 201326592 | bytes 3145728 | tf_op jit(solution)/shard_map/pallas_call | solution.py:137
  107.4 3.7 %all-to-all-start.3 = ((f32[16,128,128]{2,1,0:T(8,128)}), f32[16,128,128]{2,1,0:T(8,128)S(1)}, u32[]{:S(2)}, u32[]{:S(2)}) async-start(f32[16,128,128]{2,1,0:T(8,128)} %shard_map.71), calls=%async_computation.3 | async-start | bytes 2097152 | tf_op jit(solution)/shard_map/all_to_all | solution.py:22
  111.1 6.8 %collective-permute-start.1 = (f32[2048,128]{1,0:T(8,128)S(1)}, f32[2048,128]{1,0:T(8,128)S(1)}, u32[]{:S(2)}, u32[]{:S(2)}) collective-permute-start(f32[2048,128]{1,0:T(8,128)S(1)} %bitcast.8), channel_id=1, source_target_pairs={{0,16},{16,0},{32,48},{48,32},{64,80},{80,64},{96,112},{112,96},{1... | collective-permute-start | bytes 3145736 | tf_op jit(solution)/shard_map/ppermute | solution.py:16
  117.8 5.2 %all-to-all-done.3 = f32[16,128,128]{2,1,0:T(8,128)S(1)} async-done(((f32[16,128,128]{2,1,0:T(8,128)}), f32[16,128,128]{2,1,0:T(8,128)S(1)}, u32[]{:S(2)}, u32[]{:S(2)}) %all-to-all-start.3) | async-done | bytes 1048608 | tf_op jit(solution)/shard_map/all_to_all | solution.py:22
  123.0 8.1 %collective-permute-start.4 = (f32[2048,128]{1,0:T(8,128)S(1)}, f32[2048,128]{1,0:T(8,128)}, u32[]{:S(2)}, u32[]{:S(2)}) collective-permute-start(f32[2048,128]{1,0:T(8,128)S(1)} %bitcast.15), channel_id=1, source_target_pairs={{0,16},{16,0},{32,48},{48,32},{64,80},{80,64},{96,112},{112,96},{1... | collective-permute-start | bytes 3145736 | tf_op jit(solution)/shard_map/ppermute | solution.py:16
  131.1 0.0 collective-permute-done.1.first_other
  131.1 2.4 %collective-permute-done.4.second_other = f32[2048,128]{1,0:T(8,128)} collective-permute-done((f32[2048,128]{1,0:T(8,128)S(1)}, f32[2048,128]{1,0:T(8,128)}, u32[]{:S(2)}, u32[]{:S(2)}) %collective-permute-start.4) | collective-permute-done | bytes 1048608 | tf_op jit(solution)/shard_map/ppermute | solution.py:16
  133.5 7.7 %shard_map.72 = (f32[448,256]{1,0:T(8,128)}, f32[2,64,256]{2,1,0:T(8,128)}) custom-call(f32[448,256]{1,0:T(8,128)} %tail.1, f32[16,896,128]{2,1,0:T(8,128)} %all-gather.3.cloned.1.call-done.factor, f32[2048,128]{1,0:T(8,128)} %bitcast.9, f32[2048,128]{1,0:T(8,128)} %copy-done.9, f32[2048,128]{1,0:T(8,128)} %bitcast.16, ...), custom_call_target="tpu_custom_call" | custom-call | flops 2818572288 | bytes 7340032 | tf_op jit(solution)/shard_map/pallas_call | solution.py:170
  (14 shorter events, 0.0 us)
Async XLA Ops:
  7.2 126.3 %all-gather.3.cloned.1.call-start = ((), (), s32[]{:S(2)}) async-start(), calls=%async_computation.4 | async-start | bytes 7798784 | tf_op jit(solution)/shard_map/all_gather | solution.py:188
  7.2 98.4 %copy-start.2 = (f32[2,64,2048]{2,1,0:T(8,128)S(1)}, f32[2,64,2048]{2,1,0:T(8,128)}, u32[]{:S(2)}) copy-start(f32[2,64,2048]{2,1,0:T(8,128)} %own.1) | copy-start | bytes 3145732
  7.9 0.9 copy-start.7
  8.9 1.1 copy-start.4
  10.0 50.4 %collective-permute-start = (f32[2,64,2048]{2,1,0:T(8,128)}, f32[2,64,2048]{2,1,0:T(8,128)S(1)}, u32[]{:S(2)}, u32[]{:S(2)}) collective-permute-start(f32[2,64,2048]{2,1,0:T(8,128)} %own.1), channel_id=1, source_target_pairs={{0,16},{16,0},{32,48},{48,32},{64,80},{80,64},{96,112},{112,96},{1... | collective-permute-start | bytes 3145736 | tf_op jit(solution)/shard_map/ppermute | solution.py:16
  18.8 41.6 %all-to-all-start = ((f32[32,64,128]{2,1,0:T(8,128)}), f32[32,64,128]{2,1,0:T(8,128)S(1)}, u32[]{:S(2)}, u32[]{:S(2)}) async-start(f32[32,64,128]{2,1,0:T(8,128)} %bitcast.14), calls=%async_computation | async-start | bytes 2097152 | tf_op jit(solution)/shard_map/all_to_all | solution.py:28
  60.4 1.2 copy-start.1
  63.4 19.1 %all-to-all-start.1 = ((f32[16,128,128]{2,1,0:T(8,128)}), f32[16,128,128]{2,1,0:T(8,128)S(1)}, u32[]{:S(2)}, u32[]{:S(2)}) async-start(f32[16,128,128]{2,1,0:T(8,128)} %shard_map.69), calls=%async_computation.1 | async-start | bytes 2097152 | tf_op jit(solution)/shard_map/all_to_all | solution.py:22
  70.1 11.7 %collective-permute-start.2 = (f32[16,64,128]{2,1,0:T(8,128)}, f32[16,64,128]{2,1,0:T(8,128)S(1)}, u32[]{:S(2)}, u32[]{:S(2)}) collective-permute-start(f32[16,64,128]{2,1,0:T(8,128)} %bitcast.12), channel_id=1, source_target_pairs={{0,16},{16,0},{32,48},{48,32},{64,80},{80,64},{96,112},{112,96},{1... | collective-permute-start | bytes 1572872 | tf_op jit(solution)/shard_map/ppermute | solution.py:16
  78.6 3.1 %collective-permute-start.3 = (f32[64,128]{1,0:T(8,128)S(1)}, f32[64,128]{1,0:T(8,128)S(1)}, u32[]{:S(2)}, u32[]{:S(2)}) collective-permute-start(f32[64,128]{1,0:T(8,128)S(1)} %get-tuple-element.21), channel_id=1, source_target_pairs={{0,16},{16,0},{32,48},{48,32},{64,80},{80,64},{96,112},{112,96},{1... | collective-permute-start | bytes 98312 | tf_op jit(solution)/shard_map/ppermute | solution.py:16
  81.7 0.8 copy-start.5
  82.5 51.0 %copy-start = (f32[16,128,128]{2,1,0:T(8,128)}, f32[16,128,128]{2,1,0:T(8,128)S(1)}, u32[]{:S(2)}) copy-start(f32[16,128,128]{2,1,0:T(8,128)S(1)} %all-to-all-done.1) | copy-start | bytes 3145732
  82.5 1.4 copy-start.3
  83.9 1.1 copy-start.6
  107.4 15.6 %all-to-all-start.3 = ((f32[16,128,128]{2,1,0:T(8,128)}), f32[16,128,128]{2,1,0:T(8,128)S(1)}, u32[]{:S(2)}, u32[]{:S(2)}) async-start(f32[16,128,128]{2,1,0:T(8,128)} %shard_map.71), calls=%async_computation.3 | async-start | bytes 2097152 | tf_op jit(solution)/shard_map/all_to_all | solution.py:22
  111.1 20.0 %collective-permute-start.1 = (f32[2048,128]{1,0:T(8,128)S(1)}, f32[2048,128]{1,0:T(8,128)S(1)}, u32[]{:S(2)}, u32[]{:S(2)}) collective-permute-start(f32[2048,128]{1,0:T(8,128)S(1)} %bitcast.8), channel_id=1, source_target_pairs={{0,16},{16,0},{32,48},{48,32},{64,80},{80,64},{96,112},{112,96},{1... | collective-permute-start | bytes 3145736 | tf_op jit(solution)/shard_map/ppermute | solution.py:16
  123.0 10.5 %copy-start.8 = (f32[16,128,128]{2,1,0:T(8,128)}, f32[16,128,128]{2,1,0:T(8,128)S(1)}, u32[]{:S(2)}) copy-start(f32[16,128,128]{2,1,0:T(8,128)S(1)} %all-to-all-done.3) | copy-start | bytes 3145732
  123.0 10.5 %collective-permute-start.4 = (f32[2048,128]{1,0:T(8,128)S(1)}, f32[2048,128]{1,0:T(8,128)}, u32[]{:S(2)}, u32[]{:S(2)}) collective-permute-start(f32[2048,128]{1,0:T(8,128)S(1)} %bitcast.15), channel_id=1, source_target_pairs={{0,16},{16,0},{32,48},{48,32},{64,80},{80,64},{96,112},{112,96},{1... | collective-permute-start | bytes 3145736 | tf_op jit(solution)/shard_map/ppermute | solution.py:16
  131.1 2.4 %copy-start.9 = (f32[2048,128]{1,0:T(8,128)}, f32[2048,128]{1,0:T(8,128)S(1)}, u32[]{:S(2)}) copy-start(f32[2048,128]{1,0:T(8,128)S(1)} %collective-permute-done.1.first_other) | copy-start | bytes 3145732
Sparse Core Ops, SparseCore 0:
  10.1 105.8 all-gather.2

commit v3 on v2

--- a/solution.py
+++ b/solution.py
@@ -51,26 +51,34 @@
         out[chip] = value
 
 
-def prepare_kernel(heads, copies, keep, send):
-    half = keep.shape[1]
-    halves = [heads[0][:, core * half : (core + 1) * half] for core in range(CORES)]
-    for chip in range(copies.shape[0]):
+def prepare_kernel(heads, cross, first_copies, second_copies, cross_copies):
+    half = first_copies.shape[3]
+    for chip in range(cross_copies.shape[0]):
+        cross_copies[chip] = cross[...]
         for core in range(CORES):
-            copies[chip, core] = halves[core]
-    first = lax.axis_index("row") % CORES == 0
-    left, right = heads[1][:, :half], heads[1][:, half:]
-    keep[...] = jnp.where(first, left, right)
-    send[...] = jnp.where(first, right, left)
+            columns = slice(core * half, (core + 1) * half)
+            first_copies[chip, core] = heads[0][:, columns]
+            second_copies[chip, core] = heads[1][:, columns]
 
 
 def solve_kernel(own, other, operand, out):
     spread(product(in_order(own[0], other[0], 0), operand[...]), out)
 
 
-def cross_kernel(own, other, head, head_other, operand, out):
+def cross_kernel(own, other, cross, keep, send):
+    right = []
+    for chip in range(cross.shape[0]):
+        right.append(in_order(cross[chip], jnp.zeros_like(cross[chip]), 0))
+    part = product(jnp.concatenate([own[0], other[0]], axis=0), jnp.concatenate(right, axis=0))
+    rows = keep.shape[0]
+    keep[...] = part[:rows]
+    send[...] = part[rows:]
+
+
+def second_kernel(own, other, cross, cross_other, operand, first, out):
     row_of = lambda blocks: jnp.concatenate([blocks[i] for i in range(blocks.shape[0])], axis=1)
-    left = in_order(row_of(own), row_of(other), 0)
-    spread(in_order(head[...], head_other[...], 0) - product(left, operand[...]), out)
+    solved = product(in_order(own[0], other[0], 0), operand[...])
+    spread(solved - product(in_order(row_of(cross), row_of(cross_other), 0), first[...]), out)
 
 
 def tail_kernel(tail, factor, first, first_other, second, second_other, out, solved, total):
@@ -115,46 +123,32 @@
     return pl.CostEstimate(flops=flops, bytes_accessed=size, transcendentals=0)
 
 
-def prepare(heads):
+def prepare(heads, cross):
     _, rows, columns = heads.shape
-    half = columns // CORES
     chips = lax.axis_size("row") // CORES
-    part = jax.ShapeDtypeStruct((rows, half), jnp.float32)
+    copies = jax.ShapeDtypeStruct((chips, CORES, rows, columns // CORES), jnp.float32)
     return pl.pallas_call(
         prepare_kernel,
-        out_shape=(jax.ShapeDtypeStruct((chips, CORES, rows, half), jnp.float32), part, part),
-        compiler_params=params(8),
-        cost_estimate=estimate(0, 4 * (chips + 3) * rows * columns),
-    )(heads)
-
-
-def solve_chip(panel, own, other, operand):
+        out_shape=(copies, copies, jax.ShapeDtypeStruct((chips,) + cross.shape, jnp.float32)),
+        compiler_params=params(12),
+        cost_estimate=estimate(0, 10 * (chips + 2) * rows * columns),
+    )(heads, cross)
+
+
+def on_chip(kernel, panel, own, other, operands, shapes, flops):
     _, rows, depth = own.shape
-    columns = operand.shape[1]
-    chips = lax.axis_size("row") // CORES
     inverse = pl.BlockSpec((1, rows, depth), lambda step: (panel, 0, 0))
-    shape = (chips, CORES * rows, columns)
+    whole = lambda shape: pl.BlockSpec(shape, lambda step: (0,) * len(shape))
+    size = 8 * rows * depth + 4 * sum(operand.size for operand in operands)
     return pl.pallas_call(
-        solve_kernel,
+        kernel,
         grid=(1,),
-        in_specs=[inverse, inverse, pl.BlockSpec(operand.shape, lambda step: (0, 0))],
-        out_specs=pl.BlockSpec(shape, lambda step: (0, 0, 0)),
-        out_shape=jax.ShapeDtypeStruct(shape, jnp.float32),
-        compiler_params=params(16),
-        cost_estimate=estimate(12 * rows * depth * columns, 4 * depth * (2 * rows + 2 * columns)),
-    )(own, other, operand)
-
-
-def cross_chip(own, other, head, head_other, operand):
-    _, rows, _ = own.shape
-    depth, columns = operand.shape
-    chips = lax.axis_size("row") // CORES
-    return pl.pallas_call(
-        cross_kernel,
-        out_shape=jax.ShapeDtypeStruct((chips, CORES * rows, columns), jnp.float32),
-        compiler_params=params(16),
-        cost_estimate=estimate(12 * rows * depth * columns, 4 * depth * (2 * rows + 2 * columns)),
-    )(own, other, head, head_other, operand)
+        in_specs=[inverse, inverse] + [whole(operand.shape) for operand in operands],
+        out_specs=[whole(shape) for shape in shapes],
+        out_shape=[jax.ShapeDtypeStruct(shape, jnp.float32) for shape in shapes],
+        compiler_params=params(20),
+        cost_estimate=estimate(flops, size),
+    )(own, other, *operands)
 
 
 def tail_rows(tail, factor, halves):
@@ -185,21 +179,31 @@
 
 def local(rhs_head, rhs_tail, diag_inv, factor_cross, factor_tail):
     rows, _, width = factor_tail.shape
+    head_rows, depth = diag_inv.shape[1:]
+    chips = lax.axis_size("row") // CORES
+    chip_copies = (chips, CORES * head_rows, rhs_head.shape[2] // CORES)
+    flops = 12 * head_rows * depth * chip_copies[2]
+
     factor = lax.all_gather(factor_tail.reshape(2 * rows, width), "col", axis=0)
-    copies, head, head_other = prepare(rhs_head)
-    copies, diag_inv, factor_cross, head_other = lax.optimization_barrier(
-        (copies, diag_inv, factor_cross, head_other)
+    first_copies, second_copies, cross_copies = prepare(rhs_head, factor_cross)
+    first_copies, cross_copies, inverse = lax.optimization_barrier((first_copies, cross_copies, diag_inv))
+    cross = gather_chips(cross_copies).reshape(cross_copies.shape)
+    first_head = gather_half(first_copies)
+    inverse_other = swap(inverse)
+    part = (head_rows, width)
+    keep, send = on_chip(cross_kernel, 1, diag_inv, inverse_other, (cross,), (part, part), flops)
+    product_rows = keep + swap(send)
+
+    (first_copies,) = on_chip(solve_kernel, 0, diag_inv, inverse_other, (first_head,), (chip_copies,), flops)
+    first_copies, second_copies, product_rows = lax.optimization_barrier(
+        (first_copies, second_copies, product_rows)
     )
-    first_head = gather_half(copies)
-    inverse_other = swap(diag_inv)
-    head_other = swap(head_other)
-    cross = lax.all_gather(factor_cross, "col", axis=0)
-    first_head, cross = lax.optimization_barrier((first_head, cross))
-    cross_other = swap(cross)
-
-    first = gather_chips(solve_chip(0, diag_inv, inverse_other, first_head))
-    second_head = gather_chips(cross_chip(cross, cross_other, head, head_other, first))
-    second = gather_chips(solve_chip(1, diag_inv, inverse_other, second_head))
+    first = gather_chips(first_copies)
+    second_head = gather_half(second_copies)
+    cross = lax.all_gather(product_rows, "col", axis=0)
+    operands = (cross, swap(cross), second_head, first)
+    (second_copies,) = on_chip(second_kernel, 1, diag_inv, inverse_other, operands, (chip_copies,), 2 * flops)
+    second = gather_chips(second_copies)
     tail, solved = tail_rows(rhs_tail, factor, (first, swap(first), second, swap(second)))
     return solved, tail
 

time: 149 us -> 178 us (1.19)
  waiting for transfers between devices: 9.41 us -> 32.3 us
  local copies, waits for them, and re-layouts: 6.45 us -> 12.7 us
  blocking collectives: 57.8 us -> 55.2 us
  starting transfers between devices: 48.2 us -> 50.5 us
    ppermute x5, starting transfers between devices: 34.1 us -> 22 us  [swap(): return lax.ppermute(value, 'row', [(i, i ^ 1) for i in range(rows)])]
    all_to_all x1 -> x2, waiting for transfers between devices: 0.01 us -> 11.8 us  [gather_half(): lax.all_to_all(copies.reshape(chips * cores, rows, half), 'row', 0, 0, ti...]
    all_to_all x2, waiting for transfers between devices: 5.18 us -> 16.7 us  [gather_chips(): lax.all_to_all(copies, 'row', 0, 0, axis_index_groups=groups, tiled=True)]
    all_to_all x1 -> x2, starting transfers between devices: 3.73 us -> 13.8 us  [gather_half(): lax.all_to_all(copies.reshape(chips * cores, rows, half), 'row', 0, 0, ti...]
    unnamed x20 -> x34, local copies, waits for them, and re-layouts: 6.45 us -> 12.7 us
    all_to_all x2, starting transfers between devices: 10.3 us -> 14.6 us  [gather_chips(): lax.all_to_all(copies, 'row', 0, 0, axis_index_groups=groups, tiled=True)]
  transfers between devices with their start and end apart: 9 -> 10, of which waited for: 3 -> 5; matrix products, arithmetic and copies ran while one was open for 0% -> 0% of each run, Pallas kernels for 3% -> 3%
where the time goes in v3:
time: 178 us; the launch traced here: 177 us
  blocking collectives  55.2 us (31%)
  starting transfers between devices  50.5 us (28%)
  waiting for transfers between devices  32.3 us (18%)
  between operations  14.2 us (8%)
  local copies, waits for them, and re-layouts  12.7 us (7%)
  Pallas kernels  12.4 us (7%)
    all_gather x1, blocking collectives, local(): cross = lax.all_gather(product_rows, 'col', axis=0)  36.3 us
    ppermute x5, starting transfers between devices, swap(): return lax.ppermute(value, 'row', [(i, i ^ 1) for i in range(rows)])  22 us
    all_to_all x1, blocking collectives, gather_chips(): lax.all_to_all(copies, 'row', 0, 0, axis_index_groups=groups, tiled=True)  18.9 us
    all_to_all x2, waiting for transfers between devices, gather_chips(): lax.all_to_all(copies, 'row', 0, 0, axis_index_groups=groups, tiled=True)  16.7 us
    all_to_all x2, starting transfers between devices, gather_chips(): lax.all_to_all(copies, 'row', 0, 0, axis_index_groups=groups, tiled=True)  14.6 us
    all_to_all x2, starting transfers between devices, gather_half(): lax.all_to_all(copies.reshape(chips * cores, rows, half), 'row', 0, 0, ti...  13.8 us
    unnamed x34, local copies, waits for them, and re-layouts  12.7 us
    all_to_all x2, waiting for transfers between devices, gather_half(): lax.all_to_all(copies.reshape(chips * cores, rows, half), 'row', 0, 0, ti...  11.8 us
  transfers between devices with their start and end apart: 10, of which 5 were waited for; matrix products, arithmetic and copies ran while one was open for 0% of the time, Pallas kernels for 3%

profile of v3, /device:TPU:1, one launch (start us, length us, event | category | flops | bytes accessed | tf_op | source)
XLA Modules:
  0.0 177.4 jit_solution(17216982449567953748)
XLA Ops:
  7.9 0.9 copy-done.13
  8.8 0.8 copy-done.14
  9.6 0.9 shard_map.68
  10.5 1.0 copy-done.9
  11.5 1.1 copy-done.10
  12.6 7.7 %all-to-all-start.1 = ((f32[16,64,128]{2,1,0:T(8,128)}), f32[16,64,128]{2,1,0:T(8,128)S(1)}, u32[]{:S(2)}, u32[]{:S(2)}) async-start(f32[16,64,128]{2,1,0:T(8,128)} %get-tuple-element.20), calls=%async_computation.1 | async-start | bytes 1048576 | tf_op jit(solution)/shard_map/all_to_all | solution.py:22
  20.3 4.8 %collective-permute-start = (f32[2,64,2048]{2,1,0:T(8,128)}, f32[2,64,2048]{2,1,0:T(8,128)S(1)}, u32[]{:S(2)}, u32[]{:S(2)}) collective-permute-start(f32[2,64,2048]{2,1,0:T(8,128)} %own.5), channel_id=1, source_target_pairs={{0,16},{16,0},{32,48},{48,32},{64,80},{80,64},{96,112},{112,96},{1... | collective-permute-start | bytes 3145736 | tf_op jit(solution)/shard_map/ppermute | solution.py:16
  25.1 4.3 %all-to-all-done.1.cross = f32[16,64,128]{2,1,0:T(8,128)S(1)} async-done(((f32[16,64,128]{2,1,0:T(8,128)}), f32[16,64,128]{2,1,0:T(8,128)S(1)}, u32[]{:S(2)}, u32[]{:S(2)}) %all-to-all-start.1) | async-done | bytes 524320 | tf_op jit(solution)/shard_map/all_to_all | solution.py:22
  29.4 0.8 copy-done.5
  30.2 7.4 %all-to-all-start = ((f32[32,64,128]{2,1,0:T(8,128)}), f32[32,64,128]{2,1,0:T(8,128)S(1)}, u32[]{:S(2)}, u32[]{:S(2)}) async-start(f32[32,64,128]{2,1,0:T(8,128)} %bitcast.15), calls=%async_computation | async-start | bytes 2097152 | tf_op jit(solution)/shard_map/all_to_all | solution.py:28
  37.7 1.2 copy-done.1
  38.9 1.0 copy-done.6
  40.6 2.2 %collective-permute-start.1 = (f32[64,128]{1,0:T(8,128)S(1)}, f32[64,128]{1,0:T(8,128)S(1)}, u32[]{:S(2)}, u32[]{:S(2)}) collective-permute-start(f32[64,128]{1,0:T(8,128)S(1)} %get-tuple-element.22), channel_id=1, source_target_pairs={{0,16},{16,0},{32,48},{48,32},{64,80},{80,64},{96,112},{112,96},{1... | collective-permute-start | bytes 98312 | tf_op jit(solution)/shard_map/ppermute | solution.py:16
  42.8 11.8 %all-to-all-done = f32[32,64,128]{2,1,0:T(8,128)S(1)} async-done(((f32[32,64,128]{2,1,0:T(8,128)}), f32[32,64,128]{2,1,0:T(8,128)S(1)}, u32[]{:S(2)}, u32[]{:S(2)}) %all-to-all-start) | async-done | bytes 1048608 | tf_op jit(solution)/shard_map/all_to_all | solution.py:28
  54.6 1.2 copy-done.2
  56.6 18.9 %all_to_all.25 = f32[16,128,128]{2,1,0:T(8,128)S(1)} all-to-all(f32[16,128,128]{2,1,0:T(8,128)S(1)} %shard_map.69), channel_id=1, replica_groups={{0,32,64,96,128,160,192,224,256,288,320,352,384,416,448,480},{16,48,80,..., dimensions={0} | all-to-all | bytes 2097152 | tf_op jit(solution)/shard_map/all_to_all | solution.py:22
  75.5 6.3 %all-to-all-start.3 = ((f32[32,64,128]{2,1,0:T(8,128)}), f32[32,64,128]{2,1,0:T(8,128)}, u32[]{:S(2)}, u32[]{:S(2)}) async-start(f32[32,64,128]{2,1,0:T(8,128)} %bitcast.14), calls=%async_computation.3 | async-start | bytes 2097152 | tf_op jit(solution)/shard_map/all_to_all | solution.py:28
  81.9 36.3 %all-gather = f32[1024,128]{1,0:T(8,128)S(1)} all-gather(f32[64,128]{1,0:T(8,128)S(1)} %add.3), channel_id=2, replica_groups=mesh['row'=32,'col'=16] {'col'}, dimensions={0}, use_global_device_ids=true | all-gather | bytes 557056 | tf_op jit(solution)/shard_map/all_gather | solution.py:203
  118.2 6.8 %collective-permute-start.3 = (f32[16,64,128]{2,1,0:T(8,128)S(1)}, f32[16,64,128]{2,1,0:T(8,128)S(1)}, u32[]{:S(2)}, u32[]{:S(2)}) collective-permute-start(f32[16,64,128]{2,1,0:T(8,128)S(1)} %bitcast.12), channel_id=1, source_target_pairs={{0,16},{16,0},{32,48},{48,32},{64,80},{80,64},{96,112},{112,96},{1... | collective-permute-start | bytes 1572872 | tf_op jit(solution)/shard_map/ppermute | solution.py:16
  125.0 0.8 copy-done.7
  125.8 0.7 collective-permute-done.3.cross_other
  126.5 0.8 copy-done.11
  127.3 1.0 copy-done.8
  128.3 1.0 copy-done.12
  129.4 2.4 %shard_map.71 = f32[16,128,128]{2,1,0:T(8,128)S(1)} custom-call(f32[2,64,2048]{2,1,0:T(8,128)S(1)} %copy-done.3, f32[2,64,2048]{2,1,0:T(8,128)S(1)} %collective-permute-done.other, f32[16,64,128]{2,1,0:T(8,128)S(1)} %bitcast.13, f32[16,64,128]{2,1,0:T(8,128)S(1)} %copy-done.12, f32[2048,128]{1,0:T(8,128)} %bitcast.6.operand, f32[2048,128]{1,0:T(8,128)S(1)} %bitcast.8), custom_call_target="tpu_custom_call" | custom-call | flops 402653184 | bytes 4194304 | tf_op jit(solution)/shard_map/pallas_call | solution.py:143
  131.8 1.0 copy-done.4
  132.8 6.9 %all-to-all-start.4 = ((f32[16,128,128]{2,1,0:T(8,128)}), f32[16,128,128]{2,1,0:T(8,128)S(1)}, u32[]{:S(2)}, u32[]{:S(2)}) async-start(f32[16,128,128]{2,1,0:T(8,128)} %copy-done.4), calls=%async_computation.4 | async-start | bytes 2097152 | tf_op jit(solution)/shard_map/all_to_all | solution.py:22
  139.7 2.6 %collective-permute-start.2 = (f32[2048,128]{1,0:T(8,128)S(1)}, f32[2048,128]{1,0:T(8,128)S(1)}, u32[]{:S(2)}, u32[]{:S(2)}) collective-permute-start(f32[2048,128]{1,0:T(8,128)S(1)} %bitcast.9), channel_id=1, source_target_pairs={{0,16},{16,0},{32,48},{48,32},{64,80},{80,64},{96,112},{112,96},{1... | collective-permute-start | bytes 3145736 | tf_op jit(solution)/shard_map/ppermute | solution.py:16
  142.3 12.4 %all-to-all-done.4 = f32[16,128,128]{2,1,0:T(8,128)S(1)} async-done(((f32[16,128,128]{2,1,0:T(8,128)}), f32[16,128,128]{2,1,0:T(8,128)S(1)}, u32[]{:S(2)}, u32[]{:S(2)}) %all-to-all-start.4) | async-done | bytes 1048608 | tf_op jit(solution)/shard_map/all_to_all | solution.py:22
  154.7 5.7 %collective-permute-start.4 = (f32[2048,128]{1,0:T(8,128)S(1)}, f32[2048,128]{1,0:T(8,128)}, u32[]{:S(2)}, u32[]{:S(2)}) collective-permute-start(f32[2048,128]{1,0:T(8,128)S(1)} %bitcast.16), channel_id=1, source_target_pairs={{0,16},{16,0},{32,48},{48,32},{64,80},{80,64},{96,112},{112,96},{1... | collective-permute-start | bytes 3145736 | tf_op jit(solution)/shard_map/ppermute | solution.py:16
  160.4 2.4 %collective-permute-done.4.second_other = f32[2048,128]{1,0:T(8,128)} collective-permute-done((f32[2048,128]{1,0:T(8,128)S(1)}, f32[2048,128]{1,0:T(8,128)}, u32[]{:S(2)}, u32[]{:S(2)}) %collective-permute-start.4) | collective-permute-done | bytes 1048608 | tf_op jit(solution)/shard_map/ppermute | solution.py:16
  162.8 7.7 %shard_map.72 = (f32[448,256]{1,0:T(8,128)}, f32[2,64,256]{2,1,0:T(8,128)}) custom-call(f32[448,256]{1,0:T(8,128)} %tail.1, f32[16,896,128]{2,1,0:T(8,128)} %all-gather.3.cloned.1.call-done.factor, f32[2048,128]{1,0:T(8,128)} %bitcast.10, f32[2048,128]{1,0:T(8,128)} %copy-done.16, f32[2048,128]{1,0:T(8,128)} %bitcast.17, ...), custom_call_target="tpu_custom_call" | custom-call | flops 2818572288 | bytes 7340032 | tf_op jit(solution)/shard_map/pallas_call | solution.py:164
  (31 shorter events, 2.1 us)
Async XLA Ops:
  7.2 155.6 %all-gather.3.cloned.1.call-start = ((), (), s32[]{:S(2)}) async-start(), calls=%async_computation.5 | async-start | bytes 7798784 | tf_op jit(solution)/shard_map/all_gather | solution.py:187
  7.9 0.9 copy-start.13
  8.8 0.8 copy-start.14
  10.5 1.0 copy-start.9
  11.5 1.1 copy-start.10
  12.6 114.7 %copy-start.3 = (f32[2,64,2048]{2,1,0:T(8,128)S(1)}, f32[2,64,2048]{2,1,0:T(8,128)}, u32[]{:S(2)}) copy-start(f32[2,64,2048]{2,1,0:T(8,128)} %own.5) | copy-start | bytes 3145732
  12.6 16.8 %all-to-all-start.1 = ((f32[16,64,128]{2,1,0:T(8,128)}), f32[16,64,128]{2,1,0:T(8,128)S(1)}, u32[]{:S(2)}, u32[]{:S(2)}) async-start(f32[16,64,128]{2,1,0:T(8,128)} %get-tuple-element.20), calls=%async_computation.1 | async-start | bytes 1048576 | tf_op jit(solution)/shard_map/all_to_all | solution.py:22
  20.3 17.3 %collective-permute-start = (f32[2,64,2048]{2,1,0:T(8,128)}, f32[2,64,2048]{2,1,0:T(8,128)S(1)}, u32[]{:S(2)}, u32[]{:S(2)}) collective-permute-start(f32[2,64,2048]{2,1,0:T(8,128)} %own.5), channel_id=1, source_target_pairs={{0,16},{16,0},{32,48},{48,32},{64,80},{80,64},{96,112},{112,96},{1... | collective-permute-start | bytes 3145736 | tf_op jit(solution)/shard_map/ppermute | solution.py:16
  29.4 0.8 copy-start.5
  30.2 24.4 %all-to-all-start = ((f32[32,64,128]{2,1,0:T(8,128)}), f32[32,64,128]{2,1,0:T(8,128)S(1)}, u32[]{:S(2)}, u32[]{:S(2)}) async-start(f32[32,64,128]{2,1,0:T(8,128)} %bitcast.15), calls=%async_computation | async-start | bytes 2097152 | tf_op jit(solution)/shard_map/all_to_all | solution.py:28
  37.6 1.2 copy-start.1
  38.9 1.0 copy-start.6
  40.6 16.0 %collective-permute-start.1 = (f32[64,128]{1,0:T(8,128)S(1)}, f32[64,128]{1,0:T(8,128)S(1)}, u32[]{:S(2)}, u32[]{:S(2)}) collective-permute-start(f32[64,128]{1,0:T(8,128)S(1)} %get-tuple-element.22), channel_id=1, source_target_pairs={{0,16},{16,0},{32,48},{48,32},{64,80},{80,64},{96,112},{112,96},{1... | collective-permute-start | bytes 98312 | tf_op jit(solution)/shard_map/ppermute | solution.py:16
  54.6 1.2 copy-start.2
  75.5 87.3 %copy-start = (f32[16,128,128]{2,1,0:T(8,128)}, f32[16,128,128]{2,1,0:T(8,128)S(1)}, u32[]{:S(2)}) copy-start(f32[16,128,128]{2,1,0:T(8,128)S(1)} %all_to_all.25) | copy-start | bytes 3145732
  75.5 51.8 %all-to-all-start.3 = ((f32[32,64,128]{2,1,0:T(8,128)}), f32[32,64,128]{2,1,0:T(8,128)}, u32[]{:S(2)}, u32[]{:S(2)}) async-start(f32[32,64,128]{2,1,0:T(8,128)} %bitcast.14), calls=%async_computation.3 | async-start | bytes 2097152 | tf_op jit(solution)/shard_map/all_to_all | solution.py:28
  118.2 8.3 %collective-permute-start.3 = (f32[16,64,128]{2,1,0:T(8,128)S(1)}, f32[16,64,128]{2,1,0:T(8,128)S(1)}, u32[]{:S(2)}, u32[]{:S(2)}) collective-permute-start(f32[16,64,128]{2,1,0:T(8,128)S(1)} %bitcast.12), channel_id=1, source_target_pairs={{0,16},{16,0},{32,48},{48,32},{64,80},{80,64},{96,112},{112,96},{1... | collective-permute-start | bytes 1572872 | tf_op jit(solution)/shard_map/ppermute | solution.py:16
  125.0 0.8 copy-start.7
  126.5 0.8 copy-start.11
  127.3 1.0 copy-start.8
  128.3 1.0 copy-start.12
  131.8 1.0 copy-start.4
  132.8 21.9 %all-to-all-start.4 = ((f32[16,128,128]{2,1,0:T(8,128)}), f32[16,128,128]{2,1,0:T(8,128)S(1)}, u32[]{:S(2)}, u32[]{:S(2)}) async-start(f32[16,128,128]{2,1,0:T(8,128)} %copy-done.4), calls=%async_computation.4 | async-start | bytes 2097152 | tf_op jit(solution)/shard_map/all_to_all | solution.py:22
  139.7 20.7 %collective-permute-start.2 = (f32[2048,128]{1,0:T(8,128)S(1)}, f32[2048,128]{1,0:T(8,128)S(1)}, u32[]{:S(2)}, u32[]{:S(2)}) collective-permute-start(f32[2048,128]{1,0:T(8,128)S(1)} %bitcast.9), channel_id=1, source_target_pairs={{0,16},{16,0},{32,48},{48,32},{64,80},{80,64},{96,112},{112,96},{1... | collective-permute-start | bytes 3145736 | tf_op jit(solution)/shard_map/ppermute | solution.py:16
  154.7 8.1 %copy-start.15 = (f32[16,128,128]{2,1,0:T(8,128)}, f32[16,128,128]{2,1,0:T(8,128)S(1)}, u32[]{:S(2)}) copy-start(f32[16,128,128]{2,1,0:T(8,128)S(1)} %all-to-all-done.4) | copy-start | bytes 3145732
  154.7 8.1 %collective-permute-start.4 = (f32[2048,128]{1,0:T(8,128)S(1)}, f32[2048,128]{1,0:T(8,128)}, u32[]{:S(2)}, u32[]{:S(2)}) collective-permute-start(f32[2048,128]{1,0:T(8,128)S(1)} %bitcast.16), channel_id=1, source_target_pairs={{0,16},{16,0},{32,48},{48,32},{64,80},{80,64},{96,112},{112,96},{1... | collective-permute-start | bytes 3145736 | tf_op jit(solution)/shard_map/ppermute | solution.py:16
  160.4 2.4 %copy-start.16 = (f32[2048,128]{1,0:T(8,128)}, f32[2048,128]{1,0:T(8,128)S(1)}, u32[]{:S(2)}) copy-start(f32[2048,128]{1,0:T(8,128)S(1)} %collective-permute-done.2.first_other) | copy-start | bytes 3145732
Sparse Core Ops, SparseCore 0:
  10.1 104.5 all-gather.2

commit v4 on v2

--- a/solution.py
+++ b/solution.py
@@ -26,6 +26,15 @@
 def gather_half(copies):
     chips, cores, rows, half = copies.shape
     return lax.all_to_all(copies.reshape(chips * cores, rows, half), "row", 0, 0, tiled=True).reshape(-1, half)
+
+
+def pass_on(block, stride):
+    rows, planes = lax.axis_size("row"), lax.axis_size("col")
+    pairs = []
+    for row in range(rows):
+        turn = stride if row % CORES == 0 else -stride
+        pairs += [(row * planes + z, row * planes + (z + turn) % planes) for z in range(planes)]
+    return lax.ppermute(block, ("row", "col"), pairs)
 
 
 def split(value):
@@ -67,10 +76,17 @@
     spread(product(in_order(own[0], other[0], 0), operand[...]), out)
 
 
-def cross_kernel(own, other, head, head_other, operand, out):
-    row_of = lambda blocks: jnp.concatenate([blocks[i] for i in range(blocks.shape[0])], axis=1)
-    left = in_order(row_of(own), row_of(other), 0)
-    spread(in_order(head[...], head_other[...], 0) - product(left, operand[...]), out)
+def cross_kernel(head, head_other, operand, ring, out):
+    planes, width = lax.axis_size("col"), ring.shape[2]
+    here = lax.axis_index("col") + planes
+    turn = 2 * (lax.axis_index("row") % CORES) - 1
+    left, right = [], []
+    for i in range(planes):
+        plane = here + turn * i if i <= planes // 2 else here - turn * (i - planes // 2)
+        left.append(ring[i])
+        right.append(operand[pl.ds(pl.multiple_of(plane % planes * width, width), width), :])
+    update = product(jnp.concatenate(left, axis=1), jnp.concatenate(right, axis=0))
+    spread(in_order(head[...], head_other[...], 0) - update, out)
 
 
 def tail_kernel(tail, factor, first, first_other, second, second_other, out, solved, total):
@@ -145,8 +161,8 @@
     )(own, other, operand)
 
 
-def cross_chip(own, other, head, head_other, operand):
-    _, rows, _ = own.shape
+def cross_chip(head, head_other, operand, ring):
+    rows = head.shape[0]
     depth, columns = operand.shape
     chips = lax.axis_size("row") // CORES
     return pl.pallas_call(
@@ -154,7 +170,7 @@
         out_shape=jax.ShapeDtypeStruct((chips, CORES * rows, columns), jnp.float32),
         compiler_params=params(16),
         cost_estimate=estimate(12 * rows * depth * columns, 4 * depth * (2 * rows + 2 * columns)),
-    )(own, other, head, head_other, operand)
+    )(head, head_other, operand, ring)
 
 
 def tail_rows(tail, factor, halves):
@@ -192,13 +208,25 @@
     )
     first_head = gather_half(copies)
     inverse_other = swap(diag_inv)
+    core = lax.axis_index("row") % CORES
+    cross_other = swap(factor_cross)
+    block = jnp.where(
+        core == 0,
+        jnp.concatenate([factor_cross, cross_other]),
+        jnp.concatenate([cross_other, factor_cross]),
+    )
+    ring = [jnp.stack([pass_on(block, 1), pass_on(block, 2)])]
+    first_head, ring[0] = lax.optimization_barrier((first_head, ring[0]))
+    ring.append(pass_on(ring[-1], 2))
+    first_copies = solve_chip(0, diag_inv, inverse_other, first_head)
+    first_copies, head_other = lax.optimization_barrier((first_copies, head_other))
+    first = gather_chips(first_copies)
     head_other = swap(head_other)
-    cross = lax.all_gather(factor_cross, "col", axis=0)
-    first_head, cross = lax.optimization_barrier((first_head, cross))
-    cross_other = swap(cross)
-
-    first = gather_chips(solve_chip(0, diag_inv, inverse_other, first_head))
-    second_head = gather_chips(cross_chip(cross, cross_other, head, head_other, first))
+    while 2 * len(ring) < lax.axis_size("col") // 2:
+        ring.append(pass_on(ring[-1], 2))
+    near, far = jnp.concatenate(ring[:-1]), ring[-1]
+    blocks = jnp.concatenate([block[None], near, far, swap(near), swap(far)])
+    second_head = gather_chips(cross_chip(head, head_other, first, blocks))
     second = gather_chips(solve_chip(1, diag_inv, inverse_other, second_head))
     tail, solved = tail_rows(rhs_tail, factor, (first, swap(first), second, swap(second)))
     return solved, tail

time: 149 us -> 158 us (1.060)
  blocking collectives: 57.8 us -> 22.5 us
  waiting for transfers between devices: 9.41 us -> 35.2 us
  starting transfers between devices: 48.2 us -> 68.5 us
  local copies, waits for them, and re-layouts: 6.45 us -> 3.71 us
    all_gather x1 -> x0, blocking collectives: 37.9 us -> none  [local(): cross = lax.all_gather(factor_cross, 'col', axis=0)]
    ppermute x0 -> x5, starting transfers between devices: none -> 23.5 us  [pass_on(): return lax.ppermute(block, ('row', 'col'), pairs)]
    ppermute x0 -> x5, waiting for transfers between devices: none -> 19 us  [pass_on(): return lax.ppermute(block, ('row', 'col'), pairs)]
    ppermute x5 -> x7, starting transfers between devices: 34.1 us -> 24.5 us  [swap(): return lax.ppermute(value, 'row', [(i, i ^ 1) for i in range(rows)])]
    all_to_all x1, starting transfers between devices: 3.73 us -> 10.5 us  [gather_half(): lax.all_to_all(copies.reshape(chips * cores, rows, half), 'row', 0, 0, ti...]
    all_to_all x2, waiting for transfers between devices: 5.18 us -> 11.2 us  [gather_chips(): lax.all_to_all(copies, 'row', 0, 0, axis_index_groups=groups, tiled=True)]
    unnamed x20 -> x21, local copies, waits for them, and re-layouts: 6.45 us -> 3.7 us
    all_to_all x1, blocking collectives: 19.9 us -> 22.5 us  [gather_chips(): lax.all_to_all(copies, 'row', 0, 0, axis_index_groups=groups, tiled=True)]
  transfers between devices with their start and end apart: 9 -> 16, of which waited for: 3 -> 7; matrix products, arithmetic and copies ran while one was open for 0% -> 0% of each run, Pallas kernels for 3% -> 3%
where the time goes in v4:
time: 158 us; the launch traced here: 157 us
  starting transfers between devices  68.5 us (43%)
  waiting for transfers between devices  35.2 us (22%)
  blocking collectives  22.5 us (14%)
  between operations  14.3 us (9%)
  Pallas kernels  13.1 us (8%)
  local copies, waits for them, and re-layouts  3.71 us (2%)
    ppermute x7, starting transfers between devices, swap(): return lax.ppermute(value, 'row', [(i, i ^ 1) for i in range(rows)])  24.5 us
    ppermute x5, starting transfers between devices, pass_on(): return lax.ppermute(block, ('row', 'col'), pairs)  23.5 us
    all_to_all x1, blocking collectives, gather_chips(): lax.all_to_all(copies, 'row', 0, 0, axis_index_groups=groups, tiled=True)  22.5 us
    ppermute x5, waiting for transfers between devices, pass_on(): return lax.ppermute(block, ('row', 'col'), pairs)  19 us
    all_to_all x2, waiting for transfers between devices, gather_chips(): lax.all_to_all(copies, 'row', 0, 0, axis_index_groups=groups, tiled=True)  11.2 us
    all_to_all x1, starting transfers between devices, gather_half(): lax.all_to_all(copies.reshape(chips * cores, rows, half), 'row', 0, 0, ti...  10.5 us
    all_to_all x2, starting transfers between devices, gather_chips(): lax.all_to_all(copies, 'row', 0, 0, axis_index_groups=groups, tiled=True)  10 us
    pallas_call x1, Pallas kernels, tail_rows(): pl.pallas_call(tail_kernel, grid=(TAIL_STEPS,), in_specs=[whole(tail.shap...  7.71 us
  transfers between devices with their start and end apart: 16, of which 7 were waited for; matrix products, arithmetic and copies ran while one was open for 0% of the time, Pallas kernels for 3%

profile of v4, /device:TPU:1, one launch (start us, length us, event | category | flops | bytes accessed | tf_op | source)
XLA Modules:
  0.0 157.4 jit_solution(880047945312757584)
XLA Ops:
  7.2 0.7 all-gather.2.cloned.1.call-update
  7.9 0.9 copy-done.4
  8.8 1.2 shard_map.68
  10.0 10.5 %all-to-all-start = ((f32[32,64,128]{2,1,0:T(8,128)}), f32[32,64,128]{2,1,0:T(8,128)S(1)}, u32[]{:S(2)}, u32[]{:S(2)}) async-start(f32[32,64,128]{2,1,0:T(8,128)} %bitcast.1), calls=%async_computation | async-start | bytes 2097152 | tf_op jit(solution)/shard_map/all_to_all | solution.py:28
  20.5 2.3 %collective-permute-start = (f32[2,64,2048]{2,1,0:T(8,128)S(1)}, f32[2,64,2048]{2,1,0:T(8,128)S(1)}, u32[]{:S(2)}, u32[]{:S(2)}) collective-permute-start(f32[2,64,2048]{2,1,0:T(8,128)S(1)} %copy-done.1), channel_id=1, source_target_pairs={{0,16},{16,0},{32,48},{48,32},{64,80},{80,64},{96,112},{112,96},{1... | collective-permute-start | bytes 3145736 | tf_op jit(solution)/shard_map/ppermute | solution.py:16
  22.7 2.1 %collective-permute-start.1 = (f32[64,128]{1,0:T(8,128)S(1)}, f32[64,128]{1,0:T(8,128)S(1)}, u32[]{:S(2)}, u32[]{:S(2)}) collective-permute-start(f32[64,128]{1,0:T(8,128)S(1)} %copy-done.7), channel_id=1, source_target_pairs={{0,16},{16,0},{32,48},{48,32},{64,80},{80,64},{96,112},{112,96},{1... | collective-permute-start | bytes 98312 | tf_op jit(solution)/shard_map/ppermute | solution.py:16
  24.8 1.0 collective-permute-done.1
  25.9 9.1 %collective-permute-start.2 = (f32[128,128]{1,0:T(8,128)S(1)}, f32[128,128]{1,0:T(8,128)S(1)}, u32[]{:S(2)}, u32[]{:S(2)}) collective-permute-start(f32[128,128]{1,0:T(8,128)S(1)} %maximum_select_fusion), channel_id=1, source_target_pairs={{0,1},{1,2},{2,3},{3,4},{4,5},{5,6},{6,7},{7,8},{8,9},{9,10},{10,1... | collective-permute-start | bytes 196616 | tf_op jit(solution)/shard_map/ppermute | solution.py:37
  35.0 3.1 %collective-permute-start.3 = (f32[128,128]{1,0:T(8,128)S(1)}, f32[128,128]{1,0:T(8,128)S(1)}, u32[]{:S(2)}, u32[]{:S(2)}) collective-permute-start(f32[128,128]{1,0:T(8,128)S(1)} %maximum_select_fusion), channel_id=1, source_target_pairs={{0,2},{1,3},{2,4},{3,5},{4,6},{5,7},{6,8},{7,9},{8,10},{9,11},{10,... | collective-permute-start | bytes 196616 | tf_op jit(solution)/shard_map/ppermute | solution.py:37
  38.1 4.3 %collective-permute-done.3 = f32[128,128]{1,0:T(8,128)S(1)} collective-permute-done((f32[128,128]{1,0:T(8,128)S(1)}, f32[128,128]{1,0:T(8,128)S(1)}, u32[]{:S(2)}, u32[]{:S(2)}) %collective-permute-start.3) | collective-permute-done | bytes 65568 | tf_op jit(solution)/shard_map/ppermute | solution.py:37
  42.5 4.6 %collective-permute-start.6 = (f32[2,128,128]{2,1,0:T(8,128)S(1)}, f32[2,128,128]{2,1,0:T(8,128)S(1)}, u32[]{:S(2)}, u32[]{:S(2)}) collective-permute-start(f32[2,128,128]{2,1,0:T(8,128)S(1)} %pad_maximum_fusion.1), channel_id=1, source_target_pairs={{0,2},{1,3},{2,4},{3,5},{4,6},{5,7},{6,8},{7,9},{8,10},{9,11},{10,... | collective-permute-start | bytes 393224 | tf_op jit(solution)/shard_map/ppermute | solution.py:37
  47.1 1.8 %shard_map.69 = f32[16,128,128]{2,1,0:T(8,128)} custom-call(f32[2,64,2048]{2,1,0:T(8,128)S(1)} %copy-done.1, f32[2,64,2048]{2,1,0:T(8,128)S(1)} %collective-permute-done.other, f32[2048,128]{1,0:T(8,128)S(1)} %bitcast.13), custom_call_target="tpu_custom_call" | custom-call | flops 201326592 | bytes 3145728 | tf_op jit(solution)/shard_map/pallas_call | solution.py:153
  48.9 6.2 %all-to-all-start.1 = ((f32[16,128,128]{2,1,0:T(8,128)}), f32[16,128,128]{2,1,0:T(8,128)S(1)}, u32[]{:S(2)}, u32[]{:S(2)}) async-start(f32[16,128,128]{2,1,0:T(8,128)} %shard_map.69), calls=%async_computation.1 | async-start | bytes 2097152 | tf_op jit(solution)/shard_map/all_to_all | solution.py:22
  55.1 4.1 %collective-permute-start.7 = (f32[2,128,128]{2,1,0:T(8,128)S(1)}, f32[2,128,128]{2,1,0:T(8,128)S(1)}, u32[]{:S(2)}, u32[]{:S(2)}) collective-permute-start(f32[2,128,128]{2,1,0:T(8,128)S(1)} %collective-permute-done.6), channel_id=1, source_target_pairs={{0,2},{1,3},{2,4},{3,5},{4,6},{5,7},{6,8},{7,9},{8,10},{9,11},{10,... | collective-permute-start | bytes 393224 | tf_op jit(solution)/shard_map/ppermute | solution.py:37
  59.2 6.6 %collective-permute-done.7 = f32[2,128,128]{2,1,0:T(8,128)S(1)} collective-permute-done((f32[2,128,128]{2,1,0:T(8,128)S(1)}, f32[2,128,128]{2,1,0:T(8,128)S(1)}, u32[]{:S(2)}, u32[]{:S(2)}) %collective-permute-start.7) | collective-permute-done | bytes 131104 | tf_op jit(solution)/shard_map/ppermute | solution.py:37
  65.8 5.0 %collective-permute-start.9 = (f32[6,128,128]{2,1,0:T(8,128)S(1)}, f32[6,128,128]{2,1,0:T(8,128)S(1)}, u32[]{:S(2)}, u32[]{:S(2)}) collective-permute-start(f32[6,128,128]{2,1,0:T(8,128)S(1)} %pad_maximum_fusion), channel_id=1, source_target_pairs={{0,16},{16,0},{32,48},{48,32},{64,80},{80,64},{96,112},{112,96},{1... | collective-permute-start | bytes 1179656 | tf_op jit(solution)/shard_map/ppermute | solution.py:16
  70.8 1.9 %collective-permute-start.5 = (f32[64,128]{1,0:T(8,128)S(1)}, f32[64,128]{1,0:T(8,128)S(1)}, u32[]{:S(2)}, u32[]{:S(2)}) collective-permute-start(f32[64,128]{1,0:T(8,128)S(1)} %get-tuple-element.24), channel_id=1, source_target_pairs={{0,16},{16,0},{32,48},{48,32},{64,80},{80,64},{96,112},{112,96},{1... | collective-permute-start | bytes 98312 | tf_op jit(solution)/shard_map/ppermute | solution.py:16
  72.8 2.6 %collective-permute-start.8 = (f32[2,128,128]{2,1,0:T(8,128)S(1)}, f32[2,128,128]{2,1,0:T(8,128)S(1)}, u32[]{:S(2)}, u32[]{:S(2)}) collective-permute-start(f32[2,128,128]{2,1,0:T(8,128)S(1)} %collective-permute-done.7), channel_id=1, source_target_pairs={{0,2},{1,3},{2,4},{3,5},{4,6},{5,7},{6,8},{7,9},{8,10},{9,11},{10,... | collective-permute-start | bytes 393224 | tf_op jit(solution)/shard_map/ppermute | solution.py:37
  75.4 8.1 %collective-permute-done.8 = f32[2,128,128]{2,1,0:T(8,128)S(1)} collective-permute-done((f32[2,128,128]{2,1,0:T(8,128)S(1)}, f32[2,128,128]{2,1,0:T(8,128)S(1)}, u32[]{:S(2)}, u32[]{:S(2)}) %collective-permute-start.8) | collective-permute-done | bytes 131104 | tf_op jit(solution)/shard_map/ppermute | solution.py:37
  83.5 4.5 %collective-permute-start.10 = (f32[2,128,128]{2,1,0:T(8,128)S(1)}, f32[2,128,128]{2,1,0:T(8,128)S(1)}, u32[]{:S(2)}, u32[]{:S(2)}) collective-permute-start(f32[2,128,128]{2,1,0:T(8,128)S(1)} %collective-permute-done.8), channel_id=1, source_target_pairs={{0,16},{16,0},{32,48},{48,32},{64,80},{80,64},{96,112},{112,96},{1... | collective-permute-start | bytes 393224 | tf_op jit(solution)/shard_map/ppermute | solution.py:16
  88.0 0.9 collective-permute-done.10
  88.9 1.1 copy-done.2
  90.0 1.6 %copy-done.3 = f32[17,128,128]{2,1,0:T(8,128)S(1)} copy-done((f32[17,128,128]{2,1,0:T(8,128)S(1)}, f32[17,128,128]{2,1,0:T(8,128)}, u32[]{:S(2)}) %copy-start.3) | copy-done | bytes 1114136
  91.7 0.7 shard_map.70
  92.3 22.5 %all_to_all.20 = f32[16,128,128]{2,1,0:T(8,128)S(1)} all-to-all(f32[16,128,128]{2,1,0:T(8,128)S(1)} %shard_map.70), channel_id=1, replica_groups={{0,32,64,96,128,160,192,224,256,288,320,352,384,416,448,480},{16,48,80,..., dimensions={0} | all-to-all | bytes 2097152 | tf_op jit(solution)/shard_map/all_to_all | solution.py:22
  114.8 1.7 %shard_map.71 = f32[16,128,128]{2,1,0:T(8,128)} custom-call(f32[2,64,2048]{2,1,0:T(8,128)S(1)} %copy-done.1, f32[2,64,2048]{2,1,0:T(8,128)S(1)} %collective-permute-done.other, f32[2048,128]{1,0:T(8,128)S(1)} %bitcast.14), custom_call_target="tpu_custom_call" | custom-call | flops 201326592 | bytes 3145728 | tf_op jit(solution)/shard_map/pallas_call | solution.py:153
  116.5 3.8 %all-to-all-start.3 = ((f32[16,128,128]{2,1,0:T(8,128)}), f32[16,128,128]{2,1,0:T(8,128)S(1)}, u32[]{:S(2)}, u32[]{:S(2)}) async-start(f32[16,128,128]{2,1,0:T(8,128)} %shard_map.71), calls=%async_computation.3 | async-start | bytes 2097152 | tf_op jit(solution)/shard_map/all_to_all | solution.py:22
  120.4 3.8 %collective-permute-start.4 = (f32[2048,128]{1,0:T(8,128)S(1)}, f32[2048,128]{1,0:T(8,128)S(1)}, u32[]{:S(2)}, u32[]{:S(2)}) collective-permute-start(f32[2048,128]{1,0:T(8,128)S(1)} %bitcast.11), channel_id=1, source_target_pairs={{0,16},{16,0},{32,48},{48,32},{64,80},{80,64},{96,112},{112,96},{1... | collective-permute-start | bytes 3145736 | tf_op jit(solution)/shard_map/ppermute | solution.py:16
  124.2 11.2 %all-to-all-done.3 = f32[16,128,128]{2,1,0:T(8,128)S(1)} async-done(((f32[16,128,128]{2,1,0:T(8,128)}), f32[16,128,128]{2,1,0:T(8,128)S(1)}, u32[]{:S(2)}, u32[]{:S(2)}) %all-to-all-start.3) | async-done | bytes 1048608 | tf_op jit(solution)/shard_map/all_to_all | solution.py:22
  135.4 5.0 %collective-permute-start.11 = (f32[2048,128]{1,0:T(8,128)S(1)}, f32[2048,128]{1,0:T(8,128)}, u32[]{:S(2)}, u32[]{:S(2)}) collective-permute-start(f32[2048,128]{1,0:T(8,128)S(1)} %bitcast.15), channel_id=1, source_target_pairs={{0,16},{16,0},{32,48},{48,32},{64,80},{80,64},{96,112},{112,96},{1... | collective-permute-start | bytes 3145736 | tf_op jit(solution)/shard_map/ppermute | solution.py:16
  140.4 2.4 %collective-permute-done.11.second_other = f32[2048,128]{1,0:T(8,128)} collective-permute-done((f32[2048,128]{1,0:T(8,128)S(1)}, f32[2048,128]{1,0:T(8,128)}, u32[]{:S(2)}, u32[]{:S(2)}) %collective-permute-start.11) | collective-permute-done | bytes 1048608 | tf_op jit(solution)/shard_map/ppermute | solution.py:16
  142.8 7.7 %shard_map.72 = (f32[448,256]{1,0:T(8,128)}, f32[2,64,256]{2,1,0:T(8,128)}) custom-call(f32[448,256]{1,0:T(8,128)} %tail.1, f32[16,896,128]{2,1,0:T(8,128)} %all-gather.2.cloned.1.call-done.factor, f32[2048,128]{1,0:T(8,128)} %bitcast.12, f32[2048,128]{1,0:T(8,128)} %copy-done.6, f32[2048,128]{1,0:T(8,128)} %bitcast.16, ...), custom_call_target="tpu_custom_call" | custom-call | flops 2818572288 | bytes 7340032 | tf_op jit(solution)/shard_map/pallas_call | solution.py:186
  (33 shorter events, 0.2 us)
Async XLA Ops:
  7.2 135.7 %all-gather.2.cloned.1.call-start = ((), (), s32[]{:S(2)}) async-start(), calls=%async_computation.4 | async-start | bytes 7798784 | tf_op jit(solution)/shard_map/all_gather | solution.py:204
  7.9 0.9 copy-start.4
  8.8 11.7 %copy-start.1 = (f32[2,64,2048]{2,1,0:T(8,128)S(1)}, f32[2,64,2048]{2,1,0:T(8,128)}, u32[]{:S(2)}) copy-start(f32[2,64,2048]{2,1,0:T(8,128)} %own.1) | copy-start | bytes 3145732
  8.8 13.9 %copy-start.7 = (f32[64,128]{1,0:T(8,128)S(1)}, f32[64,128]{1,0:T(8,128)}, u32[]{:S(2)}) copy-start(f32[64,128]{1,0:T(8,128)} %param.8) | copy-start | bytes 98308
  10.0 32.5 %all-to-all-start = ((f32[32,64,128]{2,1,0:T(8,128)}), f32[32,64,128]{2,1,0:T(8,128)S(1)}, u32[]{:S(2)}, u32[]{:S(2)}) async-start(f32[32,64,128]{2,1,0:T(8,128)} %bitcast.1), calls=%async_computation | async-start | bytes 2097152 | tf_op jit(solution)/shard_map/all_to_all | solution.py:28
  20.5 26.6 %collective-permute-start = (f32[2,64,2048]{2,1,0:T(8,128)S(1)}, f32[2,64,2048]{2,1,0:T(8,128)S(1)}, u32[]{:S(2)}, u32[]{:S(2)}) collective-permute-start(f32[2,64,2048]{2,1,0:T(8,128)S(1)} %copy-done.1), channel_id=1, source_target_pairs={{0,16},{16,0},{32,48},{48,32},{64,80},{80,64},{96,112},{112,96},{1... | collective-permute-start | bytes 3145736 | tf_op jit(solution)/shard_map/ppermute | solution.py:16
  22.7 3.1 %collective-permute-start.1 = (f32[64,128]{1,0:T(8,128)S(1)}, f32[64,128]{1,0:T(8,128)S(1)}, u32[]{:S(2)}, u32[]{:S(2)}) collective-permute-start(f32[64,128]{1,0:T(8,128)S(1)} %copy-done.7), channel_id=1, source_target_pairs={{0,16},{16,0},{32,48},{48,32},{64,80},{80,64},{96,112},{112,96},{1... | collective-permute-start | bytes 98312 | tf_op jit(solution)/shard_map/ppermute | solution.py:16
  25.9 12.2 %collective-permute-start.2 = (f32[128,128]{1,0:T(8,128)S(1)}, f32[128,128]{1,0:T(8,128)S(1)}, u32[]{:S(2)}, u32[]{:S(2)}) collective-permute-start(f32[128,128]{1,0:T(8,128)S(1)} %maximum_select_fusion), channel_id=1, source_target_pairs={{0,1},{1,2},{2,3},{3,4},{4,5},{5,6},{6,7},{7,8},{8,9},{9,10},{10,1... | collective-permute-start | bytes 196616 | tf_op jit(solution)/shard_map/ppermute | solution.py:37
  35.0 7.4 %collective-permute-start.3 = (f32[128,128]{1,0:T(8,128)S(1)}, f32[128,128]{1,0:T(8,128)S(1)}, u32[]{:S(2)}, u32[]{:S(2)}) collective-permute-start(f32[128,128]{1,0:T(8,128)S(1)} %maximum_select_fusion), channel_id=1, source_target_pairs={{0,2},{1,3},{2,4},{3,5},{4,6},{5,7},{6,8},{7,9},{8,10},{9,11},{10,... | collective-permute-start | bytes 196616 | tf_op jit(solution)/shard_map/ppermute | solution.py:37
  42.5 12.6 %collective-permute-start.6 = (f32[2,128,128]{2,1,0:T(8,128)S(1)}, f32[2,128,128]{2,1,0:T(8,128)S(1)}, u32[]{:S(2)}, u32[]{:S(2)}) collective-permute-start(f32[2,128,128]{2,1,0:T(8,128)S(1)} %pad_maximum_fusion.1), channel_id=1, source_target_pairs={{0,2},{1,3},{2,4},{3,5},{4,6},{5,7},{6,8},{7,9},{8,10},{9,11},{10,... | collective-permute-start | bytes 393224 | tf_op jit(solution)/shard_map/ppermute | solution.py:37
  48.9 41.2 %all-to-all-start.1 = ((f32[16,128,128]{2,1,0:T(8,128)}), f32[16,128,128]{2,1,0:T(8,128)S(1)}, u32[]{:S(2)}, u32[]{:S(2)}) async-start(f32[16,128,128]{2,1,0:T(8,128)} %shard_map.69), calls=%async_computation.1 | async-start | bytes 2097152 | tf_op jit(solution)/shard_map/all_to_all | solution.py:22
  55.1 10.7 %collective-permute-start.7 = (f32[2,128,128]{2,1,0:T(8,128)S(1)}, f32[2,128,128]{2,1,0:T(8,128)S(1)}, u32[]{:S(2)}, u32[]{:S(2)}) collective-permute-start(f32[2,128,128]{2,1,0:T(8,128)S(1)} %collective-permute-done.6), channel_id=1, source_target_pairs={{0,2},{1,3},{2,4},{3,5},{4,6},{5,7},{6,8},{7,9},{8,10},{9,11},{10,... | collective-permute-start | bytes 393224 | tf_op jit(solution)/shard_map/ppermute | solution.py:37
  65.8 22.1 %collective-permute-start.9 = (f32[6,128,128]{2,1,0:T(8,128)S(1)}, f32[6,128,128]{2,1,0:T(8,128)S(1)}, u32[]{:S(2)}, u32[]{:S(2)}) collective-permute-start(f32[6,128,128]{2,1,0:T(8,128)S(1)} %pad_maximum_fusion), channel_id=1, source_target_pairs={{0,16},{16,0},{32,48},{48,32},{64,80},{80,64},{96,112},{112,96},{1... | collective-permute-start | bytes 1179656 | tf_op jit(solution)/shard_map/ppermute | solution.py:16
  70.8 19.2 %collective-permute-start.5 = (f32[64,128]{1,0:T(8,128)S(1)}, f32[64,128]{1,0:T(8,128)S(1)}, u32[]{:S(2)}, u32[]{:S(2)}) collective-permute-start(f32[64,128]{1,0:T(8,128)S(1)} %get-tuple-element.24), channel_id=1, source_target_pairs={{0,16},{16,0},{32,48},{48,32},{64,80},{80,64},{96,112},{112,96},{1... | collective-permute-start | bytes 98312 | tf_op jit(solution)/shard_map/ppermute | solution.py:16
  72.8 10.7 %collective-permute-start.8 = (f32[2,128,128]{2,1,0:T(8,128)S(1)}, f32[2,128,128]{2,1,0:T(8,128)S(1)}, u32[]{:S(2)}, u32[]{:S(2)}) collective-permute-start(f32[2,128,128]{2,1,0:T(8,128)S(1)} %collective-permute-done.7), channel_id=1, source_target_pairs={{0,2},{1,3},{2,4},{3,5},{4,6},{5,7},{6,8},{7,9},{8,10},{9,11},{10,... | collective-permute-start | bytes 393224 | tf_op jit(solution)/shard_map/ppermute | solution.py:37
  83.5 5.4 %collective-permute-start.10 = (f32[2,128,128]{2,1,0:T(8,128)S(1)}, f32[2,128,128]{2,1,0:T(8,128)S(1)}, u32[]{:S(2)}, u32[]{:S(2)}) collective-permute-start(f32[2,128,128]{2,1,0:T(8,128)S(1)} %collective-permute-done.8), channel_id=1, source_target_pairs={{0,16},{16,0},{32,48},{48,32},{64,80},{80,64},{96,112},{112,96},{1... | collective-permute-start | bytes 393224 | tf_op jit(solution)/shard_map/ppermute | solution.py:16
  88.9 1.1 copy-start.2
  90.0 30.4 %copy-start = (f32[16,128,128]{2,1,0:T(8,128)}, f32[16,128,128]{2,1,0:T(8,128)S(1)}, u32[]{:S(2)}) copy-start(f32[16,128,128]{2,1,0:T(8,128)S(1)} %all-to-all-done.1) | copy-start | bytes 3145732
  90.0 1.6 %copy-start.3 = (f32[17,128,128]{2,1,0:T(8,128)S(1)}, f32[17,128,128]{2,1,0:T(8,128)}, u32[]{:S(2)}) copy-start(f32[17,128,128]{2,1,0:T(8,128)} %copy-done.2) | copy-start | bytes 3342340
  116.5 18.9 %all-to-all-start.3 = ((f32[16,128,128]{2,1,0:T(8,128)}), f32[16,128,128]{2,1,0:T(8,128)S(1)}, u32[]{:S(2)}, u32[]{:S(2)}) async-start(f32[16,128,128]{2,1,0:T(8,128)} %shard_map.71), calls=%async_computation.3 | async-start | bytes 2097152 | tf_op jit(solution)/shard_map/all_to_all | solution.py:22
  120.4 20.0 %collective-permute-start.4 = (f32[2048,128]{1,0:T(8,128)S(1)}, f32[2048,128]{1,0:T(8,128)S(1)}, u32[]{:S(2)}, u32[]{:S(2)}) collective-permute-start(f32[2048,128]{1,0:T(8,128)S(1)} %bitcast.11), channel_id=1, source_target_pairs={{0,16},{16,0},{32,48},{48,32},{64,80},{80,64},{96,112},{112,96},{1... | collective-permute-start | bytes 3145736 | tf_op jit(solution)/shard_map/ppermute | solution.py:16
  135.4 7.4 %copy-start.5 = (f32[16,128,128]{2,1,0:T(8,128)}, f32[16,128,128]{2,1,0:T(8,128)S(1)}, u32[]{:S(2)}) copy-start(f32[16,128,128]{2,1,0:T(8,128)S(1)} %all-to-all-done.3) | copy-start | bytes 3145732
  135.4 7.4 %collective-permute-start.11 = (f32[2048,128]{1,0:T(8,128)S(1)}, f32[2048,128]{1,0:T(8,128)}, u32[]{:S(2)}, u32[]{:S(2)}) collective-permute-start(f32[2048,128]{1,0:T(8,128)S(1)} %bitcast.15), channel_id=1, source_target_pairs={{0,16},{16,0},{32,48},{48,32},{64,80},{80,64},{96,112},{112,96},{1... | collective-permute-start | bytes 3145736 | tf_op jit(solution)/shard_map/ppermute | solution.py:16
  140.4 2.4 %copy-start.6 = (f32[2048,128]{1,0:T(8,128)}, f32[2048,128]{1,0:T(8,128)S(1)}, u32[]{:S(2)}) copy-start(f32[2048,128]{1,0:T(8,128)S(1)} %collective-permute-done.4.first_other) | copy-start | bytes 3145732
Sparse Core Ops, SparseCore 0:
  10.1 111.3 all-gather.1

commit v5 on v2

--- a/solution.py
+++ b/solution.py
@@ -63,36 +63,52 @@
     send[...] = jnp.where(first, right, left)
 
 
-def solve_kernel(own, other, operand, out):
-    spread(product(in_order(own[0], other[0], 0), operand[...]), out)
-
-
-def cross_kernel(own, other, head, head_other, operand, out):
+def fetch(sources, targets, sems):
+    copies = [pltpu.make_async_copy(*pair, sems.at[i]) for i, pair in enumerate(zip(sources, targets))]
+    for copy in copies:
+        copy.start()
+
+    def wait():
+        for copy in copies:
+            copy.wait()
+
+    return wait
+
+
+def product_of_parts(left, right_parts):
+    high, low = split(left)
+    right_high, right_low = right_parts
+    dot = functools.partial(jnp.dot, preferred_element_type=jnp.float32)
+    return dot(high, right_high) + (dot(high, right_low) + dot(low, right_high))
+
+
+def solve_kernel(panel, inverse, inverse_other, operand, out, own, other, sems):
+    wait = fetch((inverse.at[panel], inverse_other.at[panel]), (own, other), sems)
+    right = split(operand[...])
+    wait()
+    spread(product_of_parts(in_order(own[...], other[...], 0), right), out)
+
+
+def cross_kernel(cross, cross_other, head, head_other, operand, out, own, other, sems):
+    wait = fetch((cross, cross_other), (own, other), sems)
+    right = split(operand[...])
+    wait()
     row_of = lambda blocks: jnp.concatenate([blocks[i] for i in range(blocks.shape[0])], axis=1)
-    left = in_order(row_of(own), row_of(other), 0)
-    spread(in_order(head[...], head_other[...], 0) - product(left, operand[...]), out)
-
-
-def tail_kernel(tail, factor, first, first_other, second, second_other, out, solved, total):
-    step = pl.program_id(0)
-    row = lax.axis_index("row")
-    own_rows, depth, rows = solved.shape[1], factor.shape[2], out.shape[0]
-    per_step = first.shape[0] // own_rows
+    update = product_of_parts(in_order(row_of(own), row_of(other), 0), right)
+    spread(in_order(head[...], head_other[...], 0) - update, out)
+
+
+def own_rows_of(own, other, out, step):
+    row, rows = lax.axis_index("row"), out.shape[0]
+    per_step = own.shape[0] // rows
 
     @pl.when(step == row // per_step)
     def _():
-        at = pl.ds(pl.multiple_of((row % per_step) * own_rows, own_rows), own_rows)
-        solved[0] = in_order(first[at, :], first_other[at, :], 1)
-        solved[1] = in_order(second[at, :], second_other[at, :], 1)
-
-    left, right = [], []
-    for block in range(factor.shape[0]):
-        at = pl.ds(block * depth, depth)
-        for panel, (own, other) in enumerate(((first, first_other), (second, second_other))):
-            left.append(factor[block, pl.ds(panel, rows, stride=2), :])
-            right.append(jnp.concatenate([own[at, :], other[at, :]], axis=1))
-    part = product(jnp.concatenate(left, axis=1), jnp.concatenate(right, axis=0))
-
+        at = pl.ds(pl.multiple_of(row % per_step * rows, rows), rows)
+        out[...] = in_order(own[at, :], other[at, :], 1)
+
+
+def accumulate(tail, part, out, total, step):
     @pl.when(step == 0)
     def _():
         total[...] = part
@@ -105,6 +121,31 @@
     def _():
         half = out.shape[1] // 2
         out[...] = tail[...] - in_order(total[:, :half], total[:, half:], 1)
+
+
+def first_tail_kernel(tail, factor, own, other, out, rows_out, high, low, total):
+    step = pl.program_id(0)
+    own_rows_of(own, other, rows_out, step)
+    panel = lambda k: jnp.concatenate(
+        [factor[i, pl.ds(k, out.shape[0], stride=2), :] for i in range(factor.shape[0])], axis=1
+    )
+    high[...], low[...] = split(panel(1))
+    part = product(panel(0), jnp.concatenate([own[...], other[...]], axis=1))
+    accumulate(tail, part, out, total, step)
+
+
+def second_tail_kernel(tail, high, low, own, other, first_rows, out, solved, total):
+    step = pl.program_id(0)
+    own_rows_of(own, other, solved.at[1], step)
+
+    @pl.when(step == 0)
+    def _():
+        solved[0] = first_rows[...]
+
+    right_high, right_low = split(jnp.concatenate([own[...], other[...]], axis=1))
+    dot = functools.partial(jnp.dot, preferred_element_type=jnp.float32)
+    part = dot(high[...], right_high) + (dot(high[...], right_low) + dot(low[...], right_high))
+    accumulate(tail, part, out, total, step)
 
 
 def params(mib):
@@ -128,59 +169,83 @@
     )(heads)
 
 
-def solve_chip(panel, own, other, operand):
-    _, rows, depth = own.shape
-    columns = operand.shape[1]
+def on_chip(kernel, left, left_shape, others):
+    depth, columns = others[-1].shape
     chips = lax.axis_size("row") // CORES
-    inverse = pl.BlockSpec((1, rows, depth), lambda step: (panel, 0, 0))
-    shape = (chips, CORES * rows, columns)
-    return pl.pallas_call(
-        solve_kernel,
-        grid=(1,),
-        in_specs=[inverse, inverse, pl.BlockSpec(operand.shape, lambda step: (0, 0))],
-        out_specs=pl.BlockSpec(shape, lambda step: (0, 0, 0)),
+    rows = 2 * left_shape[-2]
+    shape = (chips, rows, columns)
+    return pl.pallas_call(
+        kernel,
+        in_specs=[pl.BlockSpec(memory_space=pl.ANY)] * 2 + [pl.BlockSpec(memory_space=pltpu.VMEM)] * len(others),
         out_shape=jax.ShapeDtypeStruct(shape, jnp.float32),
-        compiler_params=params(16),
-        cost_estimate=estimate(12 * rows * depth * columns, 4 * depth * (2 * rows + 2 * columns)),
-    )(own, other, operand)
-
-
-def cross_chip(own, other, head, head_other, operand):
-    _, rows, _ = own.shape
-    depth, columns = operand.shape
-    chips = lax.axis_size("row") // CORES
-    return pl.pallas_call(
-        cross_kernel,
-        out_shape=jax.ShapeDtypeStruct((chips, CORES * rows, columns), jnp.float32),
-        compiler_params=params(16),
-        cost_estimate=estimate(12 * rows * depth * columns, 4 * depth * (2 * rows + 2 * columns)),
-    )(own, other, head, head_other, operand)
-
-
-def tail_rows(tail, factor, halves):
+        scratch_shapes=[
+            pltpu.VMEM(left_shape, jnp.float32),
+            pltpu.VMEM(left_shape, jnp.float32),
+            pltpu.SemaphoreType.DMA((2,)),
+        ],
+        compiler_params=params(20),
+        cost_estimate=estimate(6 * rows * depth * columns, 4 * depth * (rows + 2 * columns)),
+    )(*left, *others)
+
+
+def solve_chip(panel, inverse, inverse_other, operand):
+    kernel = functools.partial(solve_kernel, panel)
+    return on_chip(kernel, (inverse, inverse_other), inverse.shape[1:], (operand,))
+
+
+def cross_chip(cross, cross_other, head, head_other, operand):
+    return on_chip(cross_kernel, (cross, cross_other), cross.shape, (head, head_other, operand))
+
+
+def whole(shape):
+    return pl.BlockSpec(shape, lambda step: (0,) * len(shape))
+
+
+def first_tail(tail, factor, own, other):
     rows, columns = tail.shape
     blocks, double, width = factor.shape
-    depth, half = halves[0].shape
+    depth, half = own.shape
     own_rows = depth // lax.axis_size("row")
-    whole = lambda shape: pl.BlockSpec(shape, lambda step: (0,) * len(shape))
-    shapes = [
-        jax.ShapeDtypeStruct((rows, columns), jnp.float32),
-        jax.ShapeDtypeStruct((2, own_rows, columns), jnp.float32),
-    ]
-    return pl.pallas_call(
-        tail_kernel,
+    part = pl.BlockSpec((depth // TAIL_STEPS, half), lambda step: (step, 0))
+    parts = pl.BlockSpec((rows, depth // TAIL_STEPS), lambda step: (0, step))
+    return pl.pallas_call(
+        first_tail_kernel,
         grid=(TAIL_STEPS,),
         in_specs=[
             whole(tail.shape),
             pl.BlockSpec((blocks // TAIL_STEPS, double, width), lambda step: (step, 0, 0)),
-        ]
-        + [pl.BlockSpec((depth // TAIL_STEPS, half), lambda step: (step, 0)) for _ in halves],
-        out_specs=[whole(shape.shape) for shape in shapes],
-        out_shape=shapes,
+            part,
+            part,
+        ],
+        out_specs=[whole(tail.shape), whole((own_rows, columns)), parts, parts],
+        out_shape=[
+            jax.ShapeDtypeStruct(tail.shape, jnp.float32),
+            jax.ShapeDtypeStruct((own_rows, columns), jnp.float32),
+            jax.ShapeDtypeStruct((rows, depth), jnp.bfloat16),
+            jax.ShapeDtypeStruct((rows, depth), jnp.bfloat16),
+        ],
         scratch_shapes=[pltpu.VMEM((rows, columns), jnp.float32)],
-        compiler_params=params(55),
-        cost_estimate=estimate(12 * rows * depth * columns, 4 * blocks * double * width),
-    )(tail, factor, *halves)
+        compiler_params=params(50),
+        cost_estimate=estimate(6 * rows * depth * columns, 6 * blocks * double * width),
+    )(tail, factor, own, other)
+
+
+def second_tail(tail, high, low, own, other, first_rows):
+    rows, columns = tail.shape
+    depth, half = own.shape
+    part = pl.BlockSpec((depth // TAIL_STEPS, half), lambda step: (step, 0))
+    parts = pl.BlockSpec((rows, depth // TAIL_STEPS), lambda step: (0, step))
+    shapes = (tail.shape, (2,) + first_rows.shape)
+    return pl.pallas_call(
+        second_tail_kernel,
+        grid=(TAIL_STEPS,),
+        in_specs=[whole(tail.shape), parts, parts, part, part, whole(first_rows.shape)],
+        out_specs=[whole(shape) for shape in shapes],
+        out_shape=[jax.ShapeDtypeStruct(shape, jnp.float32) for shape in shapes],
+        scratch_shapes=[pltpu.VMEM((rows, columns), jnp.float32)],
+        compiler_params=params(50),
+        cost_estimate=estimate(6 * rows * depth * columns, 4 * rows * depth + 8 * depth * half),
+    )(tail, high, low, own, other, first_rows)
 
 
 def local(rhs_head, rhs_tail, diag_inv, factor_cross, factor_tail):
@@ -199,8 +264,12 @@
 
     first = gather_chips(solve_chip(0, diag_inv, inverse_other, first_head))
     second_head = gather_chips(cross_chip(cross, cross_other, head, head_other, first))
-    second = gather_chips(solve_chip(1, diag_inv, inverse_other, second_head))
-    tail, solved = tail_rows(rhs_tail, factor, (first, swap(first), second, swap(second)))
+    second_copies, first = lax.optimization_barrier((solve_chip(1, diag_inv, inverse_other, second_head), first))
+    second = gather_chips(second_copies)
+    first_other = swap(first)
+    tail, first_rows, high, low = first_tail(rhs_tail, factor, first, first_other)
+    second, tail, high, low = lax.optimization_barrier((second, tail, high, low))
+    tail, solved = second_tail(tail, high, low, second, swap(second), first_rows)
     return solved, tail
 
 

time: 149 us -> 154 us (1.034)
  starting transfers between devices: 48.2 us -> 43.3 us
  Pallas kernels: 12.1 us -> 17 us
  waiting for transfers between devices: 9.41 us -> 13.1 us
    ppermute x5, starting transfers between devices: 34.1 us -> 29 us  [swap(): return lax.ppermute(value, 'row', [(i, i ^ 1) for i in range(rows)])]
    pallas_call x4 -> x5, Pallas kernels: 12 us -> 16.9 us  [the longest x1 7.04 us: first_tail(): pl.pallas_call(first_tail_kernel, grid=(TAIL_STEPS,), in_specs=[whole(tai...]
    all_to_all x2, waiting for transfers between devices: 5.18 us -> 8.98 us  [gather_chips(): lax.all_to_all(copies, 'row', 0, 0, axis_index_groups=groups, tiled=True)]
  transfers between devices with their start and end apart: 9 -> 9, of which waited for: 3 -> 3; matrix products, arithmetic and copies ran while one was open for 0% -> 0% of each run, Pallas kernels for 3% -> 8%
where the time goes in v5:
time: 154 us; the launch traced here: 153 us
  blocking collectives  57.6 us (37%)
  starting transfers between devices  43.3 us (28%)
  Pallas kernels  17 us (11%)
  between operations  14.2 us (9%)
  waiting for transfers between devices  13.1 us (9%)
  local copies, waits for them, and re-layouts  7.66 us (5%)
    all_gather x1, blocking collectives, local(): cross = lax.all_gather(factor_cross, 'col', axis=0)  37.7 us
    ppermute x5, starting transfers between devices, swap(): return lax.ppermute(value, 'row', [(i, i ^ 1) for i in range(rows)])  29 us
    all_to_all x1, blocking collectives, gather_chips(): lax.all_to_all(copies, 'row', 0, 0, axis_index_groups=groups, tiled=True)  19.9 us
    all_to_all x2, starting transfers between devices, gather_chips(): lax.all_to_all(copies, 'row', 0, 0, axis_index_groups=groups, tiled=True)  10.6 us
    all_to_all x2, waiting for transfers between devices, gather_chips(): lax.all_to_all(copies, 'row', 0, 0, axis_index_groups=groups, tiled=True)  8.98 us
    unnamed x20, local copies, waits for them, and re-layouts  7.66 us
    pallas_call x1, Pallas kernels, first_tail(): pl.pallas_call(first_tail_kernel, grid=(TAIL_STEPS,), in_specs=[whole(tai...  7.04 us
    pallas_call x1, Pallas kernels, second_tail(): pl.pallas_call(second_tail_kernel, grid=(TAIL_STEPS,), in_specs=[whole(ta...  5.02 us
  transfers between devices with their start and end apart: 9, of which 3 were waited for; matrix products, arithmetic and copies ran while one was open for 0% of the time, Pallas kernels for 8%

profile of v5, /device:TPU:1, one launch (start us, length us, event | category | flops | bytes accessed | tf_op | source)
XLA Modules:
  0.0 152.8 jit_solution(12035131550619035161)
XLA Ops:
  7.2 0.0 copy-start
  7.2 0.0 all-gather.3.cloned.1.call-start
  7.2 0.7 all-gather.3.cloned.1.call-update
  7.9 0.9 copy-done.8
  8.8 0.1 shard_map.68
  8.9 1.1 copy-done.2
  10.0 8.8 %collective-permute-start = (f32[2,64,2048]{2,1,0:T(8,128)}, f32[2,64,2048]{2,1,0:T(8,128)S(1)}, u32[]{:S(2)}, u32[]{:S(2)}) collective-permute-start(f32[2,64,2048]{2,1,0:T(8,128)} %inverse.1), channel_id=1, source_target_pairs={{0,16},{16,0},{32,48},{48,32},{64,80},{80,64},{96,112},{112,96},{1... | collective-permute-start | bytes 3145736 | tf_op jit(solution)/shard_map/ppermute | solution.py:16
  18.8 3.7 %all-to-all-start = ((f32[32,64,128]{2,1,0:T(8,128)}), f32[32,64,128]{2,1,0:T(8,128)S(1)}, u32[]{:S(2)}, u32[]{:S(2)}) async-start(f32[32,64,128]{2,1,0:T(8,128)} %bitcast.16), calls=%async_computation | async-start | bytes 2097152 | tf_op jit(solution)/shard_map/all_to_all | solution.py:28
  22.5 37.7 %all-gather = f32[1024,128]{1,0:T(8,128)} all-gather(f32[64,128]{1,0:T(8,128)S(1)} %copy-done.9), channel_id=2, replica_groups=mesh['row'=32,'col'=16] {'col'}, dimensions={0}, use_global_device_ids=true | all-gather | bytes 557056 | tf_op jit(solution)/shard_map/all_gather | solution.py:261
  60.2 2.0 %shard_map.69 = f32[16,128,128]{2,1,0:T(8,128)} custom-call(f32[2,64,2048]{2,1,0:T(8,128)S(1)} %copy-done, f32[2,64,2048]{2,1,0:T(8,128)S(1)} %collective-permute-done.inverse_other, f32[2048,128]{1,0:T(8,128)S(1)} %bitcast.12), custom_call_target="tpu_custom_call" | custom-call | flops 201326592 | bytes 3145728 | tf_op jit(solution)/shard_map/pallas_call | solution.py:177
  62.2 6.9 %all-to-all-start.1 = ((f32[16,128,128]{2,1,0:T(8,128)}), f32[16,128,128]{2,1,0:T(8,128)S(1)}, u32[]{:S(2)}, u32[]{:S(2)}) async-start(f32[16,128,128]{2,1,0:T(8,128)} %shard_map.69), calls=%async_computation.1 | async-start | bytes 2097152 | tf_op jit(solution)/shard_map/all_to_all | solution.py:22
  69.1 8.5 %collective-permute-start.1 = (f32[16,64,128]{2,1,0:T(8,128)}, f32[16,64,128]{2,1,0:T(8,128)S(1)}, u32[]{:S(2)}, u32[]{:S(2)}) collective-permute-start(f32[16,64,128]{2,1,0:T(8,128)} %bitcast.14), channel_id=1, source_target_pairs={{0,16},{16,0},{32,48},{48,32},{64,80},{80,64},{96,112},{112,96},{1... | collective-permute-start | bytes 1572872 | tf_op jit(solution)/shard_map/ppermute | solution.py:16
  77.6 1.9 %collective-permute-start.2 = (f32[64,128]{1,0:T(8,128)S(1)}, f32[64,128]{1,0:T(8,128)S(1)}, u32[]{:S(2)}, u32[]{:S(2)}) collective-permute-start(f32[64,128]{1,0:T(8,128)S(1)} %get-tuple-element.30), channel_id=1, source_target_pairs={{0,16},{16,0},{32,48},{48,32},{64,80},{80,64},{96,112},{112,96},{1... | collective-permute-start | bytes 98312 | tf_op jit(solution)/shard_map/ppermute | solution.py:16
  79.6 1.2 collective-permute-done.2.head_other
  80.7 0.8 copy-done.3
  81.5 1.0 copy-done.1
  82.6 1.0 copy-done.4
  83.6 0.9 shard_map.70
  84.6 19.9 %all_to_all.20 = f32[16,128,128]{2,1,0:T(8,128)S(1)} all-to-all(f32[16,128,128]{2,1,0:T(8,128)S(1)} %shard_map.70), channel_id=1, replica_groups={{0,32,64,96,128,160,192,224,256,288,320,352,384,416,448,480},{16,48,80,..., dimensions={0} | all-to-all | bytes 2097152 | tf_op jit(solution)/shard_map/all_to_all | solution.py:22
  104.5 1.9 %shard_map.71 = f32[16,128,128]{2,1,0:T(8,128)} custom-call(f32[2,64,2048]{2,1,0:T(8,128)S(1)} %copy-done, f32[2,64,2048]{2,1,0:T(8,128)S(1)} %collective-permute-done.inverse_other, f32[2048,128]{1,0:T(8,128)S(1)} %bitcast.13), custom_call_target="tpu_custom_call" | custom-call | flops 201326592 | bytes 3145728 | tf_op jit(solution)/shard_map/pallas_call | solution.py:177
  106.4 6.8 %collective-permute-start.3 = (f32[2048,128]{1,0:T(8,128)S(1)}, f32[2048,128]{1,0:T(8,128)S(1)}, u32[]{:S(2)}, u32[]{:S(2)}) collective-permute-start(f32[2048,128]{1,0:T(8,128)S(1)} %bitcast.8), channel_id=1, source_target_pairs={{0,16},{16,0},{32,48},{48,32},{64,80},{80,64},{96,112},{112,96},{1... | collective-permute-start | bytes 3145736 | tf_op jit(solution)/shard_map/ppermute | solution.py:16
  113.2 3.7 %all-to-all-start.3 = ((f32[16,128,128]{2,1,0:T(8,128)}), f32[16,128,128]{2,1,0:T(8,128)S(1)}, u32[]{:S(2)}, u32[]{:S(2)}) async-start(f32[16,128,128]{2,1,0:T(8,128)} %shard_map.71), calls=%async_computation.3 | async-start | bytes 2097152 | tf_op jit(solution)/shard_map/all_to_all | solution.py:22
  116.9 0.0 all-gather.3.cloned.1.call-done.factor
  116.9 0.0 copy-start.7
  116.9 1.0 copy-done.7
  117.9 7.0 %shard_map.72 = (f32[448,256]{1,0:T(8,128)S(1)}, f32[64,256]{1,0:T(8,128)S(1)}, bf16[448,2048]{1,0:T(8,128)(2,1)}, bf16[448,2048]{1,0:T(8,128)(2,1)}) custom-call(f32[448,256]{1,0:T(8,128)S(1)} %copy-done.7, f32[16,896,128]{2,1,0:T(8,128)} %all-gather.3.cloned.1.call-done.factor, f32[2048,128]{1,0:T(8,128)S(1)} %bitcast.9, ...), custom_call_target="tpu_custom_call" | custom-call | flops 1409286144 | bytes 11010048 | tf_op jit(solution)/shard_map/pallas_call | solution.py:211
  125.0 0.8 copy-done.5
  125.7 9.0 %all-to-all-done.3 = f32[16,128,128]{2,1,0:T(8,128)S(1)} async-done(((f32[16,128,128]{2,1,0:T(8,128)}), f32[16,128,128]{2,1,0:T(8,128)S(1)}, u32[]{:S(2)}, u32[]{:S(2)}) %all-to-all-start.3) | async-done | bytes 1048608 | tf_op jit(solution)/shard_map/all_to_all | solution.py:22
  134.7 3.0 %collective-permute-start.4 = (f32[2048,128]{1,0:T(8,128)S(1)}, f32[2048,128]{1,0:T(8,128)S(1)}, u32[]{:S(2)}, u32[]{:S(2)}) collective-permute-start(f32[2048,128]{1,0:T(8,128)S(1)} %bitcast.10), channel_id=1, source_target_pairs={{0,16},{16,0},{32,48},{48,32},{64,80},{80,64},{96,112},{112,96},{1... | collective-permute-start | bytes 3145736 | tf_op jit(solution)/shard_map/ppermute | solution.py:16
  137.7 2.3 %collective-permute-done.4.other = f32[2048,128]{1,0:T(8,128)S(1)} collective-permute-done((f32[2048,128]{1,0:T(8,128)S(1)}, f32[2048,128]{1,0:T(8,128)S(1)}, u32[]{:S(2)}, u32[]{:S(2)}) %collective-permute-start.4) | collective-permute-done | bytes 1048608 | tf_op jit(solution)/shard_map/ppermute | solution.py:16
  140.0 1.0 copy-done.6
  141.0 5.0 %shard_map.73 = (f32[448,256]{1,0:T(8,128)}, f32[2,64,256]{2,1,0:T(8,128)}) custom-call(f32[448,256]{1,0:T(8,128)S(1)} %copy-done.6, bf16[448,2048]{1,0:T(8,128)(2,1)} %get-tuple-element.38.high, bf16[448,2048]{1,0:T(8,128)(2,1)} %get-tuple-element.39.low, f32[2048,128]{1,0:T(8,128)S(1)} %bitcast.11, f32[2048,128]{1,0:T(8,128)S(1)} %collective-permute-done.4.other, ...), custom_call_target="tpu_custom_call" | custom-call | flops 1409286144 | bytes 5767168 | tf_op jit(solution)/shard_map/pallas_call | solution.py:239
  (15 shorter events, 0.0 us)
Async XLA Ops:
  7.2 53.0 %copy-start = (f32[2,64,2048]{2,1,0:T(8,128)S(1)}, f32[2,64,2048]{2,1,0:T(8,128)}, u32[]{:S(2)}) copy-start(f32[2,64,2048]{2,1,0:T(8,128)} %inverse.1) | copy-start | bytes 3145732
  7.2 109.7 %all-gather.3.cloned.1.call-start = ((), (), s32[]{:S(2)}) async-start(), calls=%async_computation.4 | async-start | bytes 7798784 | tf_op jit(solution)/shard_map/all_gather | solution.py:253
  7.9 0.9 copy-start.8
  8.8 13.7 %copy-start.9 = (f32[64,128]{1,0:T(8,128)S(1)}, f32[64,128]{1,0:T(8,128)}, u32[]{:S(2)}) copy-start(f32[64,128]{1,0:T(8,128)} %param.8) | copy-start | bytes 98308
  8.9 1.1 copy-start.2
  10.0 50.2 %collective-permute-start = (f32[2,64,2048]{2,1,0:T(8,128)}, f32[2,64,2048]{2,1,0:T(8,128)S(1)}, u32[]{:S(2)}, u32[]{:S(2)}) collective-permute-start(f32[2,64,2048]{2,1,0:T(8,128)} %inverse.1), channel_id=1, source_target_pairs={{0,16},{16,0},{32,48},{48,32},{64,80},{80,64},{96,112},{112,96},{1... | collective-permute-start | bytes 3145736 | tf_op jit(solution)/shard_map/ppermute | solution.py:16
  18.8 41.4 %all-to-all-start = ((f32[32,64,128]{2,1,0:T(8,128)}), f32[32,64,128]{2,1,0:T(8,128)S(1)}, u32[]{:S(2)}, u32[]{:S(2)}) async-start(f32[32,64,128]{2,1,0:T(8,128)} %bitcast.16), calls=%async_computation | async-start | bytes 2097152 | tf_op jit(solution)/shard_map/all_to_all | solution.py:28
  62.2 19.3 %all-to-all-start.1 = ((f32[16,128,128]{2,1,0:T(8,128)}), f32[16,128,128]{2,1,0:T(8,128)S(1)}, u32[]{:S(2)}, u32[]{:S(2)}) async-start(f32[16,128,128]{2,1,0:T(8,128)} %shard_map.69), calls=%async_computation.1 | async-start | bytes 2097152 | tf_op jit(solution)/shard_map/all_to_all | solution.py:22
  69.1 11.6 %collective-permute-start.1 = (f32[16,64,128]{2,1,0:T(8,128)}, f32[16,64,128]{2,1,0:T(8,128)S(1)}, u32[]{:S(2)}, u32[]{:S(2)}) collective-permute-start(f32[16,64,128]{2,1,0:T(8,128)} %bitcast.14), channel_id=1, source_target_pairs={{0,16},{16,0},{32,48},{48,32},{64,80},{80,64},{96,112},{112,96},{1... | collective-permute-start | bytes 1572872 | tf_op jit(solution)/shard_map/ppermute | solution.py:16
  77.6 3.1 %collective-permute-start.2 = (f32[64,128]{1,0:T(8,128)S(1)}, f32[64,128]{1,0:T(8,128)S(1)}, u32[]{:S(2)}, u32[]{:S(2)}) collective-permute-start(f32[64,128]{1,0:T(8,128)S(1)} %get-tuple-element.30), channel_id=1, source_target_pairs={{0,16},{16,0},{32,48},{48,32},{64,80},{80,64},{96,112},{112,96},{1... | collective-permute-start | bytes 98312 | tf_op jit(solution)/shard_map/ppermute | solution.py:16
  80.7 0.8 copy-start.3
  81.5 1.0 copy-start.1
  82.6 1.0 copy-start.4
  106.4 10.5 %collective-permute-start.3 = (f32[2048,128]{1,0:T(8,128)S(1)}, f32[2048,128]{1,0:T(8,128)S(1)}, u32[]{:S(2)}, u32[]{:S(2)}) collective-permute-start(f32[2048,128]{1,0:T(8,128)S(1)} %bitcast.8), channel_id=1, source_target_pairs={{0,16},{16,0},{32,48},{48,32},{64,80},{80,64},{96,112},{112,96},{1... | collective-permute-start | bytes 3145736 | tf_op jit(solution)/shard_map/ppermute | solution.py:16
  113.2 21.5 %all-to-all-start.3 = ((f32[16,128,128]{2,1,0:T(8,128)}), f32[16,128,128]{2,1,0:T(8,128)S(1)}, u32[]{:S(2)}, u32[]{:S(2)}) async-start(f32[16,128,128]{2,1,0:T(8,128)} %shard_map.71), calls=%async_computation.3 | async-start | bytes 2097152 | tf_op jit(solution)/shard_map/all_to_all | solution.py:22
  116.9 1.0 copy-start.7
  124.9 0.8 copy-start.5
  134.7 5.3 %collective-permute-start.4 = (f32[2048,128]{1,0:T(8,128)S(1)}, f32[2048,128]{1,0:T(8,128)S(1)}, u32[]{:S(2)}, u32[]{:S(2)}) collective-permute-start(f32[2048,128]{1,0:T(8,128)S(1)} %bitcast.10), channel_id=1, source_target_pairs={{0,16},{16,0},{32,48},{48,32},{64,80},{80,64},{96,112},{112,96},{1... | collective-permute-start | bytes 3145736 | tf_op jit(solution)/shard_map/ppermute | solution.py:16
  140.0 1.0 copy-start.6
Sparse Core Ops, SparseCore 0:
  10.1 105.5 all-gather.2

commit v6 on v2

--- a/solution.py
+++ b/solution.py
@@ -14,6 +14,12 @@
 def swap(value):
     rows = lax.axis_size("row")
     return lax.ppermute(value, "row", [(i, i ^ 1) for i in range(rows)])
+
+
+def gather_cores(value):
+    rows = lax.axis_size("row")
+    pairs = [list(range(i, i + CORES)) for i in range(0, rows, CORES)]
+    return lax.all_gather(value, "row", axis=0, axis_index_groups=pairs)
 
 
 def gather_chips(copies):
@@ -63,14 +69,41 @@
     send[...] = jnp.where(first, right, left)
 
 
-def solve_kernel(own, other, operand, out):
-    spread(product(in_order(own[0], other[0], 0), operand[...]), out)
-
-
-def cross_kernel(own, other, head, head_other, operand, out):
+def fetch(sources, targets, sems):
+    copies = [pltpu.make_async_copy(*pair, sems.at[i]) for i, pair in enumerate(zip(sources, targets))]
+    for copy in copies:
+        copy.start()
+
+    def wait():
+        for copy in copies:
+            copy.wait()
+
+    return wait
+
+
+def product_of_parts(left, right_parts):
+    high, low = split(left)
+    right_high, right_low = right_parts
+    dot = functools.partial(jnp.dot, preferred_element_type=jnp.float32)
+    return dot(high, right_high) + (dot(high, right_low) + dot(low, right_high))
+
+
+def solve_kernel(panel, inverse, operand, out, left, sems):
+    rows = inverse.shape[2]
+    targets = [left.at[pl.ds(core * rows, rows), :] for core in range(CORES)]
+    wait = fetch([inverse.at[core, panel] for core in range(CORES)], targets, sems)
+    right = split(operand[...])
+    wait()
+    spread(product_of_parts(left[...], right), out)
+
+
+def cross_kernel(cross, cross_other, head, head_other, operand, out, own, other, sems):
+    wait = fetch((cross, cross_other), (own, other), sems)
+    right = split(operand[...])
+    wait()
     row_of = lambda blocks: jnp.concatenate([blocks[i] for i in range(blocks.shape[0])], axis=1)
-    left = in_order(row_of(own), row_of(other), 0)
-    spread(in_order(head[...], head_other[...], 0) - product(left, operand[...]), out)
+    update = product_of_parts(in_order(row_of(own), row_of(other), 0), right)
+    spread(in_order(head[...], head_other[...], 0) - update, out)
 
 
 def tail_kernel(tail, factor, first, first_other, second, second_other, out, solved, total):
@@ -128,33 +161,29 @@
     )(heads)
 
 
-def solve_chip(panel, own, other, operand):
-    _, rows, depth = own.shape
-    columns = operand.shape[1]
+def on_chip(kernel, lefts, scratch, others):
+    depth, columns = others[-1].shape
     chips = lax.axis_size("row") // CORES
-    inverse = pl.BlockSpec((1, rows, depth), lambda step: (panel, 0, 0))
-    shape = (chips, CORES * rows, columns)
+    shape = (chips, depth // chips, columns)
     return pl.pallas_call(
-        solve_kernel,
-        grid=(1,),
-        in_specs=[inverse, inverse, pl.BlockSpec(operand.shape, lambda step: (0, 0))],
-        out_specs=pl.BlockSpec(shape, lambda step: (0, 0, 0)),
+        kernel,
+        in_specs=[pl.BlockSpec(memory_space=pl.ANY)] * len(lefts)
+        + [pl.BlockSpec(memory_space=pltpu.VMEM)] * len(others),
         out_shape=jax.ShapeDtypeStruct(shape, jnp.float32),
-        compiler_params=params(16),
-        cost_estimate=estimate(12 * rows * depth * columns, 4 * depth * (2 * rows + 2 * columns)),
-    )(own, other, operand)
-
-
-def cross_chip(own, other, head, head_other, operand):
-    _, rows, _ = own.shape
-    depth, columns = operand.shape
-    chips = lax.axis_size("row") // CORES
-    return pl.pallas_call(
-        cross_kernel,
-        out_shape=jax.ShapeDtypeStruct((chips, CORES * rows, columns), jnp.float32),
-        compiler_params=params(16),
-        cost_estimate=estimate(12 * rows * depth * columns, 4 * depth * (2 * rows + 2 * columns)),
-    )(own, other, head, head_other, operand)
+        scratch_shapes=[pltpu.VMEM(of, jnp.float32) for of in scratch] + [pltpu.SemaphoreType.DMA((2,))],
+        compiler_params=params(20),
+        cost_estimate=estimate(6 * shape[1] * depth * columns, 4 * depth * (shape[1] + 2 * columns)),
+    )(*lefts, *others)
+
+
+def solve_chip(panel, inverse, operand):
+    _, _, rows, depth = inverse.shape
+    kernel = functools.partial(solve_kernel, panel)
+    return on_chip(kernel, (inverse,), ((CORES * rows, depth),), (operand,))
+
+
+def cross_chip(cross, cross_other, head, head_other, operand):
+    return on_chip(cross_kernel, (cross, cross_other), (cross.shape,) * 2, (head, head_other, operand))
 
 
 def tail_rows(tail, factor, halves):
@@ -185,21 +214,21 @@
 
 def local(rhs_head, rhs_tail, diag_inv, factor_cross, factor_tail):
     rows, _, width = factor_tail.shape
+    inverse = gather_cores(diag_inv)
+    copies, head, head_other = prepare(rhs_head)
+    copies, factor_cross, head_other, factor_tail = lax.optimization_barrier(
+        (copies, factor_cross, head_other, factor_tail)
+    )
     factor = lax.all_gather(factor_tail.reshape(2 * rows, width), "col", axis=0)
-    copies, head, head_other = prepare(rhs_head)
-    copies, diag_inv, factor_cross, head_other = lax.optimization_barrier(
-        (copies, diag_inv, factor_cross, head_other)
-    )
     first_head = gather_half(copies)
-    inverse_other = swap(diag_inv)
     head_other = swap(head_other)
     cross = lax.all_gather(factor_cross, "col", axis=0)
     first_head, cross = lax.optimization_barrier((first_head, cross))
     cross_other = swap(cross)
 
-    first = gather_chips(solve_chip(0, diag_inv, inverse_other, first_head))
+    first = gather_chips(solve_chip(0, inverse, first_head))
     second_head = gather_chips(cross_chip(cross, cross_other, head, head_other, first))
-    second = gather_chips(solve_chip(1, diag_inv, inverse_other, second_head))
+    second = gather_chips(solve_chip(1, inverse, second_head))
     tail, solved = tail_rows(rhs_tail, factor, (first, swap(first), second, swap(second)))
     return solved, tail
 

time: 149 us -> 151 us (1.013)
  waiting for transfers between devices: 9.41 us -> 17.1 us
  blocking collectives: 57.8 us -> 52.8 us
  starting transfers between devices: 48.2 us -> 46.5 us
    ppermute x5 -> x4, starting transfers between devices: 34.1 us -> 26.3 us  [swap(): return lax.ppermute(value, 'row', [(i, i ^ 1) for i in range(rows)])]
    all_gather x1, waiting for transfers between devices: 0.01 us -> 7.62 us  [local(): factor = lax.all_gather(factor_tail.reshape(2 * rows, width), 'col', axis=0)]
    all_to_all x1, starting transfers between devices: 3.73 us -> 10.5 us  [gather_half(): lax.all_to_all(copies.reshape(chips * cores, rows, half), 'row', 0, 0, ti...]
    all_gather x1, blocking collectives: 37.9 us -> 32.9 us  [local(): cross = lax.all_gather(factor_cross, 'col', axis=0)]
    unnamed x20 -> x22, local copies, waits for them, and re-layouts: 6.45 us -> 7.81 us
    ppermute x5 -> x4, waiting for transfers between devices: 3.56 us -> 3.55 us  [swap(): return lax.ppermute(value, 'row', [(i, i ^ 1) for i in range(rows)])]
  transfers between devices with their start and end apart: 9 -> 9, of which waited for: 3 -> 4; matrix products, arithmetic and copies ran while one was open for 0% -> 0% of each run, Pallas kernels for 3% -> 3%
where the time goes in v6:
time: 151 us; the launch traced here: 150 us
  blocking collectives  52.8 us (35%)
  starting transfers between devices  46.5 us (31%)
  waiting for transfers between devices  17.1 us (11%)
  between operations  14.2 us (9%)
  Pallas kernels  11.6 us (8%)
  local copies, waits for them, and re-layouts  7.81 us (5%)
    all_gather x1, blocking collectives, local(): cross = lax.all_gather(factor_cross, 'col', axis=0)  32.9 us
    ppermute x4, starting transfers between devices, swap(): return lax.ppermute(value, 'row', [(i, i ^ 1) for i in range(rows)])  26.3 us
    all_to_all x1, blocking collectives, gather_chips(): lax.all_to_all(copies, 'row', 0, 0, axis_index_groups=groups, tiled=True)  19.9 us
    all_to_all x1, starting transfers between devices, gather_half(): lax.all_to_all(copies.reshape(chips * cores, rows, half), 'row', 0, 0, ti...  10.5 us
    all_to_all x2, starting transfers between devices, gather_chips(): lax.all_to_all(copies, 'row', 0, 0, axis_index_groups=groups, tiled=True)  9.6 us
    unnamed x22, local copies, waits for them, and re-layouts  7.81 us
    pallas_call x1, Pallas kernels, tail_rows(): pl.pallas_call(tail_kernel, grid=(TAIL_STEPS,), in_specs=[whole(tail.shap...  7.72 us
    all_gather x1, waiting for transfers between devices, local(): factor = lax.all_gather(factor_tail.reshape(2 * rows, width), 'col', axis=0)  7.62 us
  transfers between devices with their start and end apart: 9, of which 4 were waited for; matrix products, arithmetic and copies ran while one was open for 0% of the time, Pallas kernels for 3%

profile of v6, /device:TPU:1, one launch (start us, length us, event | category | flops | bytes accessed | tf_op | source)
XLA Modules:
  0.0 149.9 jit_solution(16263556745806807469)
XLA Ops:
  7.2 0.0 all-gather.7.cloned.1.call-start
  7.2 0.7 all-gather.7.cloned.1.call-update
  7.9 0.0 all-gather.5.cloned.1.call-start
  8.0 0.9 copy-done.8
  8.8 1.1 shard_map.68
  10.0 0.0 all-gather.5.cloned.1.call-update
  10.0 10.5 %all-to-all-start = ((f32[32,64,128]{2,1,0:T(8,128)}), f32[32,64,128]{2,1,0:T(8,128)S(1)}, u32[]{:S(2)}, u32[]{:S(2)}) async-start(f32[32,64,128]{2,1,0:T(8,128)} %bitcast.2), calls=%async_computation | async-start | bytes 2097152 | tf_op jit(solution)/shard_map/all_to_all | solution.py:34
  20.5 32.9 %all-gather.1 = f32[1024,128]{1,0:T(8,128)} all-gather(f32[64,128]{1,0:T(8,128)} %param.8), channel_id=3, replica_groups=mesh['row'=32,'col'=16] {'col'}, dimensions={0}, use_global_device_ids=true | all-gather | bytes 557056 | tf_op jit(solution)/shard_map/all_gather | solution.py:225
  53.3 0.0 all-to-all-done
  53.3 1.6 %copy-done.1 = f32[4,64,2048]{2,1,0:T(8,128)S(1)} copy-done((f32[4,64,2048]{2,1,0:T(8,128)S(1)}, f32[4,64,2048]{2,1,0:T(8,128)}, u32[]{:S(2)}) %copy-start.1) | copy-done | bytes 2097176
  54.9 0.9 shard_map.69
  55.8 1.0 copy-done.3
  56.8 5.9 %all-to-all-start.1 = ((f32[16,128,128]{2,1,0:T(8,128)}), f32[16,128,128]{2,1,0:T(8,128)S(1)}, u32[]{:S(2)}, u32[]{:S(2)}) async-start(f32[16,128,128]{2,1,0:T(8,128)} %copy-done.3), calls=%async_computation.1 | async-start | bytes 2097152 | tf_op jit(solution)/shard_map/all_to_all | solution.py:28
  62.8 9.6 %collective-permute-start.1 = (f32[16,64,128]{2,1,0:T(8,128)}, f32[16,64,128]{2,1,0:T(8,128)S(1)}, u32[]{:S(2)}, u32[]{:S(2)}) collective-permute-start(f32[16,64,128]{2,1,0:T(8,128)} %bitcast.15), channel_id=1, source_target_pairs={{0,16},{16,0},{32,48},{48,32},{64,80},{80,64},{96,112},{112,96},{1... | collective-permute-start | bytes 1572872 | tf_op jit(solution)/shard_map/ppermute | solution.py:16
  72.4 1.9 %collective-permute-start.2 = (f32[64,128]{1,0:T(8,128)S(1)}, f32[64,128]{1,0:T(8,128)S(1)}, u32[]{:S(2)}, u32[]{:S(2)}) collective-permute-start(f32[64,128]{1,0:T(8,128)S(1)} %get-tuple-element.21), channel_id=1, source_target_pairs={{0,16},{16,0},{32,48},{48,32},{64,80},{80,64},{96,112},{112,96},{1... | collective-permute-start | bytes 98312 | tf_op jit(solution)/shard_map/ppermute | solution.py:16
  74.3 1.2 collective-permute-done.2.head_other
  75.5 0.0 collective-permute-done.1.cross_other
  75.5 0.8 copy-done.6
  76.3 0.0 all-to-all-done.1
  76.3 1.4 copy-done.5
  77.7 1.0 copy-done.7
  78.7 0.9 shard_map.70
  79.7 19.9 %all_to_all.20 = f32[16,128,128]{2,1,0:T(8,128)S(1)} all-to-all(f32[16,128,128]{2,1,0:T(8,128)S(1)} %shard_map.70), channel_id=1, replica_groups={{0,32,64,96,128,160,192,224,256,288,320,352,384,416,448,480},{16,48,80,..., dimensions={0} | all-to-all | bytes 2097152 | tf_op jit(solution)/shard_map/all_to_all | solution.py:28
  99.6 0.9 shard_map.71
  100.5 1.1 copy-done.4
  101.6 3.7 %all-to-all-start.3 = ((f32[16,128,128]{2,1,0:T(8,128)}), f32[16,128,128]{2,1,0:T(8,128)S(1)}, u32[]{:S(2)}, u32[]{:S(2)}) async-start(f32[16,128,128]{2,1,0:T(8,128)} %copy-done.4), calls=%async_computation.3 | async-start | bytes 2097152 | tf_op jit(solution)/shard_map/all_to_all | solution.py:28
  105.3 6.8 %collective-permute-start = (f32[2048,128]{1,0:T(8,128)S(1)}, f32[2048,128]{1,0:T(8,128)S(1)}, u32[]{:S(2)}, u32[]{:S(2)}) collective-permute-start(f32[2048,128]{1,0:T(8,128)S(1)} %bitcast.9), channel_id=1, source_target_pairs={{0,16},{16,0},{32,48},{48,32},{64,80},{80,64},{96,112},{112,96},{1... | collective-permute-start | bytes 3145736 | tf_op jit(solution)/shard_map/ppermute | solution.py:16
  112.0 5.2 %all-to-all-done.3 = f32[16,128,128]{2,1,0:T(8,128)S(1)} async-done(((f32[16,128,128]{2,1,0:T(8,128)}), f32[16,128,128]{2,1,0:T(8,128)S(1)}, u32[]{:S(2)}, u32[]{:S(2)}) %all-to-all-start.3) | async-done | bytes 1048608 | tf_op jit(solution)/shard_map/all_to_all | solution.py:28
  117.2 8.1 %collective-permute-start.3 = (f32[2048,128]{1,0:T(8,128)S(1)}, f32[2048,128]{1,0:T(8,128)}, u32[]{:S(2)}, u32[]{:S(2)}) collective-permute-start(f32[2048,128]{1,0:T(8,128)S(1)} %bitcast.17), channel_id=1, source_target_pairs={{0,16},{16,0},{32,48},{48,32},{64,80},{80,64},{96,112},{112,96},{1... | collective-permute-start | bytes 3145736 | tf_op jit(solution)/shard_map/ppermute | solution.py:16
  125.3 2.4 %collective-permute-done.3.second_other = f32[2048,128]{1,0:T(8,128)} collective-permute-done((f32[2048,128]{1,0:T(8,128)S(1)}, f32[2048,128]{1,0:T(8,128)}, u32[]{:S(2)}, u32[]{:S(2)}) %collective-permute-start.3) | collective-permute-done | bytes 1048608 | tf_op jit(solution)/shard_map/ppermute | solution.py:16
  127.7 7.6 %all-gather.5.cloned.1.call-done.factor = f32[16,896,128]{2,1,0:T(8,128)} async-done(((f32[1,896,128]{2,1,0:T(8,128)}), f32[16,896,128]{2,1,0:T(8,128)}) %all-gather.5.cloned.1.call-update) | async-done | bytes 7340048 | tf_op jit(solution)/shard_map/all_gather | solution.py:222
  135.3 7.7 %shard_map.72 = (f32[448,256]{1,0:T(8,128)}, f32[2,64,256]{2,1,0:T(8,128)}) custom-call(f32[448,256]{1,0:T(8,128)} %tail.1, f32[16,896,128]{2,1,0:T(8,128)} %all-gather.5.cloned.1.call-done.factor, f32[2048,128]{1,0:T(8,128)} %bitcast.10, f32[2048,128]{1,0:T(8,128)} %copy-done.10, f32[2048,128]{1,0:T(8,128)} %bitcast.18, ...), custom_call_target="tpu_custom_call" | custom-call | flops 2818572288 | bytes 7340032 | tf_op jit(solution)/shard_map/pallas_call | solution.py:199
  (17 shorter events, 0.0 us)
Async XLA Ops:
  7.2 46.2 %all-gather.7.cloned.1.call-start = ((), (), s32[]{:S(2)}) async-start(), calls=%async_computation.5 | async-start | bytes 3145728 | tf_op jit(solution)/shard_map/all_gather | solution.py:22
  7.9 127.4 %all-gather.5.cloned.1.call-start = ((), (), s32[]{:S(2)}) async-start(), calls=%async_computation.4 | async-start | bytes 7798784 | tf_op jit(solution)/shard_map/all_gather | solution.py:222
  7.9 0.9 copy-start.8
  10.0 43.3 %all-to-all-start = ((f32[32,64,128]{2,1,0:T(8,128)}), f32[32,64,128]{2,1,0:T(8,128)S(1)}, u32[]{:S(2)}, u32[]{:S(2)}) async-start(f32[32,64,128]{2,1,0:T(8,128)} %bitcast.2), calls=%async_computation | async-start | bytes 2097152 | tf_op jit(solution)/shard_map/all_to_all | solution.py:34
  53.3 1.6 %copy-start.1 = (f32[4,64,2048]{2,1,0:T(8,128)S(1)}, f32[4,64,2048]{2,1,0:T(8,128)}, u32[]{:S(2)}) copy-start(f32[4,64,2048]{2,1,0:T(8,128)} %all-gather.7.cloned.1.call-done) | copy-start | bytes 6291460
  54.9 44.7 %copy-start.2 = (f32[4,64,2048]{2,1,0:T(8,128)S(1)}, f32[4,64,2048]{2,1,0:T(8,128)}, u32[]{:S(2)}) copy-start(f32[4,64,2048]{2,1,0:T(8,128)} %all-gather.7.cloned.1.call-done) | copy-start | bytes 6291460
  55.8 1.0 copy-start.3
  56.8 19.4 %all-to-all-start.1 = ((f32[16,128,128]{2,1,0:T(8,128)}), f32[16,128,128]{2,1,0:T(8,128)S(1)}, u32[]{:S(2)}, u32[]{:S(2)}) async-start(f32[16,128,128]{2,1,0:T(8,128)} %copy-done.3), calls=%async_computation.1 | async-start | bytes 2097152 | tf_op jit(solution)/shard_map/all_to_all | solution.py:28
  62.8 12.7 %collective-permute-start.1 = (f32[16,64,128]{2,1,0:T(8,128)}, f32[16,64,128]{2,1,0:T(8,128)S(1)}, u32[]{:S(2)}, u32[]{:S(2)}) collective-permute-start(f32[16,64,128]{2,1,0:T(8,128)} %bitcast.15), channel_id=1, source_target_pairs={{0,16},{16,0},{32,48},{48,32},{64,80},{80,64},{96,112},{112,96},{1... | collective-permute-start | bytes 1572872 | tf_op jit(solution)/shard_map/ppermute | solution.py:16
  72.4 3.1 %collective-permute-start.2 = (f32[64,128]{1,0:T(8,128)S(1)}, f32[64,128]{1,0:T(8,128)S(1)}, u32[]{:S(2)}, u32[]{:S(2)}) collective-permute-start(f32[64,128]{1,0:T(8,128)S(1)} %get-tuple-element.21), channel_id=1, source_target_pairs={{0,16},{16,0},{32,48},{48,32},{64,80},{80,64},{96,112},{112,96},{1... | collective-permute-start | bytes 98312 | tf_op jit(solution)/shard_map/ppermute | solution.py:16
  75.5 0.8 copy-start.6
  76.3 59.0 %copy-start = (f32[16,128,128]{2,1,0:T(8,128)}, f32[16,128,128]{2,1,0:T(8,128)S(1)}, u32[]{:S(2)}) copy-start(f32[16,128,128]{2,1,0:T(8,128)S(1)} %all-to-all-done.1) | copy-start | bytes 3145732
  76.3 1.4 copy-start.5
  77.7 1.0 copy-start.7
  100.5 1.1 copy-start.4
  101.6 15.6 %all-to-all-start.3 = ((f32[16,128,128]{2,1,0:T(8,128)}), f32[16,128,128]{2,1,0:T(8,128)S(1)}, u32[]{:S(2)}, u32[]{:S(2)}) async-start(f32[16,128,128]{2,1,0:T(8,128)} %copy-done.4), calls=%async_computation.3 | async-start | bytes 2097152 | tf_op jit(solution)/shard_map/all_to_all | solution.py:28
  105.3 20.0 %collective-permute-start = (f32[2048,128]{1,0:T(8,128)S(1)}, f32[2048,128]{1,0:T(8,128)S(1)}, u32[]{:S(2)}, u32[]{:S(2)}) collective-permute-start(f32[2048,128]{1,0:T(8,128)S(1)} %bitcast.9), channel_id=1, source_target_pairs={{0,16},{16,0},{32,48},{48,32},{64,80},{80,64},{96,112},{112,96},{1... | collective-permute-start | bytes 3145736 | tf_op jit(solution)/shard_map/ppermute | solution.py:16
  117.2 18.1 %copy-start.9 = (f32[16,128,128]{2,1,0:T(8,128)}, f32[16,128,128]{2,1,0:T(8,128)S(1)}, u32[]{:S(2)}) copy-start(f32[16,128,128]{2,1,0:T(8,128)S(1)} %all-to-all-done.3) | copy-start | bytes 3145732
  117.2 10.5 %collective-permute-start.3 = (f32[2048,128]{1,0:T(8,128)S(1)}, f32[2048,128]{1,0:T(8,128)}, u32[]{:S(2)}, u32[]{:S(2)}) collective-permute-start(f32[2048,128]{1,0:T(8,128)S(1)} %bitcast.17), channel_id=1, source_target_pairs={{0,16},{16,0},{32,48},{48,32},{64,80},{80,64},{96,112},{112,96},{1... | collective-permute-start | bytes 3145736 | tf_op jit(solution)/shard_map/ppermute | solution.py:16
  125.3 10.0 %copy-start.10 = (f32[2048,128]{1,0:T(8,128)}, f32[2048,128]{1,0:T(8,128)S(1)}, u32[]{:S(2)}) copy-start(f32[2048,128]{1,0:T(8,128)S(1)} %collective-permute-done.first_other) | copy-start | bytes 3145732
Sparse Core Ops, SparseCore 0:
  10.1 27.7 all-gather.6
  40.0 95.2 all-gather.4

commit v7 on v6

--- a/solution.py
+++ b/solution.py
@@ -88,13 +88,18 @@
     return dot(high, right_high) + (dot(high, right_low) + dot(low, right_high))
 
 
-def solve_kernel(panel, inverse, operand, out, left, sems):
-    rows = inverse.shape[2]
-    targets = [left.at[pl.ds(core * rows, rows), :] for core in range(CORES)]
-    wait = fetch([inverse.at[core, panel] for core in range(CORES)], targets, sems)
+def first_kernel(inverse, operand, out, own, other, sems):
+    wait = fetch([inverse.at[core] for core in range(CORES)], (own, other), sems)
     right = split(operand[...])
     wait()
-    spread(product_of_parts(left[...], right), out)
+    spread(product_of_parts(jnp.concatenate([own[...], other[...]], axis=0), right), out)
+
+
+def second_kernel(inverse, inverse_other, operand, out, own, other, sems):
+    wait = fetch((inverse.at[1], inverse_other), (own, other), sems)
+    right = split(operand[...])
+    wait()
+    spread(product_of_parts(in_order(own[...], other[...], 0), right), out)
 
 
 def cross_kernel(cross, cross_other, head, head_other, operand, out, own, other, sems):
@@ -174,12 +179,6 @@
         compiler_params=params(20),
         cost_estimate=estimate(6 * shape[1] * depth * columns, 4 * depth * (shape[1] + 2 * columns)),
     )(*lefts, *others)
-
-
-def solve_chip(panel, inverse, operand):
-    _, _, rows, depth = inverse.shape
-    kernel = functools.partial(solve_kernel, panel)
-    return on_chip(kernel, (inverse,), ((CORES * rows, depth),), (operand,))
 
 
 def cross_chip(cross, cross_other, head, head_other, operand):
@@ -214,7 +213,7 @@
 
 def local(rhs_head, rhs_tail, diag_inv, factor_cross, factor_tail):
     rows, _, width = factor_tail.shape
-    inverse = gather_cores(diag_inv)
+    inverse = gather_cores(diag_inv[0])
     copies, head, head_other = prepare(rhs_head)
     copies, factor_cross, head_other, factor_tail = lax.optimization_barrier(
         (copies, factor_cross, head_other, factor_tail)
@@ -226,9 +225,13 @@
     first_head, cross = lax.optimization_barrier((first_head, cross))
     cross_other = swap(cross)
 
-    first = gather_chips(solve_chip(0, inverse, first_head))
+    both = (diag_inv.shape[1:],) * 2
+    first_copies = on_chip(first_kernel, (inverse,), both, (first_head,))
+    first_copies, second_inverse = lax.optimization_barrier((first_copies, diag_inv[1]))
+    first = gather_chips(first_copies)
+    inverse_other = swap(second_inverse)
     second_head = gather_chips(cross_chip(cross, cross_other, head, head_other, first))
-    second = gather_chips(solve_chip(1, inverse, second_head))
+    second = gather_chips(on_chip(second_kernel, (diag_inv, inverse_other), both, (second_head,)))
     tail, solved = tail_rows(rhs_tail, factor, (first, swap(first), second, swap(second)))
     return solved, tail
 

time: 151 us -> 149 us (0.987)
  blocking collectives: 52.8 us -> 30.9 us
  starting transfers between devices: 46.5 us -> 61.5 us
  waiting for transfers between devices: 17.1 us -> 20.7 us
    all_to_all x1 -> x0, blocking collectives: 19.9 us -> none  [gather_chips(): lax.all_to_all(copies, 'row', 0, 0, axis_index_groups=groups, tiled=True)]
    ppermute x4 -> x5, starting transfers between devices: 26.3 us -> 34.1 us  [swap(): return lax.ppermute(value, 'row', [(i, i ^ 1) for i in range(rows)])]
    all_to_all x2 -> x3, starting transfers between devices: 9.6 us -> 16.8 us  [gather_chips(): lax.all_to_all(copies, 'row', 0, 0, axis_index_groups=groups, tiled=True)]
    squeeze x0 -> x1, local copies, waits for them, and re-layouts: none -> 2.31 us  [local(): diag_inv[1]]
    all_to_all x2 -> x3, waiting for transfers between devices: 5.18 us -> 7.24 us  [gather_chips(): lax.all_to_all(copies, 'row', 0, 0, axis_index_groups=groups, tiled=True)]
    all_gather x1, blocking collectives: 32.9 us -> 30.9 us  [local(): cross = lax.all_gather(factor_cross, 'col', axis=0)]
    ppermute x4 -> x5, waiting for transfers between devices: 3.55 us -> 5.28 us  [swap(): return lax.ppermute(value, 'row', [(i, i ^ 1) for i in range(rows)])]
    unnamed x22 -> x20, local copies, waits for them, and re-layouts: 7.81 us -> 6.11 us
  transfers between devices with their start and end apart: 9 -> 11, of which waited for: 4 -> 6; matrix products, arithmetic and copies ran while one was open for 0% -> 0% of each run, Pallas kernels for 3% -> 3%
where the time goes in v7:
time: 149 us; the launch traced here: 148 us
  starting transfers between devices  61.5 us (41%)
  blocking collectives  30.9 us (21%)
  waiting for transfers between devices  20.7 us (14%)
  between operations  14.2 us (10%)
  Pallas kernels  12.7 us (9%)
  local copies, waits for them, and re-layouts  8.42 us (6%)
    ppermute x5, starting transfers between devices, swap(): return lax.ppermute(value, 'row', [(i, i ^ 1) for i in range(rows)])  34.1 us
    all_gather x1, blocking collectives, local(): cross = lax.all_gather(factor_cross, 'col', axis=0)  30.9 us
    all_to_all x3, starting transfers between devices, gather_chips(): lax.all_to_all(copies, 'row', 0, 0, axis_index_groups=groups, tiled=True)  16.8 us
    all_to_all x1, starting transfers between devices, gather_half(): lax.all_to_all(copies.reshape(chips * cores, rows, half), 'row', 0, 0, ti...  10.5 us
    all_gather x1, waiting for transfers between devices, local(): factor = lax.all_gather(factor_tail.reshape(2 * rows, width), 'col', axis=0)  8.12 us
    pallas_call x1, Pallas kernels, tail_rows(): pl.pallas_call(tail_kernel, grid=(TAIL_STEPS,), in_specs=[whole(tail.shap...  7.71 us
    all_to_all x3, waiting for transfers between devices, gather_chips(): lax.all_to_all(copies, 'row', 0, 0, axis_index_groups=groups, tiled=True)  7.24 us
    unnamed x20, local copies, waits for them, and re-layouts  6.11 us
  transfers between devices with their start and end apart: 11, of which 6 were waited for; matrix products, arithmetic and copies ran while one was open for 0% of the time, Pallas kernels for 3%

profile of v7, /device:TPU:1, one launch (start us, length us, event | category | flops | bytes accessed | tf_op | source)
XLA Modules:
  0.0 148.3 jit_solution(6287308482393313250)
XLA Ops:
  7.2 0.0 all-gather.6.cloned.1.call-start
  7.2 2.3 %slice_bitcast_fusion = (f32[64,2048]{1,0:T(8,128)}, f32[1,64,2048]{2,1,0:T(8,128)}) fusion(f32[2,64,2048]{2,1,0:T(8,128)} %inverse.1), kind=kLoop, calls=%fused_computation | loop fusion | bytes 2097152 | tf_op jit(solution)/shard_map/squeeze | solution.py:230
  9.5 0.0 all-gather.6.cloned.1.call-update
  9.5 0.0 all-gather.4.cloned.1.call-start
  9.6 1.0 copy-done.7
  10.6 1.1 shard_map.68
  11.7 0.0 all-gather.4.cloned.1.call-update
  11.7 10.5 %all-to-all-start = ((f32[32,64,128]{2,1,0:T(8,128)}), f32[32,64,128]{2,1,0:T(8,128)S(1)}, u32[]{:S(2)}, u32[]{:S(2)}) async-start(f32[32,64,128]{2,1,0:T(8,128)} %bitcast.1), calls=%async_computation | async-start | bytes 2097152 | tf_op jit(solution)/shard_map/all_to_all | solution.py:34
  22.2 30.9 %all-gather = f32[1024,128]{1,0:T(8,128)S(1)} all-gather(f32[64,128]{1,0:T(8,128)} %param.8), channel_id=2, replica_groups=mesh['row'=32,'col'=16] {'col'}, dimensions={0}, use_global_device_ids=true | all-gather | bytes 557056 | tf_op jit(solution)/shard_map/all_gather | solution.py:224
  53.1 1.2 copy-done.4
  54.3 2.0 %shard_map.69 = f32[16,128,128]{2,1,0:T(8,128)} custom-call(f32[2,64,2048]{2,1,0:T(8,128)S(1)} %copy-done.4, f32[2048,128]{1,0:T(8,128)S(1)} %bitcast.13), custom_call_target="tpu_custom_call" | custom-call | flops 201326592 | bytes 3145728 | tf_op jit(solution)/shard_map/pallas_call | solution.py:173
  56.3 5.8 %all-to-all-start.1 = ((f32[16,128,128]{2,1,0:T(8,128)}), f32[16,128,128]{2,1,0:T(8,128)S(1)}, u32[]{:S(2)}, u32[]{:S(2)}) async-start(f32[16,128,128]{2,1,0:T(8,128)} %shard_map.69), calls=%async_computation.1 | async-start | bytes 2097152 | tf_op jit(solution)/shard_map/all_to_all | solution.py:28
  62.1 9.5 %collective-permute-start.2 = (f32[16,64,128]{2,1,0:T(8,128)S(1)}, f32[16,64,128]{2,1,0:T(8,128)S(1)}, u32[]{:S(2)}, u32[]{:S(2)}) collective-permute-start(f32[16,64,128]{2,1,0:T(8,128)S(1)} %bitcast.14), channel_id=1, source_target_pairs={{0,16},{16,0},{32,48},{48,32},{64,80},{80,64},{96,112},{112,96},{1... | collective-permute-start | bytes 1572872 | tf_op jit(solution)/shard_map/ppermute | solution.py:16
  71.6 1.9 %collective-permute-start.3 = (f32[64,128]{1,0:T(8,128)S(1)}, f32[64,128]{1,0:T(8,128)S(1)}, u32[]{:S(2)}, u32[]{:S(2)}) collective-permute-start(f32[64,128]{1,0:T(8,128)S(1)} %get-tuple-element.25), channel_id=1, source_target_pairs={{0,16},{16,0},{32,48},{48,32},{64,80},{80,64},{96,112},{112,96},{1... | collective-permute-start | bytes 98312 | tf_op jit(solution)/shard_map/ppermute | solution.py:16
  73.5 1.2 collective-permute-done.3.head_other
  74.7 0.9 shard_map.70
  75.7 1.0 copy-done.2
  76.7 6.9 %all-to-all-start.2 = ((f32[16,128,128]{2,1,0:T(8,128)}), f32[16,128,128]{2,1,0:T(8,128)S(1)}, u32[]{:S(2)}, u32[]{:S(2)}) async-start(f32[16,128,128]{2,1,0:T(8,128)} %copy-done.2), calls=%async_computation.2 | async-start | bytes 2097152 | tf_op jit(solution)/shard_map/all_to_all | solution.py:28
  83.6 6.5 %collective-permute-start.1 = (f32[64,2048]{1,0:T(8,128)}, f32[64,2048]{1,0:T(8,128)S(1)}, u32[]{:S(2)}, u32[]{:S(2)}) collective-permute-start(f32[64,2048]{1,0:T(8,128)} %get-tuple-element.22), channel_id=1, source_target_pairs={{0,16},{16,0},{32,48},{48,32},{64,80},{80,64},{96,112},{112,96},{1... | collective-permute-start | bytes 1572872 | tf_op jit(solution)/shard_map/ppermute | solution.py:16
  90.1 1.7 %collective-permute-done.1.inverse_other = f32[64,2048]{1,0:T(8,128)S(1)} collective-permute-done((f32[64,2048]{1,0:T(8,128)}, f32[64,2048]{1,0:T(8,128)S(1)}, u32[]{:S(2)}, u32[]{:S(2)}) %collective-permute-start.1) | collective-permute-done | bytes 524320 | tf_op jit(solution)/shard_map/ppermute | solution.py:16
  91.9 0.8 copy-done.5
  92.7 3.0 %all-to-all-done.2 = f32[16,128,128]{2,1,0:T(8,128)S(1)} async-done(((f32[16,128,128]{2,1,0:T(8,128)}), f32[16,128,128]{2,1,0:T(8,128)S(1)}, u32[]{:S(2)}, u32[]{:S(2)}) %all-to-all-start.2) | async-done | bytes 1048608 | tf_op jit(solution)/shard_map/all_to_all | solution.py:28
  95.6 1.1 copy-done.6
  96.7 0.9 shard_map.71
  97.6 1.0 copy-done.3
  98.7 4.1 %all-to-all-start.3 = ((f32[16,128,128]{2,1,0:T(8,128)}), f32[16,128,128]{2,1,0:T(8,128)S(1)}, u32[]{:S(2)}, u32[]{:S(2)}) async-start(f32[16,128,128]{2,1,0:T(8,128)} %copy-done.3), calls=%async_computation.3 | async-start | bytes 2097152 | tf_op jit(solution)/shard_map/all_to_all | solution.py:28
  102.8 7.6 %collective-permute-start = (f32[2048,128]{1,0:T(8,128)S(1)}, f32[2048,128]{1,0:T(8,128)S(1)}, u32[]{:S(2)}, u32[]{:S(2)}) collective-permute-start(f32[2048,128]{1,0:T(8,128)S(1)} %bitcast.10), channel_id=1, source_target_pairs={{0,16},{16,0},{32,48},{48,32},{64,80},{80,64},{96,112},{112,96},{1... | collective-permute-start | bytes 3145736 | tf_op jit(solution)/shard_map/ppermute | solution.py:16
  110.4 4.3 %all-to-all-done.3 = f32[16,128,128]{2,1,0:T(8,128)S(1)} async-done(((f32[16,128,128]{2,1,0:T(8,128)}), f32[16,128,128]{2,1,0:T(8,128)S(1)}, u32[]{:S(2)}, u32[]{:S(2)}) %all-to-all-start.3) | async-done | bytes 1048608 | tf_op jit(solution)/shard_map/all_to_all | solution.py:28
  114.7 8.6 %collective-permute-start.4 = (f32[2048,128]{1,0:T(8,128)S(1)}, f32[2048,128]{1,0:T(8,128)}, u32[]{:S(2)}, u32[]{:S(2)}) collective-permute-start(f32[2048,128]{1,0:T(8,128)S(1)} %bitcast.16), channel_id=1, source_target_pairs={{0,16},{16,0},{32,48},{48,32},{64,80},{80,64},{96,112},{112,96},{1... | collective-permute-start | bytes 3145736 | tf_op jit(solution)/shard_map/ppermute | solution.py:16
  123.3 2.4 %collective-permute-done.4.second_other = f32[2048,128]{1,0:T(8,128)} collective-permute-done((f32[2048,128]{1,0:T(8,128)S(1)}, f32[2048,128]{1,0:T(8,128)}, u32[]{:S(2)}, u32[]{:S(2)}) %collective-permute-start.4) | collective-permute-done | bytes 1048608 | tf_op jit(solution)/shard_map/ppermute | solution.py:16
  125.7 8.1 %all-gather.4.cloned.1.call-done.factor = f32[16,896,128]{2,1,0:T(8,128)} async-done(((f32[1,896,128]{2,1,0:T(8,128)}), f32[16,896,128]{2,1,0:T(8,128)}) %all-gather.4.cloned.1.call-update) | async-done | bytes 7340048 | tf_op jit(solution)/shard_map/all_gather | solution.py:221
  133.8 7.7 %shard_map.72 = (f32[448,256]{1,0:T(8,128)}, f32[2,64,256]{2,1,0:T(8,128)}) custom-call(f32[448,256]{1,0:T(8,128)} %tail.1, f32[16,896,128]{2,1,0:T(8,128)} %all-gather.4.cloned.1.call-done.factor, f32[2048,128]{1,0:T(8,128)} %bitcast.11, f32[2048,128]{1,0:T(8,128)} %copy-done.9, f32[2048,128]{1,0:T(8,128)} %bitcast.17, ...), custom_call_target="tpu_custom_call" | custom-call | flops 2818572288 | bytes 7340032 | tf_op jit(solution)/shard_map/pallas_call | solution.py:198
  (19 shorter events, 0.0 us)
Async XLA Ops:
  7.2 45.9 %all-gather.6.cloned.1.call-start = ((), (), s32[]{:S(2)}) async-start(), calls=%async_computation.5 | async-start | bytes 1572864 | tf_op jit(solution)/shard_map/all_gather | solution.py:22
  9.5 86.1 %copy-start.1 = (f32[2,64,2048]{2,1,0:T(8,128)S(1)}, f32[2,64,2048]{2,1,0:T(8,128)}, u32[]{:S(2)}) copy-start(f32[2,64,2048]{2,1,0:T(8,128)} %inverse.1) | copy-start | bytes 3145732
  9.5 124.2 %all-gather.4.cloned.1.call-start = ((), (), s32[]{:S(2)}) async-start(), calls=%async_computation.4 | async-start | bytes 7798784 | tf_op jit(solution)/shard_map/all_gather | solution.py:221
  9.6 1.0 copy-start.7
  11.7 41.3 %all-to-all-start = ((f32[32,64,128]{2,1,0:T(8,128)}), f32[32,64,128]{2,1,0:T(8,128)S(1)}, u32[]{:S(2)}, u32[]{:S(2)}) async-start(f32[32,64,128]{2,1,0:T(8,128)} %bitcast.1), calls=%async_computation | async-start | bytes 2097152 | tf_op jit(solution)/shard_map/all_to_all | solution.py:34
  53.1 1.2 copy-start.4
  56.3 18.4 %all-to-all-start.1 = ((f32[16,128,128]{2,1,0:T(8,128)}), f32[16,128,128]{2,1,0:T(8,128)S(1)}, u32[]{:S(2)}, u32[]{:S(2)}) async-start(f32[16,128,128]{2,1,0:T(8,128)} %shard_map.69), calls=%async_computation.1 | async-start | bytes 2097152 | tf_op jit(solution)/shard_map/all_to_all | solution.py:28
  62.1 12.6 %collective-permute-start.2 = (f32[16,64,128]{2,1,0:T(8,128)S(1)}, f32[16,64,128]{2,1,0:T(8,128)S(1)}, u32[]{:S(2)}, u32[]{:S(2)}) collective-permute-start(f32[16,64,128]{2,1,0:T(8,128)S(1)} %bitcast.14), channel_id=1, source_target_pairs={{0,16},{16,0},{32,48},{48,32},{64,80},{80,64},{96,112},{112,96},{1... | collective-permute-start | bytes 1572872 | tf_op jit(solution)/shard_map/ppermute | solution.py:16
  71.6 3.1 %collective-permute-start.3 = (f32[64,128]{1,0:T(8,128)S(1)}, f32[64,128]{1,0:T(8,128)S(1)}, u32[]{:S(2)}, u32[]{:S(2)}) collective-permute-start(f32[64,128]{1,0:T(8,128)S(1)} %get-tuple-element.25), channel_id=1, source_target_pairs={{0,16},{16,0},{32,48},{48,32},{64,80},{80,64},{96,112},{112,96},{1... | collective-permute-start | bytes 98312 | tf_op jit(solution)/shard_map/ppermute | solution.py:16
  74.7 59.1 %copy-start = (f32[16,128,128]{2,1,0:T(8,128)}, f32[16,128,128]{2,1,0:T(8,128)S(1)}, u32[]{:S(2)}) copy-start(f32[16,128,128]{2,1,0:T(8,128)S(1)} %all-to-all-done.1) | copy-start | bytes 3145732
  75.7 1.0 copy-start.2
  76.7 18.9 %all-to-all-start.2 = ((f32[16,128,128]{2,1,0:T(8,128)}), f32[16,128,128]{2,1,0:T(8,128)S(1)}, u32[]{:S(2)}, u32[]{:S(2)}) async-start(f32[16,128,128]{2,1,0:T(8,128)} %copy-done.2), calls=%async_computation.2 | async-start | bytes 2097152 | tf_op jit(solution)/shard_map/all_to_all | solution.py:28
  83.6 8.2 %collective-permute-start.1 = (f32[64,2048]{1,0:T(8,128)}, f32[64,2048]{1,0:T(8,128)S(1)}, u32[]{:S(2)}, u32[]{:S(2)}) collective-permute-start(f32[64,2048]{1,0:T(8,128)} %get-tuple-element.22), channel_id=1, source_target_pairs={{0,16},{16,0},{32,48},{48,32},{64,80},{80,64},{96,112},{112,96},{1... | collective-permute-start | bytes 1572872 | tf_op jit(solution)/shard_map/ppermute | solution.py:16
  91.9 0.8 copy-start.5
  95.6 1.1 copy-start.6
  97.6 1.0 copy-start.3
  98.7 16.0 %all-to-all-start.3 = ((f32[16,128,128]{2,1,0:T(8,128)}), f32[16,128,128]{2,1,0:T(8,128)S(1)}, u32[]{:S(2)}, u32[]{:S(2)}) async-start(f32[16,128,128]{2,1,0:T(8,128)} %copy-done.3), calls=%async_computation.3 | async-start | bytes 2097152 | tf_op jit(solution)/shard_map/all_to_all | solution.py:28
  102.8 20.5 %collective-permute-start = (f32[2048,128]{1,0:T(8,128)S(1)}, f32[2048,128]{1,0:T(8,128)S(1)}, u32[]{:S(2)}, u32[]{:S(2)}) collective-permute-start(f32[2048,128]{1,0:T(8,128)S(1)} %bitcast.10), channel_id=1, source_target_pairs={{0,16},{16,0},{32,48},{48,32},{64,80},{80,64},{96,112},{112,96},{1... | collective-permute-start | bytes 3145736 | tf_op jit(solution)/shard_map/ppermute | solution.py:16
  114.7 19.1 %copy-start.8 = (f32[16,128,128]{2,1,0:T(8,128)}, f32[16,128,128]{2,1,0:T(8,128)S(1)}, u32[]{:S(2)}) copy-start(f32[16,128,128]{2,1,0:T(8,128)S(1)} %all-to-all-done.3) | copy-start | bytes 3145732
  114.7 11.0 %collective-permute-start.4 = (f32[2048,128]{1,0:T(8,128)S(1)}, f32[2048,128]{1,0:T(8,128)}, u32[]{:S(2)}, u32[]{:S(2)}) collective-permute-start(f32[2048,128]{1,0:T(8,128)S(1)} %bitcast.16), channel_id=1, source_target_pairs={{0,16},{16,0},{32,48},{48,32},{64,80},{80,64},{96,112},{112,96},{1... | collective-permute-start | bytes 3145736 | tf_op jit(solution)/shard_map/ppermute | solution.py:16
  123.3 10.5 %copy-start.9 = (f32[2048,128]{1,0:T(8,128)}, f32[2048,128]{1,0:T(8,128)S(1)}, u32[]{:S(2)}) copy-start(f32[2048,128]{1,0:T(8,128)S(1)} %collective-permute-done.first_other) | copy-start | bytes 3145732
Sparse Core Ops, SparseCore 0:
  10.1 26.2 all-gather.5
  38.5 95.2 all-gather.3

commit v8 on v6

--- a/solution.py
+++ b/solution.py
@@ -14,12 +14,6 @@
 def swap(value):
     rows = lax.axis_size("row")
     return lax.ppermute(value, "row", [(i, i ^ 1) for i in range(rows)])
-
-
-def gather_cores(value):
-    rows = lax.axis_size("row")
-    pairs = [list(range(i, i + CORES)) for i in range(0, rows, CORES)]
-    return lax.all_gather(value, "row", axis=0, axis_index_groups=pairs)
 
 
 def gather_chips(copies):
@@ -88,13 +82,11 @@
     return dot(high, right_high) + (dot(high, right_low) + dot(low, right_high))
 
 
-def solve_kernel(panel, inverse, operand, out, left, sems):
-    rows = inverse.shape[2]
-    targets = [left.at[pl.ds(core * rows, rows), :] for core in range(CORES)]
-    wait = fetch([inverse.at[core, panel] for core in range(CORES)], targets, sems)
+def solve_kernel(panel, inverse, inverse_other, operand, out, own, other, sems):
+    wait = fetch((inverse.at[panel], inverse_other.at[panel]), (own, other), sems)
     right = split(operand[...])
     wait()
-    spread(product_of_parts(left[...], right), out)
+    spread(product_of_parts(in_order(own[...], other[...], 0), right), out)
 
 
 def cross_kernel(cross, cross_other, head, head_other, operand, out, own, other, sems):
@@ -161,29 +153,32 @@
     )(heads)
 
 
-def on_chip(kernel, lefts, scratch, others):
+def on_chip(kernel, left, left_shape, others):
     depth, columns = others[-1].shape
     chips = lax.axis_size("row") // CORES
-    shape = (chips, depth // chips, columns)
+    rows = 2 * left_shape[-2]
+    shape = (chips, rows, columns)
     return pl.pallas_call(
         kernel,
-        in_specs=[pl.BlockSpec(memory_space=pl.ANY)] * len(lefts)
-        + [pl.BlockSpec(memory_space=pltpu.VMEM)] * len(others),
+        in_specs=[pl.BlockSpec(memory_space=pl.ANY)] * 2 + [pl.BlockSpec(memory_space=pltpu.VMEM)] * len(others),
         out_shape=jax.ShapeDtypeStruct(shape, jnp.float32),
-        scratch_shapes=[pltpu.VMEM(of, jnp.float32) for of in scratch] + [pltpu.SemaphoreType.DMA((2,))],
+        scratch_shapes=[
+            pltpu.VMEM(left_shape, jnp.float32),
+            pltpu.VMEM(left_shape, jnp.float32),
+            pltpu.SemaphoreType.DMA((2,)),
+        ],
         compiler_params=params(20),
-        cost_estimate=estimate(6 * shape[1] * depth * columns, 4 * depth * (shape[1] + 2 * columns)),
-    )(*lefts, *others)
-
-
-def solve_chip(panel, inverse, operand):
-    _, _, rows, depth = inverse.shape
+        cost_estimate=estimate(6 * rows * depth * columns, 4 * depth * (rows + 2 * columns)),
+    )(*left, *others)
+
+
+def solve_chip(panel, inverse, inverse_other, operand):
     kernel = functools.partial(solve_kernel, panel)
-    return on_chip(kernel, (inverse,), ((CORES * rows, depth),), (operand,))
+    return on_chip(kernel, (inverse, inverse_other), inverse.shape[1:], (operand,))
 
 
 def cross_chip(cross, cross_other, head, head_other, operand):
-    return on_chip(cross_kernel, (cross, cross_other), (cross.shape,) * 2, (head, head_other, operand))
+    return on_chip(cross_kernel, (cross, cross_other), cross.shape, (head, head_other, operand))
 
 
 def tail_rows(tail, factor, halves):
@@ -214,21 +209,21 @@
 
 def local(rhs_head, rhs_tail, diag_inv, factor_cross, factor_tail):
     rows, _, width = factor_tail.shape
-    inverse = gather_cores(diag_inv)
     copies, head, head_other = prepare(rhs_head)
-    copies, factor_cross, head_other, factor_tail = lax.optimization_barrier(
-        (copies, factor_cross, head_other, factor_tail)
+    copies, diag_inv, factor_cross, head_other, factor_tail = lax.optimization_barrier(
+        (copies, diag_inv, factor_cross, head_other, factor_tail)
     )
     factor = lax.all_gather(factor_tail.reshape(2 * rows, width), "col", axis=0)
     first_head = gather_half(copies)
+    inverse_other = swap(diag_inv)
     head_other = swap(head_other)
     cross = lax.all_gather(factor_cross, "col", axis=0)
     first_head, cross = lax.optimization_barrier((first_head, cross))
     cross_other = swap(cross)
 
-    first = gather_chips(solve_chip(0, inverse, first_head))
+    first = gather_chips(solve_chip(0, diag_inv, inverse_other, first_head))
     second_head = gather_chips(cross_chip(cross, cross_other, head, head_other, first))
-    second = gather_chips(solve_chip(1, inverse, second_head))
+    second = gather_chips(solve_chip(1, diag_inv, inverse_other, second_head))
     tail, solved = tail_rows(rhs_tail, factor, (first, swap(first), second, swap(second)))
     return solved, tail
 

time: 151 us -> 148 us (0.980)
  waiting for transfers between devices: 17.1 us -> 8.77 us
  blocking collectives: 52.8 us -> 57.3 us
  starting transfers between devices: 46.5 us -> 48.2 us
    all_gather x1, waiting for transfers between devices: 7.62 us -> 0.01 us  [local(): factor = lax.all_gather(factor_tail.reshape(2 * rows, width), 'col', axis=0)]
    ppermute x4 -> x5, starting transfers between devices: 26.3 us -> 33.9 us  [swap(): return lax.ppermute(value, 'row', [(i, i ^ 1) for i in range(rows)])]
    all_to_all x1, starting transfers between devices: 10.5 us -> 3.73 us  [gather_half(): lax.all_to_all(copies.reshape(chips * cores, rows, half), 'row', 0, 0, ti...]
    all_gather x1, blocking collectives: 32.9 us -> 37.3 us  [local(): cross = lax.all_gather(factor_cross, 'col', axis=0)]
    pallas_call x3, Pallas kernels: 2.74 us -> 4.94 us  [on_chip(): pl.pallas_call(kernel, in_specs=[pl.BlockSpec(memory_space=pl.ANY)] * 2 +...]
    unnamed x22 -> x20, local copies, waits for them, and re-layouts: 7.81 us -> 6.45 us
    ppermute x4 -> x5, waiting for transfers between devices: 3.55 us -> 3.56 us  [swap(): return lax.ppermute(value, 'row', [(i, i ^ 1) for i in range(rows)])]
  transfers between devices with their start and end apart: 9 -> 9, of which waited for: 4 -> 3; matrix products, arithmetic and copies ran while one was open for 0% -> 0% of each run, Pallas kernels for 3% -> 3%
where the time goes in v8:
time: 148 us
  blocking collectives  57.3 us (39%)
  starting transfers between devices  48.2 us (33%)
  between operations  14.2 us (10%)
  Pallas kernels  12.8 us (9%)
  waiting for transfers between devices  8.77 us (6%)
  local copies, waits for them, and re-layouts  6.45 us (4%)
    all_gather x1, blocking collectives, local(): cross = lax.all_gather(factor_cross, 'col', axis=0)  37.3 us
    ppermute x5, starting transfers between devices, swap(): return lax.ppermute(value, 'row', [(i, i ^ 1) for i in range(rows)])  33.9 us
    all_to_all x1, blocking collectives, gather_chips(): lax.all_to_all(copies, 'row', 0, 0, axis_index_groups=groups, tiled=True)  20 us
    all_to_all x2, starting transfers between devices, gather_chips(): lax.all_to_all(copies, 'row', 0, 0, axis_index_groups=groups, tiled=True)  10.5 us
    pallas_call x1, Pallas kernels, tail_rows(): pl.pallas_call(tail_kernel, grid=(TAIL_STEPS,), in_specs=[whole(tail.shap...  7.72 us
    unnamed x20, local copies, waits for them, and re-layouts  6.45 us
    all_to_all x2, waiting for transfers between devices, gather_chips(): lax.all_to_all(copies, 'row', 0, 0, axis_index_groups=groups, tiled=True)  5.2 us
    pallas_call x3, Pallas kernels, on_chip(): pl.pallas_call(kernel, in_specs=[pl.BlockSpec(memory_space=pl.ANY)] * 2 +...  4.94 us
  transfers between devices with their start and end apart: 9, of which 3 were waited for; matrix products, arithmetic and copies ran while one was open for 0% of the time, Pallas kernels for 3%

profile of v8, /device:TPU:1, one launch (start us, length us, event | category | flops | bytes accessed | tf_op | source)
XLA Modules:
  0.0 147.6 jit_solution(4197552757631380907)
XLA Ops:
  7.2 0.0 all-gather.3.cloned.1.call-start
  7.2 0.0 copy-start.7
  7.2 0.9 copy-done.7
  8.1 0.1 shard_map.68
  8.2 1.1 copy-done.4
  9.3 0.0 all-gather.3.cloned.1.call-update
  9.3 8.9 %collective-permute-start = (f32[2,64,2048]{2,1,0:T(8,128)}, f32[2,64,2048]{2,1,0:T(8,128)S(1)}, u32[]{:S(2)}, u32[]{:S(2)}) collective-permute-start(f32[2,64,2048]{2,1,0:T(8,128)} %inverse.1), channel_id=1, source_target_pairs={{0,16},{16,0},{32,48},{48,32},{64,80},{80,64},{96,112},{112,96},{1... | collective-permute-start | bytes 3145736 | tf_op jit(solution)/shard_map/ppermute | solution.py:16
  18.2 3.7 %all-to-all-start = ((f32[32,64,128]{2,1,0:T(8,128)}), f32[32,64,128]{2,1,0:T(8,128)S(1)}, u32[]{:S(2)}, u32[]{:S(2)}) async-start(f32[32,64,128]{2,1,0:T(8,128)} %bitcast.14), calls=%async_computation | async-start | bytes 2097152 | tf_op jit(solution)/shard_map/all_to_all | solution.py:28
  22.0 37.3 %all-gather = f32[1024,128]{1,0:T(8,128)} all-gather(f32[64,128]{1,0:T(8,128)} %param.8), channel_id=2, replica_groups=mesh['row'=32,'col'=16] {'col'}, dimensions={0}, use_global_device_ids=true | all-gather | bytes 557056 | tf_op jit(solution)/shard_map/all_gather | solution.py:220
  59.3 0.0 all-to-all-done
  59.3 0.0 collective-permute-done.inverse_other
  59.3 1.2 copy-done.1
  60.5 2.0 %shard_map.69 = f32[16,128,128]{2,1,0:T(8,128)} custom-call(f32[2,64,2048]{2,1,0:T(8,128)S(1)} %copy-done.1, f32[2,64,2048]{2,1,0:T(8,128)S(1)} %collective-permute-done.inverse_other, f32[2048,128]{1,0:T(8,128)S(1)} %bitcast.10), custom_call_target="tpu_custom_call" | custom-call | flops 201326592 | bytes 3145728 | tf_op jit(solution)/shard_map/pallas_call | solution.py:161
  62.6 6.9 %all-to-all-start.1 = ((f32[16,128,128]{2,1,0:T(8,128)}), f32[16,128,128]{2,1,0:T(8,128)S(1)}, u32[]{:S(2)}, u32[]{:S(2)}) async-start(f32[16,128,128]{2,1,0:T(8,128)} %shard_map.69), calls=%async_computation.1 | async-start | bytes 2097152 | tf_op jit(solution)/shard_map/all_to_all | solution.py:22
  69.4 8.2 %collective-permute-start.2 = (f32[16,64,128]{2,1,0:T(8,128)}, f32[16,64,128]{2,1,0:T(8,128)S(1)}, u32[]{:S(2)}, u32[]{:S(2)}) collective-permute-start(f32[16,64,128]{2,1,0:T(8,128)} %bitcast.12), channel_id=1, source_target_pairs={{0,16},{16,0},{32,48},{48,32},{64,80},{80,64},{96,112},{112,96},{1... | collective-permute-start | bytes 1572872 | tf_op jit(solution)/shard_map/ppermute | solution.py:16
  77.6 1.9 %collective-permute-start.3 = (f32[64,128]{1,0:T(8,128)S(1)}, f32[64,128]{1,0:T(8,128)S(1)}, u32[]{:S(2)}, u32[]{:S(2)}) collective-permute-start(f32[64,128]{1,0:T(8,128)S(1)} %get-tuple-element.23), channel_id=1, source_target_pairs={{0,16},{16,0},{32,48},{48,32},{64,80},{80,64},{96,112},{112,96},{1... | collective-permute-start | bytes 98312 | tf_op jit(solution)/shard_map/ppermute | solution.py:16
  79.6 1.2 collective-permute-done.3.head_other
  80.7 0.0 collective-permute-done.2.cross_other
  80.7 0.8 copy-done.5
  81.5 0.0 all-to-all-done.1
  81.6 1.4 copy-done.3
  83.0 1.1 copy-done.6
  84.0 0.9 shard_map.70
  85.0 20.0 %all_to_all.20 = f32[16,128,128]{2,1,0:T(8,128)S(1)} all-to-all(f32[16,128,128]{2,1,0:T(8,128)S(1)} %shard_map.70), channel_id=1, replica_groups={{0,32,64,96,128,160,192,224,256,288,320,352,384,416,448,480},{16,48,80,..., dimensions={0} | all-to-all | bytes 2097152 | tf_op jit(solution)/shard_map/all_to_all | solution.py:22
  104.9 2.0 %shard_map.71 = f32[16,128,128]{2,1,0:T(8,128)} custom-call(f32[2,64,2048]{2,1,0:T(8,128)S(1)} %copy-done.2, f32[2,64,2048]{2,1,0:T(8,128)S(1)} %collective-permute-done.inverse_other, f32[2048,128]{1,0:T(8,128)S(1)} %bitcast.11), custom_call_target="tpu_custom_call" | custom-call | flops 201326592 | bytes 3145728 | tf_op jit(solution)/shard_map/pallas_call | solution.py:161
  106.9 3.7 %all-to-all-start.3 = ((f32[16,128,128]{2,1,0:T(8,128)}), f32[16,128,128]{2,1,0:T(8,128)S(1)}, u32[]{:S(2)}, u32[]{:S(2)}) async-start(f32[16,128,128]{2,1,0:T(8,128)} %shard_map.71), calls=%async_computation.3 | async-start | bytes 2097152 | tf_op jit(solution)/shard_map/all_to_all | solution.py:22
  110.6 6.7 %collective-permute-start.1 = (f32[2048,128]{1,0:T(8,128)S(1)}, f32[2048,128]{1,0:T(8,128)S(1)}, u32[]{:S(2)}, u32[]{:S(2)}) collective-permute-start(f32[2048,128]{1,0:T(8,128)S(1)} %bitcast.8), channel_id=1, source_target_pairs={{0,16},{16,0},{32,48},{48,32},{64,80},{80,64},{96,112},{112,96},{1... | collective-permute-start | bytes 3145736 | tf_op jit(solution)/shard_map/ppermute | solution.py:16
  117.3 5.2 %all-to-all-done.3 = f32[16,128,128]{2,1,0:T(8,128)S(1)} async-done(((f32[16,128,128]{2,1,0:T(8,128)}), f32[16,128,128]{2,1,0:T(8,128)S(1)}, u32[]{:S(2)}, u32[]{:S(2)}) %all-to-all-start.3) | async-done | bytes 1048608 | tf_op jit(solution)/shard_map/all_to_all | solution.py:22
  122.5 8.1 %collective-permute-start.4 = (f32[2048,128]{1,0:T(8,128)S(1)}, f32[2048,128]{1,0:T(8,128)}, u32[]{:S(2)}, u32[]{:S(2)}) collective-permute-start(f32[2048,128]{1,0:T(8,128)S(1)} %bitcast.15), channel_id=1, source_target_pairs={{0,16},{16,0},{32,48},{48,32},{64,80},{80,64},{96,112},{112,96},{1... | collective-permute-start | bytes 3145736 | tf_op jit(solution)/shard_map/ppermute | solution.py:16
  130.6 0.0 collective-permute-done.1.first_other
  130.7 2.4 %collective-permute-done.4.second_other = f32[2048,128]{1,0:T(8,128)} collective-permute-done((f32[2048,128]{1,0:T(8,128)S(1)}, f32[2048,128]{1,0:T(8,128)}, u32[]{:S(2)}, u32[]{:S(2)}) %collective-permute-start.4) | collective-permute-done | bytes 1048608 | tf_op jit(solution)/shard_map/ppermute | solution.py:16
  133.1 7.7 %shard_map.72 = (f32[448,256]{1,0:T(8,128)}, f32[2,64,256]{2,1,0:T(8,128)}) custom-call(f32[448,256]{1,0:T(8,128)} %tail.1, f32[16,896,128]{2,1,0:T(8,128)} %all-gather.3.cloned.1.call-done.factor, f32[2048,128]{1,0:T(8,128)} %bitcast.9, f32[2048,128]{1,0:T(8,128)} %copy-done.9, f32[2048,128]{1,0:T(8,128)} %bitcast.16, ...), custom_call_target="tpu_custom_call" | custom-call | flops 2818572288 | bytes 7340032 | tf_op jit(solution)/shard_map/pallas_call | solution.py:194
  (14 shorter events, 0.0 us)
Async XLA Ops:
  7.2 125.9 %all-gather.3.cloned.1.call-start = ((), (), s32[]{:S(2)}) async-start(), calls=%async_computation.4 | async-start | bytes 7798784 | tf_op jit(solution)/shard_map/all_gather | solution.py:216
  7.2 0.9 copy-start.7
  8.2 1.1 copy-start.4
  9.3 95.6 %copy-start.2 = (f32[2,64,2048]{2,1,0:T(8,128)S(1)}, f32[2,64,2048]{2,1,0:T(8,128)}, u32[]{:S(2)}) copy-start(f32[2,64,2048]{2,1,0:T(8,128)} %inverse.1) | copy-start | bytes 3145732
  9.3 50.0 %collective-permute-start = (f32[2,64,2048]{2,1,0:T(8,128)}, f32[2,64,2048]{2,1,0:T(8,128)S(1)}, u32[]{:S(2)}, u32[]{:S(2)}) collective-permute-start(f32[2,64,2048]{2,1,0:T(8,128)} %inverse.1), channel_id=1, source_target_pairs={{0,16},{16,0},{32,48},{48,32},{64,80},{80,64},{96,112},{112,96},{1... | collective-permute-start | bytes 3145736 | tf_op jit(solution)/shard_map/ppermute | solution.py:16
  18.2 41.1 %all-to-all-start = ((f32[32,64,128]{2,1,0:T(8,128)}), f32[32,64,128]{2,1,0:T(8,128)S(1)}, u32[]{:S(2)}, u32[]{:S(2)}) async-start(f32[32,64,128]{2,1,0:T(8,128)} %bitcast.14), calls=%async_computation | async-start | bytes 2097152 | tf_op jit(solution)/shard_map/all_to_all | solution.py:28
  59.3 1.2 copy-start.1
  62.6 19.0 %all-to-all-start.1 = ((f32[16,128,128]{2,1,0:T(8,128)}), f32[16,128,128]{2,1,0:T(8,128)S(1)}, u32[]{:S(2)}, u32[]{:S(2)}) async-start(f32[16,128,128]{2,1,0:T(8,128)} %shard_map.69), calls=%async_computation.1 | async-start | bytes 2097152 | tf_op jit(solution)/shard_map/all_to_all | solution.py:22
  69.4 11.3 %collective-permute-start.2 = (f32[16,64,128]{2,1,0:T(8,128)}, f32[16,64,128]{2,1,0:T(8,128)S(1)}, u32[]{:S(2)}, u32[]{:S(2)}) collective-permute-start(f32[16,64,128]{2,1,0:T(8,128)} %bitcast.12), channel_id=1, source_target_pairs={{0,16},{16,0},{32,48},{48,32},{64,80},{80,64},{96,112},{112,96},{1... | collective-permute-start | bytes 1572872 | tf_op jit(solution)/shard_map/ppermute | solution.py:16
  77.6 3.1 %collective-permute-start.3 = (f32[64,128]{1,0:T(8,128)S(1)}, f32[64,128]{1,0:T(8,128)S(1)}, u32[]{:S(2)}, u32[]{:S(2)}) collective-permute-start(f32[64,128]{1,0:T(8,128)S(1)} %get-tuple-element.23), channel_id=1, source_target_pairs={{0,16},{16,0},{32,48},{48,32},{64,80},{80,64},{96,112},{112,96},{1... | collective-permute-start | bytes 98312 | tf_op jit(solution)/shard_map/ppermute | solution.py:16
  80.7 0.8 copy-start.5
  81.6 51.5 %copy-start = (f32[16,128,128]{2,1,0:T(8,128)}, f32[16,128,128]{2,1,0:T(8,128)S(1)}, u32[]{:S(2)}) copy-start(f32[16,128,128]{2,1,0:T(8,128)S(1)} %all-to-all-done.1) | copy-start | bytes 3145732
  81.6 1.4 copy-start.3
  83.0 1.1 copy-start.6
  106.9 15.6 %all-to-all-start.3 = ((f32[16,128,128]{2,1,0:T(8,128)}), f32[16,128,128]{2,1,0:T(8,128)S(1)}, u32[]{:S(2)}, u32[]{:S(2)}) async-start(f32[16,128,128]{2,1,0:T(8,128)} %shard_map.71), calls=%async_computation.3 | async-start | bytes 2097152 | tf_op jit(solution)/shard_map/all_to_all | solution.py:22
  110.6 20.0 %collective-permute-start.1 = (f32[2048,128]{1,0:T(8,128)S(1)}, f32[2048,128]{1,0:T(8,128)S(1)}, u32[]{:S(2)}, u32[]{:S(2)}) collective-permute-start(f32[2048,128]{1,0:T(8,128)S(1)} %bitcast.8), channel_id=1, source_target_pairs={{0,16},{16,0},{32,48},{48,32},{64,80},{80,64},{96,112},{112,96},{1... | collective-permute-start | bytes 3145736 | tf_op jit(solution)/shard_map/ppermute | solution.py:16
  122.5 10.5 %copy-start.8 = (f32[16,128,128]{2,1,0:T(8,128)}, f32[16,128,128]{2,1,0:T(8,128)S(1)}, u32[]{:S(2)}) copy-start(f32[16,128,128]{2,1,0:T(8,128)S(1)} %all-to-all-done.3) | copy-start | bytes 3145732
  122.5 10.5 %collective-permute-start.4 = (f32[2048,128]{1,0:T(8,128)S(1)}, f32[2048,128]{1,0:T(8,128)}, u32[]{:S(2)}, u32[]{:S(2)}) collective-permute-start(f32[2048,128]{1,0:T(8,128)S(1)} %bitcast.15), channel_id=1, source_target_pairs={{0,16},{16,0},{32,48},{48,32},{64,80},{80,64},{96,112},{112,96},{1... | collective-permute-start | bytes 3145736 | tf_op jit(solution)/shard_map/ppermute | solution.py:16
  130.7 2.4 %copy-start.9 = (f32[2048,128]{1,0:T(8,128)}, f32[2048,128]{1,0:T(8,128)S(1)}, u32[]{:S(2)}) copy-start(f32[2048,128]{1,0:T(8,128)S(1)} %collective-permute-done.1.first_other) | copy-start | bytes 3145732
Sparse Core Ops, SparseCore 0:
  10.1 105.2 all-gather.2
